TPU v7x, 32 devices: a whole 2x2x4 slice. The times are simulated.
32 devices in a mesh: groups: 2 (over x), mp: 16 (over z, y, core).
Axes of the slice: x: 2, y: 2, z: 4, core: 2. Of those that a mesh axis runs over, the one named last changes fastest.
Arguments:
- activations: bfloat16 [128, 16384], P(('groups', 'mp')), parts along dimension 0, may hold values from -6 to 6
- gain: bfloat16 [16384], replicated, may hold values from 0.5 to 1.5
- q_weight: bfloat16 [16384, 16384], P(None, 'mp'), may hold values from -0.046875 to 0.046875
- kv_weight: bfloat16 [16384, 2048], P(None, 'mp'), may hold values from -0.046875 to 0.046875
- o_weight: bfloat16 [16384, 16384], P(None, 'mp'), may hold values from -0.75 to 0.75
- key_cache: bfloat16 [128, 8, 512, 128], P(('groups', 'mp')), parts along dimension 0, may hold values from -400 to 400
- value_cache: bfloat16 [128, 8, 512, 128], P(('groups', 'mp')), parts along dimension 0, may hold values from -6 to 6
- lengths: int32 [128], P(('groups', 'mp')), parts along dimension 0, may hold values from 1 to 512, as said below
Outputs:
- attention_out: bfloat16 [128, 16384], P('groups', 'mp'), parts along dimension 0
There are 2 independent parts, one for each index of `groups`. A program takes and returns all parts, laid end to end along the dimension named above; an argument that names none is the same for every part. Nothing has to cross between parts.
Inputs may be any that keep to these rules, and one draw needn't show every extreme that they name: Request b attends to key_cache[b, :, t] and value_cache[b, :, t] for t < lengths[b]; some request has exactly 512.
All inputs are finite; a program needn't handle non-finite values.
Results may differ from a plain program's by a relative error of at most 0.007.
The roundings to bfloat16 on the way count: a program that leaves them out, or rounds other values in their place, can miss the bound.
Values may be sent and summed in bfloat16 or wider, within the bound.
No kernel may reach another device: no remote copies, remote signals or barrier semaphores. Data moves between devices by JAX's collectives and lax.ppermute only.
A program may use at most 128 MiB of HBM per device.

v0:
```python
import math

import jax
import jax.numpy as jnp
from jax import lax
from jax.sharding import PartitionSpec as P

HEADS = 128
KV_HEADS = 8
HEAD_DIM = 128
CACHE = 512


rope_base = 500000.0
norm_eps = 1e-05


def rotate(vector, position):
    middle = vector.shape[-1] // 2
    offsets = jnp.arange(middle, dtype=jnp.float32)
    frequency = jnp.exp(offsets * (-2.0 * math.log(rope_base) / vector.shape[-1]))
    angles = position * frequency
    cosine = jnp.cos(angles)
    sine = jnp.sin(angles)
    leading = vector[..., :middle]
    trailing = vector[..., middle:]
    return jnp.concatenate(
        [leading * cosine - trailing * sine, trailing * cosine + leading * sine], axis=-1
    )


def normalize(activations, gain):
    widened = activations.astype(jnp.float32)
    inverse = lax.rsqrt(jnp.mean(widened * widened, axis=-1, keepdims=True) + norm_eps)
    return (widened * inverse * gain.astype(jnp.float32)).astype(jnp.bfloat16)


def shards(activations, gain, q_weight, kv_weight, o_weight, key_cache, value_cache, lengths):
    normed = normalize(activations, gain)
    piece = lax.all_gather(normed, "mp", axis=0, tiled=True)
    projected = jnp.concatenate(
        [
            jnp.dot(piece, q_weight, preferred_element_type=jnp.float32),
            jnp.dot(piece, kv_weight, preferred_element_type=jnp.float32),
        ],
        axis=1,
    ).astype(jnp.bfloat16)
    query_cols = q_weight.shape[1]
    query_all, pairs_all = (
        lax.all_to_all(projected[:, :query_cols], "mp", split_axis=0, concat_axis=1, tiled=True),
        lax.all_to_all(projected[:, query_cols:], "mp", split_axis=0, concat_axis=1, tiled=True),
    )
    requests = query_all.shape[0]
    per_group = HEADS // KV_HEADS
    scaling = 1.0 / math.sqrt(HEAD_DIM)
    position = lengths.astype(jnp.float32)
    query = rotate(
        query_all.astype(jnp.float32).reshape(requests, KV_HEADS, per_group, HEAD_DIM),
        position[:, None, None, None],
    ).astype(jnp.bfloat16)
    fresh_key = rotate(
        pairs_all[:, : KV_HEADS * HEAD_DIM]
        .astype(jnp.float32)
        .reshape(requests, KV_HEADS, HEAD_DIM),
        position[:, None, None],
    ).astype(jnp.bfloat16)
    fresh_value = pairs_all[:, KV_HEADS * HEAD_DIM :].reshape(requests, KV_HEADS, HEAD_DIM)
    scores = (
        jnp.einsum("rgqd,rgtd->rgqt", query, key_cache, preferred_element_type=jnp.float32)
        * scaling
    )
    visible = jnp.arange(CACHE, dtype=jnp.int32)[None, :] < lengths[:, None]
    scores = jnp.where(visible[:, None, None, :], scores, -1e30)
    own = (
        jnp.einsum("rgqd,rgd->rgq", query, fresh_key, preferred_element_type=jnp.float32) * scaling
    )
    highest = jnp.maximum(jnp.max(scores, axis=-1), own)
    weights = jnp.where(visible[:, None, None, :], jnp.exp(scores - highest[..., None]), 0.0)
    own_weight = jnp.exp(own - highest)
    denominator = jnp.sum(weights, axis=-1) + own_weight
    probs = (weights / denominator[..., None]).astype(jnp.bfloat16)
    own_prob = (own_weight / denominator).astype(jnp.bfloat16)
    mixed = jnp.einsum("rgqt,rgtd->rgqd", probs, value_cache, preferred_element_type=jnp.float32)
    mixed = (
        mixed
        + own_prob.astype(jnp.float32)[..., None] * fresh_value.astype(jnp.float32)[:, :, None, :]
    )
    attended = mixed.reshape(requests, HEADS * HEAD_DIM).astype(jnp.bfloat16)
    result = jnp.dot(
        lax.all_gather(attended, "mp", axis=0, tiled=True),
        o_weight,
        preferred_element_type=jnp.float32,
    )
    return result.astype(jnp.bfloat16)


def solution(mesh):
    placed = (
        P(("groups", "mp"), None),
        P(),
        P(None, "mp"),
        P(None, "mp"),
        P(None, "mp"),
        P(("groups", "mp"), None, None, None),
        P(("groups", "mp"), None, None, None),
        P(("groups", "mp")),
    )
    return jax.shard_map(
        shards, mesh=mesh, in_specs=placed, out_specs=P("groups", "mp"), check_vma=False
    )
```

profile of v0, /device:TPU:0, one launch (start us, length us, event | category | flops | bytes accessed | tf_op | source)
XLA Modules:
  0.0 161.5 jit_solution(6633450354537254687)
XLA Ops:
  6.5 0.0 all-gather.5.cloned.1.call-start
  6.5 0.8 convert_element_type.55
  7.3 1.2 fusion.7
  8.5 1.7 %fusion.10 = bf16[1,4,16384]{2,1,0:T(4,128)(2,1)} fusion(bf16[4,16384]{1,0:T(4,128)(2,1)} %param.8, f32[16384]{0:T(1024)S(1)} %convert_element_type.55, f32[4]{0:T(128)S(1)} %add_rsqrt_fusion), kind=kLoop, calls=%fused_computation.22 | loop fusion | flops 262144 | bytes 327696
  10.2 0.0 all-gather.5.cloned.1.call-update
  10.2 0.7 convert_element_type.60
  10.9 0.7 iota_compare_fusion
  11.6 0.1 multiply_cosine_fusion
  11.7 42.7 %all-gather.5.cloned.1.call-done = bf16[16,4,16384]{2,1,0:T(4,128)(2,1)} async-done(((bf16[1,4,16384]{2,1,0:T(4,128)(2,1)}), bf16[16,4,16384]{2,1,0:T(4,128)(2,1)}) %all-gather.5.cloned.1.call-update) | async-done | bytes 2097168 | tf_op jit(solution)/shard_map/all_gather | solution.py:40
  54.4 2.5 %reshape.180 = bf16[64,16384]{1,0:T(8,128)(2,1)S(1)} reshape(bf16[16,4,16384]{2,1,0:T(4,128)(2,1)} %all-gather.5.cloned.1.call-done) | data formatting | bytes 4194304
  57.0 3.6 %convolution_convert_fusion.2 = bf16[64,128]{1,0:T(8,128)(2,1)} fusion(bf16[64,16384]{1,0:T(8,128)(2,1)S(1)} %reshape.180, bf16[16384,128]{1,0:T(8,128)(2,1)} %param.11), kind=kOutput, calls=%fused_computation.6 | convolution fusion | flops 268443648 | bytes 6307840 | tf_op jit(solution)/shard_map/dot_general | solution.py:44
  60.6 3.5 %all-to-all-start.1 = ((bf16[16,4,128]{2,1,0:T(4,128)(2,1)}), bf16[16,4,128]{2,1,0:T(4,128)(2,1)S(1)}, u32[]{:S(2)}, u32[]{:S(2)}) async-start(bf16[16,4,128]{2,1,0:T(4,128)(2,1)} %bitcast.2), calls=%async_computation.1 | async-start | bytes 32768 | tf_op jit(solution)/shard_map/all_to_all | solution.py:51
  64.1 13.6 %convolution_convert_fusion.1 = bf16[64,1024]{1,0:T(8,128)(2,1)S(1)} fusion(bf16[64,16384]{1,0:T(8,128)(2,1)S(1)} %reshape.180, bf16[16384,1024]{1,0:T(8,128)(2,1)} %param.10), kind=kOutput, calls=%fused_computation.5 | convolution fusion | flops 2147549184 | bytes 35782656 | tf_op jit(solution)/shard_map/dot_general | solution.py:43
  77.7 0.7 all_to_all.24
  78.4 0.0 all-to-all-done.1
  78.4 6.0 %all-to-all-start = ((bf16[16,4,1024]{2,1,0:T(4,128)(2,1)}), bf16[16,4,1024]{2,1,0:T(4,128)(2,1)S(1)}, u32[]{:S(2)}, u32[]{:S(2)}) async-start(bf16[16,4,1024]{2,1,0:T(4,128)(2,1)} %all_to_all.24), calls=%async_computation | async-start | bytes 262144 | tf_op jit(solution)/shard_map/all_to_all | solution.py:50
  84.4 0.0 all-gather.7.cloned.1.call-start
  84.5 0.1 subtract_convert_fusion.1
  84.6 0.1 maximum_bitcast_fusion
  84.7 7.7 %all-to-all-done = bf16[16,4,1024]{2,1,0:T(4,128)(2,1)S(1)} async-done(((bf16[16,4,1024]{2,1,0:T(4,128)(2,1)}), bf16[16,4,1024]{2,1,0:T(4,128)(2,1)S(1)}, u32[]{:S(2)}, u32[]{:S(2)}) %all-to-all-start) | async-done | bytes 131104 | tf_op jit(solution)/shard_map/all_to_all | solution.py:50
  92.4 0.2 copy.10
  92.6 0.0 copy-start
  92.6 0.1 subtract_convert_fusion
  92.8 0.2 fusion.11
  93.0 3.7 %fusion.18 = (f32[4,8,16]{2,1,0:T(8,128)S(1)}, f32[4,8,16,512]{3,2,1,0:T(8,128)S(1)}) fusion(bf16[4,8,512,128]{3,2,1,0:T(8,128)(2,1)} %param.13, bf16[4,8,16,64]{3,2,1,0:T(8,128)(2,1)S(1)} %get-tuple-element.6, bf16[4,8,16,64]{3,2,1,0:T(8,128)(2,1)S(1)} %get-tuple-element.5, pred[4,512]{1,0:T(4,128)(4,1)S(1)} %iota_compare_fusion), kind=kOutput, calls=%fused_computation.46 | convolution fusion | flops 68156928 | bytes 5378048 | tf_op jit(solution)/shard_map/rgqd,rgtd->rgqt/dot_general | solution.py:69
  96.8 0.4 fusion.2
  97.2 0.0 copy-done
  97.2 0.8 fusion.1
  98.0 0.7 reshape.181
  98.7 0.0 all-gather.7.cloned.1.call-update
  98.7 39.2 %all-gather.7.cloned.1.call-done = bf16[16,4,16384]{2,1,0:T(4,128)(2,1)} async-done(((bf16[1,4,16384]{2,1,0:T(4,128)(2,1)}), bf16[16,4,16384]{2,1,0:T(4,128)(2,1)}) %all-gather.7.cloned.1.call-update) | async-done | bytes 2097168 | tf_op jit(solution)/shard_map/all_gather | solution.py:90
  137.9 2.5 %reshape.182 = bf16[64,16384]{1,0:T(8,128)(2,1)S(1)} reshape(bf16[16,4,16384]{2,1,0:T(4,128)(2,1)} %all-gather.7.cloned.1.call-done) | data formatting | bytes 4194304
  140.5 14.2 %convolution_convert_fusion = bf16[64,1024]{1,0:T(8,128)(2,1)} fusion(bf16[64,16384]{1,0:T(8,128)(2,1)S(1)} %reshape.182, bf16[16384,1024]{1,0:T(8,128)(2,1)} %param.12), kind=kOutput, calls=%fused_computation.4 | convolution fusion | flops 2147549184 | bytes 35782656 | tf_op jit(solution)/shard_map/dot_general | solution.py:89
  (8 shorter events, 0.1 us)
Async XLA Ops:
  6.5 47.9 %all-gather.5.cloned.1.call-start = ((), (), s32[]{:S(2)}) async-start(), calls=%async_computation.2 | async-start | bytes 2228224 | tf_op jit(solution)/shard_map/all_gather | solution.py:40
  60.6 17.8 %all-to-all-start.1 = ((bf16[16,4,128]{2,1,0:T(4,128)(2,1)}), bf16[16,4,128]{2,1,0:T(4,128)(2,1)S(1)}, u32[]{:S(2)}, u32[]{:S(2)}) async-start(bf16[16,4,128]{2,1,0:T(4,128)(2,1)} %bitcast.2), calls=%async_computation.1 | async-start | bytes 32768 | tf_op jit(solution)/shard_map/all_to_all | solution.py:51
  78.4 13.9 %all-to-all-start = ((bf16[16,4,1024]{2,1,0:T(4,128)(2,1)}), bf16[16,4,1024]{2,1,0:T(4,128)(2,1)S(1)}, u32[]{:S(2)}, u32[]{:S(2)}) async-start(bf16[16,4,1024]{2,1,0:T(4,128)(2,1)} %all_to_all.24), calls=%async_computation | async-start | bytes 262144 | tf_op jit(solution)/shard_map/all_to_all | solution.py:50
  84.4 53.5 %all-gather.7.cloned.1.call-start = ((), (), s32[]{:S(2)}) async-start(), calls=%async_computation.3 | async-start | bytes 2228224 | tf_op jit(solution)/shard_map/all_gather | solution.py:90
  92.6 4.5 %copy-start = (bf16[4,8,512,128]{3,2,1,0:T(8,128)(2,1)S(1)}, bf16[4,8,512,128]{3,2,1,0:T(8,128)(2,1)}, u32[]{:S(2)}) copy-start(bf16[4,8,512,128]{3,2,1,0:T(8,128)(2,1)} %param.14) | copy-start | bytes 12582916
Sparse Core Ops, SparseCore 0:
  10.3 44.0 all-gather.4
  98.8 39.0 all-gather.6
where the time goes:
time: 162 us
  waiting for transfers between devices  89.7 us (55%)
  matrix products  36.2 us (22%)
  between operations  13.5 us (8%)
  starting transfers between devices  9.53 us (6%)
  local copies, waits for them, and re-layouts  6.73 us (4%)
  other arithmetic  5.85 us (4%)
    all_gather x1, waiting for transfers between devices, shards(): piece = lax.all_gather(normed, 'mp', axis=0, tiled=True)  42.7 us
    all_gather x1, waiting for transfers between devices, shards(): lax.all_gather(attended, 'mp', axis=0, tiled=True)  39.2 us
    dot_general x1, matrix products, shards(): jnp.dot(lax.all_gather(attended, 'mp', axis=0, tiled=True), o_weight, pre...  14.2 us
    dot_general x1, matrix products, shards(): jnp.dot(piece, q_weight, preferred_element_type=jnp.float32)  13.6 us
    all_to_all x1, waiting for transfers between devices, shards(): lax.all_to_all(projected[:, :query_cols], 'mp', split_axis=0, concat_axis...  7.7 us
    all_to_all x1, starting transfers between devices, shards(): lax.all_to_all(projected[:, :query_cols], 'mp', split_axis=0, concat_axis...  6 us
    unnamed x5, local copies, waits for them, and re-layouts  5.81 us
    dot_general x1, matrix products, shards(): jnp.einsum('rgqd,rgtd->rgqt', query, key_cache, preferred_element_type=jn...  3.73 us
  transfers between devices with their start and end apart: 4, of which 3 were waited for; matrix products, arithmetic and copies ran while one was open for 9% of the time, Pallas kernels for 0%

commit v1 on v0

--- a/solution.py
+++ b/solution.py
@@ -35,9 +35,47 @@
     return (widened * inverse * gain.astype(jnp.float32)).astype(jnp.bfloat16)
 
 
+def swap(block, size, distance):
+    return lax.ppermute(block, "mp", [(i, i ^ distance) for i in range(size)])
+
+
+def gather_blocks(block, size):
+    held = {0: block}
+    for far in (8, 4, 12):
+        if far < size:
+            held[far] = swap(block, size, far)
+    held[2] = swap(block, size, 2)
+    for far in (4, 8, 12):
+        if far < size:
+            held[far ^ 2] = swap(held[far], size, 2)
+    for even in range(0, size, 2):
+        held[even ^ 1] = swap(held[even], size, 1)
+    return [held[r] for r in range(size)]
+
+
+def gather_rows(block, size):
+    rows = block.shape[0]
+    if size not in (4, 8, 16):
+        gathered = lax.all_gather(block, "mp", axis=0, tiled=True)
+        return gathered, None
+    gathered = jnp.concatenate(gather_blocks(block, size), axis=0)
+    me = lax.axis_index("mp")
+    to = jnp.arange(size * rows, dtype=jnp.int32)[:, None]
+    source = jnp.arange(size * rows, dtype=jnp.int32)[None, :]
+    place = (to == ((source // rows) ^ me) * rows + source % rows).astype(block.dtype)
+    return gathered, place
+
+
+def in_order(place, values):
+    if place is None:
+        return values
+    return jnp.dot(place, values, preferred_element_type=jnp.float32).astype(values.dtype)
+
+
 def shards(activations, gain, q_weight, kv_weight, o_weight, key_cache, value_cache, lengths):
     normed = normalize(activations, gain)
-    piece = lax.all_gather(normed, "mp", axis=0, tiled=True)
+    size = lax.axis_size("mp")
+    piece, place = gather_rows(normed, size)
     projected = jnp.concatenate(
         [
             jnp.dot(piece, q_weight, preferred_element_type=jnp.float32),
@@ -45,6 +83,7 @@
         ],
         axis=1,
     ).astype(jnp.bfloat16)
+    projected = in_order(place, projected)
     query_cols = q_weight.shape[1]
     query_all, pairs_all = (
         lax.all_to_all(projected[:, :query_cols], "mp", split_axis=0, concat_axis=1, tiled=True),
@@ -86,12 +125,9 @@
         + own_prob.astype(jnp.float32)[..., None] * fresh_value.astype(jnp.float32)[:, :, None, :]
     )
     attended = mixed.reshape(requests, HEADS * HEAD_DIM).astype(jnp.bfloat16)
-    result = jnp.dot(
-        lax.all_gather(attended, "mp", axis=0, tiled=True),
-        o_weight,
-        preferred_element_type=jnp.float32,
-    )
-    return result.astype(jnp.bfloat16)
+    everyone, place = gather_rows(attended, size)
+    result = jnp.dot(everyone, o_weight, preferred_element_type=jnp.float32)
+    return in_order(place, result.astype(jnp.bfloat16))
 
 
 def solution(mesh):

time: 162 us -> 127 us (0.78)
  waiting for transfers between devices: 89.7 us -> 37.8 us
  starting transfers between devices: 9.53 us -> 30.8 us
  between operations: 13.5 us -> 0.29 us
  local copies, waits for them, and re-layouts: 6.73 us -> 15.5 us
    all_gather x2 -> x0, waiting for transfers between devices: 81.9 us -> none  [the longest x1 42.7 us: shards(): piece = lax.all_gather(normed, 'mp', axis=0, tiled=True)]
    ppermute x0 -> x30, waiting for transfers between devices: none -> 24.6 us  [swap(): return lax.ppermute(block, 'mp', [(i, i ^ distance) for i in range(size)])]
    ppermute x0 -> x30, starting transfers between devices: none -> 20.5 us  [swap(): return lax.ppermute(block, 'mp', [(i, i ^ distance) for i in range(size)])]
    concatenate x0 -> x2, local copies, waits for them, and re-layouts: none -> 11.6 us  [gather_rows(): gathered = jnp.concatenate(gather_blocks(block, size), axis=0)]
    all_to_all x1, waiting for transfers between devices: 0.01 us -> 5.67 us  [shards(): lax.all_to_all(projected[:, query_cols:], 'mp', split_axis=0, concat_axis...]
    unnamed x5 -> x23, local copies, waits for them, and re-layouts: 5.81 us -> 2.36 us
    dot_general x1 -> x2, matrix products: 14.2 us -> 17.4 us  [in_order(): jnp.dot(place, values, preferred_element_type=jnp.float32)]
    all_to_all x1, starting transfers between devices: 3.48 us -> 6.61 us  [shards(): lax.all_to_all(projected[:, query_cols:], 'mp', split_axis=0, concat_axis...]
  transfers between devices with their start and end apart: 4 -> 32, of which waited for: 3 -> 14; matrix products, arithmetic and copies ran while one was open for 9% -> 1% of each run, Pallas kernels for 0% -> 0%
where the time goes in v1:
time: 127 us; the launch traced here: 126 us
  waiting for transfers between devices  37.8 us (30%)
  matrix products  36.9 us (29%)
  starting transfers between devices  30.8 us (24%)
  local copies, waits for them, and re-layouts  15.5 us (12%)
  other arithmetic  4.54 us (4%)
    ppermute x30, waiting for transfers between devices, swap(): return lax.ppermute(block, 'mp', [(i, i ^ distance) for i in range(size)])  24.6 us
    ppermute x30, starting transfers between devices, swap(): return lax.ppermute(block, 'mp', [(i, i ^ distance) for i in range(size)])  20.5 us
    dot_general x2, matrix products, in_order(): jnp.dot(place, values, preferred_element_type=jnp.float32)  17.4 us
    dot_general x1, matrix products, shards(): jnp.dot(piece, q_weight, preferred_element_type=jnp.float32)  13.7 us
    concatenate x2, local copies, waits for them, and re-layouts, gather_rows(): gathered = jnp.concatenate(gather_blocks(block, size), axis=0)  11.6 us
    all_to_all x1, waiting for transfers between devices, shards(): lax.all_to_all(projected[:, :query_cols], 'mp', split_axis=0, concat_axis...  7.53 us
    all_to_all x1, starting transfers between devices, shards(): lax.all_to_all(projected[:, query_cols:], 'mp', split_axis=0, concat_axis...  6.61 us
    all_to_all x1, waiting for transfers between devices, shards(): lax.all_to_all(projected[:, query_cols:], 'mp', split_axis=0, concat_axis...  5.67 us
  transfers between devices with their start and end apart: 32, of which 14 were waited for; matrix products, arithmetic and copies ran while one was open for 1% of the time, Pallas kernels for 0%

profile of v1, /device:TPU:0, one launch (start us, length us, event | category | flops | bytes accessed | tf_op | source)
XLA Modules:
  0.0 125.9 jit_solution(10693265591183394167)
XLA Ops:
  0.0 0.8 convert_element_type.63
  0.8 1.2 fusion.7
  1.9 1.0 fusion.9
  3.0 4.1 %collective-permute-start.7 = (bf16[4,16384]{1,0:T(4,128)(2,1)S(1)}, bf16[4,16384]{1,0:T(4,128)(2,1)S(1)}, u32[]{:S(2)}, u32[]{:S(2)}) collective-permute-start(bf16[4,16384]{1,0:T(4,128)(2,1)S(1)} %fusion.9), channel_id=1, source_target_pairs={{0,8},{1,9},{2,10},{3,11},{4,12},{5,13},{6,14},{7,15},{8,0},{9,1},... | collective-permute-start | bytes 393224 | tf_op jit(solution)/shard_map/ppermute | solution.py:39
  7.1 1.3 %collective-permute-start.11 = (bf16[4,16384]{1,0:T(4,128)(2,1)S(1)}, bf16[4,16384]{1,0:T(4,128)(2,1)S(1)}, u32[]{:S(2)}, u32[]{:S(2)}) collective-permute-start(bf16[4,16384]{1,0:T(4,128)(2,1)S(1)} %fusion.9), channel_id=1, source_target_pairs={{0,12},{1,13},{2,14},{3,15},{4,8},{5,9},{6,10},{7,11},{8,4},{9,5},... | collective-permute-start | bytes 393224 | tf_op jit(solution)/shard_map/ppermute | solution.py:39
  8.4 0.2 collective-permute-start.3
  8.7 1.5 %collective-permute-start.1 = (bf16[4,16384]{1,0:T(4,128)(2,1)S(1)}, bf16[4,16384]{1,0:T(4,128)(2,1)S(1)}, u32[]{:S(2)}, u32[]{:S(2)}) collective-permute-start(bf16[4,16384]{1,0:T(4,128)(2,1)S(1)} %fusion.9), channel_id=1, source_target_pairs={{0,2},{1,3},{2,0},{3,1},{4,6},{5,7},{6,4},{7,5},{8,10},{9,11},{10,... | collective-permute-start | bytes 393224 | tf_op jit(solution)/shard_map/ppermute | solution.py:39
  10.2 6.9 %collective-permute-done.7 = bf16[4,16384]{1,0:T(4,128)(2,1)S(1)} collective-permute-done((bf16[4,16384]{1,0:T(4,128)(2,1)S(1)}, bf16[4,16384]{1,0:T(4,128)(2,1)S(1)}, u32[]{:S(2)}, u32[]{:S(2)}) %collective-permute-start.7) | collective-permute-done | bytes 131104 | tf_op jit(solution)/shard_map/ppermute | solution.py:39
  17.1 1.9 %collective-permute-start.9 = (bf16[4,16384]{1,0:T(4,128)(2,1)S(1)}, bf16[4,16384]{1,0:T(4,128)(2,1)S(1)}, u32[]{:S(2)}, u32[]{:S(2)}) collective-permute-start(bf16[4,16384]{1,0:T(4,128)(2,1)S(1)} %collective-permute-done.7), channel_id=1, source_target_pairs={{0,2},{1,3},{2,0},{3,1},{4,6},{5,7},{6,4},{7,5},{8,10},{9,11},{10,... | collective-permute-start | bytes 393224 | tf_op jit(solution)/shard_map/ppermute | solution.py:39
  18.9 0.2 collective-permute-start.13
  19.1 1.9 %collective-permute-start.5 = (bf16[4,16384]{1,0:T(4,128)(2,1)S(1)}, bf16[4,16384]{1,0:T(4,128)(2,1)S(1)}, u32[]{:S(2)}, u32[]{:S(2)}) collective-permute-start(bf16[4,16384]{1,0:T(4,128)(2,1)S(1)} %collective-permute-done.3), channel_id=1, source_target_pairs={{0,2},{1,3},{2,0},{3,1},{4,6},{5,7},{6,4},{7,5},{8,10},{9,11},{10,... | collective-permute-start | bytes 393224 | tf_op jit(solution)/shard_map/ppermute | solution.py:39
  21.0 0.5 collective-permute-start.4
  21.5 0.7 convert_element_type.69
  22.2 1.3 %collective-permute-done.9 = bf16[4,16384]{1,0:T(4,128)(2,1)S(1)} collective-permute-done((bf16[4,16384]{1,0:T(4,128)(2,1)S(1)}, bf16[4,16384]{1,0:T(4,128)(2,1)S(1)}, u32[]{:S(2)}, u32[]{:S(2)}) %collective-permute-start.9) | collective-permute-done | bytes 131104 | tf_op jit(solution)/shard_map/ppermute | solution.py:39
  23.5 1.6 %collective-permute-done.13 = bf16[4,16384]{1,0:T(4,128)(2,1)S(1)} collective-permute-done((bf16[4,16384]{1,0:T(4,128)(2,1)S(1)}, bf16[4,16384]{1,0:T(4,128)(2,1)S(1)}, u32[]{:S(2)}, u32[]{:S(2)}) %collective-permute-start.13) | collective-permute-done | bytes 131104 | tf_op jit(solution)/shard_map/ppermute | solution.py:39
  25.1 1.4 %collective-permute-done.5 = bf16[4,16384]{1,0:T(4,128)(2,1)S(1)} collective-permute-done((bf16[4,16384]{1,0:T(4,128)(2,1)S(1)}, bf16[4,16384]{1,0:T(4,128)(2,1)S(1)}, u32[]{:S(2)}, u32[]{:S(2)}) %collective-permute-start.5) | collective-permute-done | bytes 131104 | tf_op jit(solution)/shard_map/ppermute | solution.py:39
  26.5 0.5 collective-permute-start.14
  27.1 0.1 collective-permute-start.6
  27.1 0.1 multiply_cosine_fusion
  27.3 0.6 collective-permute-done.10
  27.9 0.2 collective-permute-done.14
  28.1 0.5 copy-done.3
  28.5 0.6 copy-done.5
  29.2 5.8 %concatenate.18 = bf16[64,16384]{1,0:T(8,128)(2,1)S(1)} concatenate(bf16[4,16384]{1,0:T(4,128)(2,1)S(1)} %fusion.9, bf16[4,16384]{1,0:T(4,128)(2,1)S(1)} %collective-permute-done, bf16[4,16384]{1,0:T(4,128)(2,1)S(1)} %collective-permute-done.1, bf16[4,16384]{1,0:T(4,128)(2,1)} %copy-done.2, bf16[4,16384]{1,0:T(4,128)(2,1)S(1)} %collective-permute-done.3, ...), dimensions={0} | concatenate | bytes 4194304 | tf_op jit(solution)/shard_map/concatenate | solution.py:61
  35.0 13.7 %convolution_convert_fusion.3 = bf16[64,1024]{1,0:T(8,128)(2,1)S(1)} fusion(bf16[64,16384]{1,0:T(8,128)(2,1)S(1)} %concatenate.18, bf16[16384,1024]{1,0:T(8,128)(2,1)} %param.10), kind=kOutput, calls=%fused_computation.7 | convolution fusion | flops 2147549184 | bytes 35782656 | tf_op jit(solution)/shard_map/dot_general | solution.py:81
  48.8 0.9 convolution_convert_fusion.4
  49.7 0.2 convolution_convert_fusion
  49.9 0.6 slice.35
  50.5 6.6 %all-to-all-start.1 = ((bf16[16,4,128]{2,1,0:T(4,128)(2,1)}), bf16[16,4,128]{2,1,0:T(4,128)(2,1)S(1)}, u32[]{:S(2)}, u32[]{:S(2)}) async-start(bf16[16,4,128]{2,1,0:T(4,128)(2,1)} %bitcast.1), calls=%async_computation.1 | async-start | bytes 32768 | tf_op jit(solution)/shard_map/all_to_all | solution.py:90
  57.1 0.1 iota_compare_fusion.3
  57.2 0.7 all_to_all.24
  57.9 5.7 %all-to-all-done.1 = bf16[16,4,128]{2,1,0:T(4,128)(2,1)S(1)} async-done(((bf16[16,4,128]{2,1,0:T(4,128)(2,1)}), bf16[16,4,128]{2,1,0:T(4,128)(2,1)S(1)}, u32[]{:S(2)}, u32[]{:S(2)}) %all-to-all-start.1) | async-done | bytes 16416 | tf_op jit(solution)/shard_map/all_to_all | solution.py:90
  63.6 3.7 %all-to-all-start = ((bf16[16,4,1024]{2,1,0:T(4,128)(2,1)}), bf16[16,4,1024]{2,1,0:T(4,128)(2,1)S(1)}, u32[]{:S(2)}, u32[]{:S(2)}) async-start(bf16[16,4,1024]{2,1,0:T(4,128)(2,1)} %all_to_all.24), calls=%async_computation | async-start | bytes 262144 | tf_op jit(solution)/shard_map/all_to_all | solution.py:89
  67.3 0.1 subtract_convert_fusion.1
  67.4 0.1 maximum_bitcast_fusion
  67.5 7.5 %all-to-all-done = bf16[16,4,1024]{2,1,0:T(4,128)(2,1)S(1)} async-done(((bf16[16,4,1024]{2,1,0:T(4,128)(2,1)}), bf16[16,4,1024]{2,1,0:T(4,128)(2,1)S(1)}, u32[]{:S(2)}, u32[]{:S(2)}) %all-to-all-start) | async-done | bytes 131104 | tf_op jit(solution)/shard_map/all_to_all | solution.py:89
  75.0 0.2 copy.9
  75.3 0.0 copy-start.10
  75.3 0.1 subtract_convert_fusion
  75.4 0.2 fusion.13
  75.7 3.7 %fusion.26 = (f32[4,8,16]{2,1,0:T(8,128)S(1)}, f32[4,8,16,512]{3,2,1,0:T(8,128)S(1)}) fusion(bf16[4,8,512,128]{3,2,1,0:T(8,128)(2,1)} %param.13, bf16[4,8,16,64]{3,2,1,0:T(8,128)(2,1)S(1)} %get-tuple-element.6, bf16[4,8,16,64]{3,2,1,0:T(8,128)(2,1)S(1)} %get-tuple-element.5, pred[4,512]{1,0:T(4,128)(4,1)S(1)} %iota_compare_fusion.3), kind=kOutput, calls=%fused_computation.63 | convolution fusion | flops 68156928 | bytes 5378048 | tf_op jit(solution)/shard_map/rgqd,rgtd->rgqt/dot_general | solution.py:108
  79.4 0.4 fusion.2
  79.8 0.8 fusion.1
  80.6 0.1 copy.20
  80.7 0.1 collective-permute-start.18
  80.8 1.2 collective-permute-start.22
  82.0 3.2 %collective-permute-start.26 = (bf16[4,16384]{1,0:T(4,128)(2,1)S(1)}, bf16[4,16384]{1,0:T(4,128)(2,1)S(1)}, u32[]{:S(2)}, u32[]{:S(2)}) collective-permute-start(bf16[4,16384]{1,0:T(4,128)(2,1)S(1)} %bitcast.33), channel_id=1, source_target_pairs={{0,12},{1,13},{2,14},{3,15},{4,8},{5,9},{6,10},{7,11},{8,4},{9,5},... | collective-permute-start | bytes 393224 | tf_op jit(solution)/shard_map/ppermute | solution.py:39
  85.2 2.2 %collective-permute-done.18 = bf16[4,16384]{1,0:T(4,128)(2,1)S(1)} collective-permute-done((bf16[4,16384]{1,0:T(4,128)(2,1)S(1)}, bf16[4,16384]{1,0:T(4,128)(2,1)S(1)}, u32[]{:S(2)}, u32[]{:S(2)}) %collective-permute-start.18) | collective-permute-done | bytes 131104 | tf_op jit(solution)/shard_map/ppermute | solution.py:39
  87.4 0.7 collective-permute-start.20
  88.1 5.7 %collective-permute-done.22 = bf16[4,16384]{1,0:T(4,128)(2,1)S(1)} collective-permute-done((bf16[4,16384]{1,0:T(4,128)(2,1)S(1)}, bf16[4,16384]{1,0:T(4,128)(2,1)S(1)}, u32[]{:S(2)}, u32[]{:S(2)}) %collective-permute-start.22) | collective-permute-done | bytes 131104 | tf_op jit(solution)/shard_map/ppermute | solution.py:39
  93.7 0.2 collective-permute-start.24
  94.0 1.8 %collective-permute-start.28 = (bf16[4,16384]{1,0:T(4,128)(2,1)S(1)}, bf16[4,16384]{1,0:T(4,128)(2,1)S(1)}, u32[]{:S(2)}, u32[]{:S(2)}) collective-permute-start(bf16[4,16384]{1,0:T(4,128)(2,1)S(1)} %collective-permute-done.26), channel_id=1, source_target_pairs={{0,2},{1,3},{2,0},{3,1},{4,6},{5,7},{6,4},{7,5},{8,10},{9,11},{10,... | collective-permute-start | bytes 393224 | tf_op jit(solution)/shard_map/ppermute | solution.py:39
  95.8 0.5 collective-permute-start.19
  96.3 0.1 collective-permute-start.23
  96.4 2.3 %collective-permute-done.24 = bf16[4,16384]{1,0:T(4,128)(2,1)S(1)} collective-permute-done((bf16[4,16384]{1,0:T(4,128)(2,1)S(1)}, bf16[4,16384]{1,0:T(4,128)(2,1)S(1)}, u32[]{:S(2)}, u32[]{:S(2)}) %collective-permute-start.24) | collective-permute-done | bytes 131104 | tf_op jit(solution)/shard_map/ppermute | solution.py:39
  98.7 1.4 %collective-permute-done.28 = bf16[4,16384]{1,0:T(4,128)(2,1)S(1)} collective-permute-done((bf16[4,16384]{1,0:T(4,128)(2,1)S(1)}, bf16[4,16384]{1,0:T(4,128)(2,1)S(1)}, u32[]{:S(2)}, u32[]{:S(2)}) %collective-permute-start.28) | collective-permute-done | bytes 131104 | tf_op jit(solution)/shard_map/ppermute | solution.py:39
  100.1 0.5 collective-permute-start.25
  100.6 0.1 collective-permute-start.29
  100.7 0.7 collective-permute-done.21
  101.5 0.2 collective-permute-done.25
  101.7 0.5 copy-done.7
  102.1 0.6 copy-done.8
  102.8 5.8 %concatenate.22 = bf16[64,16384]{1,0:T(8,128)(2,1)S(1)} concatenate(bf16[4,16384]{1,0:T(4,128)(2,1)S(1)} %bitcast.36, bf16[4,16384]{1,0:T(4,128)(2,1)S(1)} %collective-permute-done.15, bf16[4,16384]{1,0:T(4,128)(2,1)S(1)} %collective-permute-done.16, bf16[4,16384]{1,0:T(4,128)(2,1)S(1)} %collective-permute-done.17, bf16[4,16384]{1,0:T(4,128)(2,1)S(1)} %collective-permute-done.18, ...), dimensions={0} | concatenate | bytes 4194304 | tf_op jit(solution)/shard_map/concatenate | solution.py:61
  108.6 17.3 %convolution_convert_fusion.1 = bf16[64,1024]{1,0:T(8,128)(2,1)} fusion(bf16[64,16384]{1,0:T(8,128)(2,1)S(1)} %concatenate.22, bf16[16384,1024]{1,0:T(8,128)(2,1)} %param.12, s32[64]{0:T(128)S(1)} %fusion.19), kind=kOutput, calls=%fused_computation.5 | convolution fusion | flops 2156007424 | bytes 35782912 | tf_op jit(solution)/shard_map/dot_general | solution.py:72
  (55 shorter events, 0.2 us)
Async XLA Ops:
  3.0 14.1 %collective-permute-start.7 = (bf16[4,16384]{1,0:T(4,128)(2,1)S(1)}, bf16[4,16384]{1,0:T(4,128)(2,1)S(1)}, u32[]{:S(2)}, u32[]{:S(2)}) collective-permute-start(bf16[4,16384]{1,0:T(4,128)(2,1)S(1)} %fusion.9), channel_id=1, source_target_pairs={{0,8},{1,9},{2,10},{3,11},{4,12},{5,13},{6,14},{7,15},{8,0},{9,1},... | collective-permute-start | bytes 393224 | tf_op jit(solution)/shard_map/ppermute | solution.py:39
  7.1 11.9 %collective-permute-start.11 = (bf16[4,16384]{1,0:T(4,128)(2,1)S(1)}, bf16[4,16384]{1,0:T(4,128)(2,1)S(1)}, u32[]{:S(2)}, u32[]{:S(2)}) collective-permute-start(bf16[4,16384]{1,0:T(4,128)(2,1)S(1)} %fusion.9), channel_id=1, source_target_pairs={{0,12},{1,13},{2,14},{3,15},{4,8},{5,9},{6,10},{7,11},{8,4},{9,5},... | collective-permute-start | bytes 393224 | tf_op jit(solution)/shard_map/ppermute | solution.py:39
  8.4 10.7 %collective-permute-start.3 = (bf16[4,16384]{1,0:T(4,128)(2,1)S(1)}, bf16[4,16384]{1,0:T(4,128)(2,1)S(1)}, u32[]{:S(2)}, u32[]{:S(2)}) collective-permute-start(bf16[4,16384]{1,0:T(4,128)(2,1)S(1)} %fusion.9), channel_id=1, source_target_pairs={{0,4},{1,5},{2,6},{3,7},{4,0},{5,1},{6,2},{7,3},{8,12},{9,13},{10,... | collective-permute-start | bytes 393224 | tf_op jit(solution)/shard_map/ppermute | solution.py:39
  8.7 12.3 %collective-permute-start.1 = (bf16[4,16384]{1,0:T(4,128)(2,1)S(1)}, bf16[4,16384]{1,0:T(4,128)(2,1)S(1)}, u32[]{:S(2)}, u32[]{:S(2)}) collective-permute-start(bf16[4,16384]{1,0:T(4,128)(2,1)S(1)} %fusion.9), channel_id=1, source_target_pairs={{0,2},{1,3},{2,0},{3,1},{4,6},{5,7},{6,4},{7,5},{8,10},{9,11},{10,... | collective-permute-start | bytes 393224 | tf_op jit(solution)/shard_map/ppermute | solution.py:39
  10.2 10.8 %collective-permute-start = (bf16[4,16384]{1,0:T(4,128)(2,1)S(1)}, bf16[4,16384]{1,0:T(4,128)(2,1)S(1)}, u32[]{:S(2)}, u32[]{:S(2)}) collective-permute-start(bf16[4,16384]{1,0:T(4,128)(2,1)S(1)} %fusion.9), channel_id=1, source_target_pairs={{0,1},{1,0},{2,3},{3,2},{4,5},{5,4},{6,7},{7,6},{8,9},{9,8},{10,11... | collective-permute-start | bytes 393224 | tf_op jit(solution)/shard_map/ppermute | solution.py:39
  17.1 6.4 %collective-permute-start.9 = (bf16[4,16384]{1,0:T(4,128)(2,1)S(1)}, bf16[4,16384]{1,0:T(4,128)(2,1)S(1)}, u32[]{:S(2)}, u32[]{:S(2)}) collective-permute-start(bf16[4,16384]{1,0:T(4,128)(2,1)S(1)} %collective-permute-done.7), channel_id=1, source_target_pairs={{0,2},{1,3},{2,0},{3,1},{4,6},{5,7},{6,4},{7,5},{8,10},{9,11},{10,... | collective-permute-start | bytes 393224 | tf_op jit(solution)/shard_map/ppermute | solution.py:39
  18.9 6.2 %collective-permute-start.13 = (bf16[4,16384]{1,0:T(4,128)(2,1)S(1)}, bf16[4,16384]{1,0:T(4,128)(2,1)S(1)}, u32[]{:S(2)}, u32[]{:S(2)}) collective-permute-start(bf16[4,16384]{1,0:T(4,128)(2,1)S(1)} %collective-permute-done.11), channel_id=1, source_target_pairs={{0,2},{1,3},{2,0},{3,1},{4,6},{5,7},{6,4},{7,5},{8,10},{9,11},{10,... | collective-permute-start | bytes 393224 | tf_op jit(solution)/shard_map/ppermute | solution.py:39
  19.1 7.4 %collective-permute-start.5 = (bf16[4,16384]{1,0:T(4,128)(2,1)S(1)}, bf16[4,16384]{1,0:T(4,128)(2,1)S(1)}, u32[]{:S(2)}, u32[]{:S(2)}) collective-permute-start(bf16[4,16384]{1,0:T(4,128)(2,1)S(1)} %collective-permute-done.3), channel_id=1, source_target_pairs={{0,2},{1,3},{2,0},{3,1},{4,6},{5,7},{6,4},{7,5},{8,10},{9,11},{10,... | collective-permute-start | bytes 393224 | tf_op jit(solution)/shard_map/ppermute | solution.py:39
  21.0 5.6 %collective-permute-start.12 = (bf16[4,16384]{1,0:T(4,128)(2,1)S(1)}, bf16[4,16384]{1,0:T(4,128)(2,1)S(1)}, u32[]{:S(2)}, u32[]{:S(2)}) collective-permute-start(bf16[4,16384]{1,0:T(4,128)(2,1)S(1)} %collective-permute-done.11), channel_id=1, source_target_pairs={{0,1},{1,0},{2,3},{3,2},{4,5},{5,4},{6,7},{7,6},{8,9},{9,8},{10,11... | collective-permute-start | bytes 393224 | tf_op jit(solution)/shard_map/ppermute | solution.py:39
  21.0 6.1 %collective-permute-start.4 = (bf16[4,16384]{1,0:T(4,128)(2,1)S(1)}, bf16[4,16384]{1,0:T(4,128)(2,1)S(1)}, u32[]{:S(2)}, u32[]{:S(2)}) collective-permute-start(bf16[4,16384]{1,0:T(4,128)(2,1)S(1)} %collective-permute-done.3), channel_id=1, source_target_pairs={{0,1},{1,0},{2,3},{3,2},{4,5},{5,4},{6,7},{7,6},{8,9},{9,8},{10,11... | collective-permute-start | bytes 393224 | tf_op jit(solution)/shard_map/ppermute | solution.py:39
  23.5 3.8 %collective-permute-start.8 = (bf16[4,16384]{1,0:T(4,128)(2,1)S(1)}, bf16[4,16384]{1,0:T(4,128)(2,1)S(1)}, u32[]{:S(2)}, u32[]{:S(2)}) collective-permute-start(bf16[4,16384]{1,0:T(4,128)(2,1)S(1)} %collective-permute-done.7), channel_id=1, source_target_pairs={{0,1},{1,0},{2,3},{3,2},{4,5},{5,4},{6,7},{7,6},{8,9},{9,8},{10,11... | collective-permute-start | bytes 393224 | tf_op jit(solution)/shard_map/ppermute | solution.py:39
  25.1 2.1 %collective-permute-start.2 = (bf16[4,16384]{1,0:T(4,128)(2,1)S(1)}, bf16[4,16384]{1,0:T(4,128)(2,1)S(1)}, u32[]{:S(2)}, u32[]{:S(2)}) collective-permute-start(bf16[4,16384]{1,0:T(4,128)(2,1)S(1)} %collective-permute-done.1), channel_id=1, source_target_pairs={{0,1},{1,0},{2,3},{3,2},{4,5},{5,4},{6,7},{7,6},{8,9},{9,8},{10,11... | collective-permute-start | bytes 393224 | tf_op jit(solution)/shard_map/ppermute | solution.py:39
  26.5 1.3 %collective-permute-start.10 = (bf16[4,16384]{1,0:T(4,128)(2,1)S(1)}, bf16[4,16384]{1,0:T(4,128)(2,1)S(1)}, u32[]{:S(2)}, u32[]{:S(2)}) collective-permute-start(bf16[4,16384]{1,0:T(4,128)(2,1)S(1)} %collective-permute-done.9), channel_id=1, source_target_pairs={{0,1},{1,0},{2,3},{3,2},{4,5},{5,4},{6,7},{7,6},{8,9},{9,8},{10,11... | collective-permute-start | bytes 393224 | tf_op jit(solution)/shard_map/ppermute | solution.py:39
  26.5 1.5 %collective-permute-start.14 = (bf16[4,16384]{1,0:T(4,128)(2,1)S(1)}, bf16[4,16384]{1,0:T(4,128)(2,1)S(1)}, u32[]{:S(2)}, u32[]{:S(2)}) collective-permute-start(bf16[4,16384]{1,0:T(4,128)(2,1)S(1)} %collective-permute-done.13), channel_id=1, source_target_pairs={{0,1},{1,0},{2,3},{3,2},{4,5},{5,4},{6,7},{7,6},{8,9},{9,8},{10,11... | collective-permute-start | bytes 393224 | tf_op jit(solution)/shard_map/ppermute | solution.py:39
  27.1 2.1 %collective-permute-start.6 = (bf16[4,16384]{1,0:T(4,128)(2,1)S(1)}, bf16[4,16384]{1,0:T(4,128)(2,1)}, u32[]{:S(2)}, u32[]{:S(2)}) collective-permute-start(bf16[4,16384]{1,0:T(4,128)(2,1)S(1)} %collective-permute-done.5), channel_id=1, source_target_pairs={{0,1},{1,0},{2,3},{3,2},{4,5},{5,4},{6,7},{7,6},{8,9},{9,8},{10,11... | collective-permute-start | bytes 393224 | tf_op jit(solution)/shard_map/ppermute | solution.py:39
  27.3 0.8 copy-start.1
  27.3 0.8 copy-start.2
  27.9 0.7 copy-start.3
  28.5 0.6 copy-start.5
  35.0 13.8 %copy-start = (bf16[16384,128]{1,0:T(8,128)(2,1)S(1)}, bf16[16384,128]{1,0:T(8,128)(2,1)}, u32[]{:S(2)}) copy-start(bf16[16384,128]{1,0:T(8,128)(2,1)} %param.11) | copy-start | bytes 12582916
  48.8 8.3 %copy-start.9 = (s32[4]{0:T(128)S(1)}, s32[4]{0:T(128)}, u32[]{:S(2)}) copy-start(s32[4]{0:T(128)} %param.15) | copy-start | bytes 52
  50.5 13.1 %all-to-all-start.1 = ((bf16[16,4,128]{2,1,0:T(4,128)(2,1)}), bf16[16,4,128]{2,1,0:T(4,128)(2,1)S(1)}, u32[]{:S(2)}, u32[]{:S(2)}) async-start(bf16[16,4,128]{2,1,0:T(4,128)(2,1)} %bitcast.1), calls=%async_computation.1 | async-start | bytes 32768 | tf_op jit(solution)/shard_map/all_to_all | solution.py:90
  63.6 11.4 %all-to-all-start = ((bf16[16,4,1024]{2,1,0:T(4,128)(2,1)}), bf16[16,4,1024]{2,1,0:T(4,128)(2,1)S(1)}, u32[]{:S(2)}, u32[]{:S(2)}) async-start(bf16[16,4,1024]{2,1,0:T(4,128)(2,1)} %all_to_all.24), calls=%async_computation | async-start | bytes 262144 | tf_op jit(solution)/shard_map/all_to_all | solution.py:89
  75.3 4.5 %copy-start.10 = (bf16[4,8,512,128]{3,2,1,0:T(8,128)(2,1)S(1)}, bf16[4,8,512,128]{3,2,1,0:T(8,128)(2,1)}, u32[]{:S(2)}) copy-start(bf16[4,8,512,128]{3,2,1,0:T(8,128)(2,1)} %param.14) | copy-start | bytes 12582916
  80.7 6.6 %collective-permute-start.18 = (bf16[4,16384]{1,0:T(4,128)(2,1)S(1)}, bf16[4,16384]{1,0:T(4,128)(2,1)S(1)}, u32[]{:S(2)}, u32[]{:S(2)}) collective-permute-start(bf16[4,16384]{1,0:T(4,128)(2,1)S(1)} %bitcast.31), channel_id=1, source_target_pairs={{0,4},{1,5},{2,6},{3,7},{4,0},{5,1},{6,2},{7,3},{8,12},{9,13},{10,... | collective-permute-start | bytes 393224 | tf_op jit(solution)/shard_map/ppermute | solution.py:39
  80.8 12.9 %collective-permute-start.22 = (bf16[4,16384]{1,0:T(4,128)(2,1)S(1)}, bf16[4,16384]{1,0:T(4,128)(2,1)S(1)}, u32[]{:S(2)}, u32[]{:S(2)}) collective-permute-start(bf16[4,16384]{1,0:T(4,128)(2,1)S(1)} %bitcast.32), channel_id=1, source_target_pairs={{0,8},{1,9},{2,10},{3,11},{4,12},{5,13},{6,14},{7,15},{8,0},{9,1},... | collective-permute-start | bytes 393224 | tf_op jit(solution)/shard_map/ppermute | solution.py:39
  82.0 12.0 %collective-permute-start.26 = (bf16[4,16384]{1,0:T(4,128)(2,1)S(1)}, bf16[4,16384]{1,0:T(4,128)(2,1)S(1)}, u32[]{:S(2)}, u32[]{:S(2)}) collective-permute-start(bf16[4,16384]{1,0:T(4,128)(2,1)S(1)} %bitcast.33), channel_id=1, source_target_pairs={{0,12},{1,13},{2,14},{3,15},{4,8},{5,9},{6,10},{7,11},{8,4},{9,5},... | collective-permute-start | bytes 393224 | tf_op jit(solution)/shard_map/ppermute | solution.py:39
  85.2 10.6 %collective-permute-start.16 = (bf16[4,16384]{1,0:T(4,128)(2,1)S(1)}, bf16[4,16384]{1,0:T(4,128)(2,1)S(1)}, u32[]{:S(2)}, u32[]{:S(2)}) collective-permute-start(bf16[4,16384]{1,0:T(4,128)(2,1)S(1)} %bitcast.34), channel_id=1, source_target_pairs={{0,2},{1,3},{2,0},{3,1},{4,6},{5,7},{6,4},{7,5},{8,10},{9,11},{10,... | collective-permute-start | bytes 393224 | tf_op jit(solution)/shard_map/ppermute | solution.py:39
  85.2 10.6 %collective-permute-start.15 = (bf16[4,16384]{1,0:T(4,128)(2,1)S(1)}, bf16[4,16384]{1,0:T(4,128)(2,1)S(1)}, u32[]{:S(2)}, u32[]{:S(2)}) collective-permute-start(bf16[4,16384]{1,0:T(4,128)(2,1)S(1)} %bitcast.35), channel_id=1, source_target_pairs={{0,1},{1,0},{2,3},{3,2},{4,5},{5,4},{6,7},{7,6},{8,9},{9,8},{10,11... | collective-permute-start | bytes 393224 | tf_op jit(solution)/shard_map/ppermute | solution.py:39
  87.4 8.9 %collective-permute-start.20 = (bf16[4,16384]{1,0:T(4,128)(2,1)S(1)}, bf16[4,16384]{1,0:T(4,128)(2,1)S(1)}, u32[]{:S(2)}, u32[]{:S(2)}) collective-permute-start(bf16[4,16384]{1,0:T(4,128)(2,1)S(1)} %collective-permute-done.18), channel_id=1, source_target_pairs={{0,2},{1,3},{2,0},{3,1},{4,6},{5,7},{6,4},{7,5},{8,10},{9,11},{10,... | collective-permute-start | bytes 393224 | tf_op jit(solution)/shard_map/ppermute | solution.py:39
  93.7 5.0 %collective-permute-start.24 = (bf16[4,16384]{1,0:T(4,128)(2,1)S(1)}, bf16[4,16384]{1,0:T(4,128)(2,1)S(1)}, u32[]{:S(2)}, u32[]{:S(2)}) collective-permute-start(bf16[4,16384]{1,0:T(4,128)(2,1)S(1)} %collective-permute-done.22), channel_id=1, source_target_pairs={{0,2},{1,3},{2,0},{3,1},{4,6},{5,7},{6,4},{7,5},{8,10},{9,11},{10,... | collective-permute-start | bytes 393224 | tf_op jit(solution)/shard_map/ppermute | solution.py:39
  94.0 6.1 %collective-permute-start.28 = (bf16[4,16384]{1,0:T(4,128)(2,1)S(1)}, bf16[4,16384]{1,0:T(4,128)(2,1)S(1)}, u32[]{:S(2)}, u32[]{:S(2)}) collective-permute-start(bf16[4,16384]{1,0:T(4,128)(2,1)S(1)} %collective-permute-done.26), channel_id=1, source_target_pairs={{0,2},{1,3},{2,0},{3,1},{4,6},{5,7},{6,4},{7,5},{8,10},{9,11},{10,... | collective-permute-start | bytes 393224 | tf_op jit(solution)/shard_map/ppermute | solution.py:39
  95.8 4.3 %collective-permute-start.17 = (bf16[4,16384]{1,0:T(4,128)(2,1)S(1)}, bf16[4,16384]{1,0:T(4,128)(2,1)S(1)}, u32[]{:S(2)}, u32[]{:S(2)}) collective-permute-start(bf16[4,16384]{1,0:T(4,128)(2,1)S(1)} %collective-permute-done.16), channel_id=1, source_target_pairs={{0,1},{1,0},{2,3},{3,2},{4,5},{5,4},{6,7},{7,6},{8,9},{9,8},{10,11... | collective-permute-start | bytes 393224 | tf_op jit(solution)/shard_map/ppermute | solution.py:39
  95.8 4.8 %collective-permute-start.19 = (bf16[4,16384]{1,0:T(4,128)(2,1)S(1)}, bf16[4,16384]{1,0:T(4,128)(2,1)S(1)}, u32[]{:S(2)}, u32[]{:S(2)}) collective-permute-start(bf16[4,16384]{1,0:T(4,128)(2,1)S(1)} %collective-permute-done.18), channel_id=1, source_target_pairs={{0,1},{1,0},{2,3},{3,2},{4,5},{5,4},{6,7},{7,6},{8,9},{9,8},{10,11... | collective-permute-start | bytes 393224 | tf_op jit(solution)/shard_map/ppermute | solution.py:39
  96.3 4.4 %collective-permute-start.23 = (bf16[4,16384]{1,0:T(4,128)(2,1)S(1)}, bf16[4,16384]{1,0:T(4,128)(2,1)S(1)}, u32[]{:S(2)}, u32[]{:S(2)}) collective-permute-start(bf16[4,16384]{1,0:T(4,128)(2,1)S(1)} %collective-permute-done.22), channel_id=1, source_target_pairs={{0,1},{1,0},{2,3},{3,2},{4,5},{5,4},{6,7},{7,6},{8,9},{9,8},{10,11... | collective-permute-start | bytes 393224 | tf_op jit(solution)/shard_map/ppermute | solution.py:39
  98.7 2.0 %collective-permute-start.27 = (bf16[4,16384]{1,0:T(4,128)(2,1)S(1)}, bf16[4,16384]{1,0:T(4,128)(2,1)S(1)}, u32[]{:S(2)}, u32[]{:S(2)}) collective-permute-start(bf16[4,16384]{1,0:T(4,128)(2,1)S(1)} %collective-permute-done.26), channel_id=1, source_target_pairs={{0,1},{1,0},{2,3},{3,2},{4,5},{5,4},{6,7},{7,6},{8,9},{9,8},{10,11... | collective-permute-start | bytes 393224 | tf_op jit(solution)/shard_map/ppermute | solution.py:39
  100.1 1.3 %collective-permute-start.21 = (bf16[4,16384]{1,0:T(4,128)(2,1)S(1)}, bf16[4,16384]{1,0:T(4,128)(2,1)S(1)}, u32[]{:S(2)}, u32[]{:S(2)}) collective-permute-start(bf16[4,16384]{1,0:T(4,128)(2,1)S(1)} %collective-permute-done.20), channel_id=1, source_target_pairs={{0,1},{1,0},{2,3},{3,2},{4,5},{5,4},{6,7},{7,6},{8,9},{9,8},{10,11... | collective-permute-start | bytes 393224 | tf_op jit(solution)/shard_map/ppermute | solution.py:39
  100.1 1.5 %collective-permute-start.25 = (bf16[4,16384]{1,0:T(4,128)(2,1)S(1)}, bf16[4,16384]{1,0:T(4,128)(2,1)S(1)}, u32[]{:S(2)}, u32[]{:S(2)}) collective-permute-start(bf16[4,16384]{1,0:T(4,128)(2,1)S(1)} %collective-permute-done.24), channel_id=1, source_target_pairs={{0,1},{1,0},{2,3},{3,2},{4,5},{5,4},{6,7},{7,6},{8,9},{9,8},{10,11... | collective-permute-start | bytes 393224 | tf_op jit(solution)/shard_map/ppermute | solution.py:39
  100.6 2.1 %collective-permute-start.29 = (bf16[4,16384]{1,0:T(4,128)(2,1)S(1)}, bf16[4,16384]{1,0:T(4,128)(2,1)}, u32[]{:S(2)}, u32[]{:S(2)}) collective-permute-start(bf16[4,16384]{1,0:T(4,128)(2,1)S(1)} %collective-permute-done.28), channel_id=1, source_target_pairs={{0,1},{1,0},{2,3},{3,2},{4,5},{5,4},{6,7},{7,6},{8,9},{9,8},{10,11... | collective-permute-start | bytes 393224 | tf_op jit(solution)/shard_map/ppermute | solution.py:39
  100.7 0.9 copy-start.4
  100.7 0.9 copy-start.6
  101.5 0.7 copy-start.7
  102.1 0.6 copy-start.8

commit v2 on v0

--- a/solution.py
+++ b/solution.py
@@ -1,8 +1,11 @@
+import functools
 import math
 
 import jax
 import jax.numpy as jnp
 from jax import lax
+from jax.experimental import pallas as pl
+from jax.experimental.pallas import tpu as pltpu
 from jax.sharding import PartitionSpec as P
 
 HEADS = 128
@@ -10,9 +13,16 @@
 HEAD_DIM = 128
 CACHE = 512
 
+MIB = 1 << 20
+STEP = 2048
+LANES = 128
 
 rope_base = 500000.0
 norm_eps = 1e-05
+
+IN_VMEM = pl.BlockSpec(memory_space=pltpu.VMEM)
+IN_HBM = pl.BlockSpec(memory_space=pltpu.HBM)
+IN_SMEM = pl.BlockSpec(memory_space=pltpu.SMEM)
 
 
 def rotate(vector, position):
@@ -29,27 +39,178 @@
     )
 
 
+def norm_kernel(x_hbm, gain_hbm, out_ref, x_ref, gain_ref, sems):
+    copies = [
+        pltpu.make_async_copy(x_hbm, x_ref, sems.at[0]),
+        pltpu.make_async_copy(gain_hbm, gain_ref, sems.at[1]),
+    ]
+    for copy in copies:
+        copy.start()
+    for copy in copies:
+        copy.wait()
+    widened = x_ref[...].astype(jnp.float32)
+    inverse = lax.rsqrt(jnp.mean(widened * widened, axis=-1, keepdims=True) + norm_eps)
+    lanes = gain_ref.shape[1]
+    for j in range(gain_ref.shape[0]):
+        columns = pl.ds(j * lanes, lanes)
+        gain = gain_ref[pl.ds(j, 1), :].astype(jnp.float32)
+        out_ref[:, columns] = (x_ref[:, columns].astype(jnp.float32) * inverse * gain).astype(
+            out_ref.dtype
+        )
+
+
 def normalize(activations, gain):
-    widened = activations.astype(jnp.float32)
-    inverse = lax.rsqrt(jnp.mean(widened * widened, axis=-1, keepdims=True) + norm_eps)
-    return (widened * inverse * gain.astype(jnp.float32)).astype(jnp.bfloat16)
-
-
-def shards(activations, gain, q_weight, kv_weight, o_weight, key_cache, value_cache, lengths):
-    normed = normalize(activations, gain)
-    piece = lax.all_gather(normed, "mp", axis=0, tiled=True)
-    projected = jnp.concatenate(
-        [
-            jnp.dot(piece, q_weight, preferred_element_type=jnp.float32),
-            jnp.dot(piece, kv_weight, preferred_element_type=jnp.float32),
+    return pl.pallas_call(
+        norm_kernel,
+        out_shape=pltpu.VMEM(activations.shape, jnp.bfloat16),
+        in_specs=[IN_HBM, IN_HBM],
+        out_specs=IN_VMEM,
+        scratch_shapes=[
+            pltpu.VMEM(activations.shape, activations.dtype),
+            pltpu.VMEM((gain.shape[0] // LANES, LANES), gain.dtype),
+            pltpu.SemaphoreType.DMA((2,)),
         ],
-        axis=1,
-    ).astype(jnp.bfloat16)
-    query_cols = q_weight.shape[1]
-    query_all, pairs_all = (
-        lax.all_to_all(projected[:, :query_cols], "mp", split_axis=0, concat_axis=1, tiled=True),
-        lax.all_to_all(projected[:, query_cols:], "mp", split_axis=0, concat_axis=1, tiled=True),
-    )
+        compiler_params=pltpu.CompilerParams(vmem_limit_bytes=56 * MIB),
+        name="norm",
+    )(activations, gain.reshape(-1, LANES))
+
+
+def swap(block, size, distance):
+    return lax.ppermute(block, "mp", [(i, i ^ distance) for i in range(size)])
+
+
+def gather_blocks(block, size):
+    held = {0: block}
+    for far in (8, 4, 12):
+        if far < size:
+            held[far] = swap(block, size, far)
+    held[2] = swap(block, size, 2)
+    for far in (4, 8, 12):
+        if far < size:
+            held[far ^ 2] = swap(held[far], size, 2)
+    for even in range(0, size, 2):
+        held[even ^ 1] = swap(held[even], size, 1)
+    return [held[r] for r in range(size)]
+
+
+def load_kernel(parts, w_ref, out_ref, sems):
+    rows = out_ref.shape[0] // parts
+    copies = [
+        pltpu.make_async_copy(
+            w_ref.at[pl.ds(i * rows, rows)], out_ref.at[pl.ds(i * rows, rows)], sems.at[i]
+        )
+        for i in range(parts)
+    ]
+    for copy in copies:
+        copy.start()
+    for copy in copies:
+        copy.wait()
+
+
+def load(weight, rows):
+    parts = 4
+    return pl.pallas_call(
+        functools.partial(load_kernel, parts),
+        out_shape=pltpu.VMEM((rows, weight.shape[1]), weight.dtype),
+        in_specs=[IN_HBM],
+        out_specs=IN_VMEM,
+        scratch_shapes=[pltpu.SemaphoreType.DMA((parts,))],
+        cost_estimate=pl.CostEstimate(
+            flops=0, bytes_accessed=rows * weight.shape[1] * 2, transcendentals=0
+        ),
+        compiler_params=pltpu.CompilerParams(vmem_limit_bytes=36 * MIB),
+        name="load",
+    )(weight)
+
+
+def product_kernel(count, streamed, ordered, *refs):
+    me_ref, blocks, resident = refs[0], refs[1 : 1 + count], refs[1 + count]
+    weights = refs[2 + count : 2 + count + streamed]
+    out_ref = refs[2 + count + streamed]
+    buffers = refs[3 + count + streamed : 3 + count + 2 * streamed]
+    total, sems = refs[3 + count + 2 * streamed :]
+    depth = blocks[0].shape[1]
+    rows = blocks[0].shape[0]
+    held = resident.shape[0]
+    main = resident.shape[1]
+    copies = {}
+    for w, (weight, buffer) in enumerate(zip(weights, buffers)):
+        first = held if w == 0 else 0
+        for at in range(first, depth, STEP):
+            copies[w, at] = pltpu.make_async_copy(
+                weight.at[pl.ds(at, STEP)],
+                buffer.at[pl.ds(at - first, STEP)],
+                sems.at[w, at // STEP],
+            )
+    for key in sorted(copies, key=lambda k: (k[1], k[0])):
+        copies[key].start()
+
+    def joined(at):
+        return jnp.concatenate([block[:, pl.ds(at, STEP)] for block in blocks], axis=0)
+
+    for at in range(0, depth, STEP):
+        x = joined(at)
+        column = 0
+        for w, (weight, buffer) in enumerate(zip(weights, buffers)):
+            if (w, at) in copies:
+                copies[w, at].wait()
+                piece = buffer[pl.ds(at - (held if w == 0 else 0), STEP), :]
+            else:
+                piece = resident[pl.ds(at, STEP), :]
+            columns = pl.ds(column, weight.shape[1])
+            term = jnp.dot(x, piece, preferred_element_type=jnp.float32)
+            if at == 0:
+                total[:, columns] = term
+            else:
+                total[:, columns] += term
+            column += weight.shape[1]
+    me = me_ref[0]
+    if ordered:
+        to = lax.broadcasted_iota(jnp.int32, (count * rows, count * rows), 0)
+        source = lax.broadcasted_iota(jnp.int32, (count * rows, count * rows), 1)
+        place = to == ((source // rows) ^ me) * rows + source % rows
+        out_ref[...] = jnp.dot(
+            place.astype(jnp.bfloat16),
+            total[...].astype(jnp.bfloat16),
+            preferred_element_type=jnp.float32,
+        ).astype(out_ref.dtype)
+    else:
+        for r in range(count):
+            out_ref[me ^ r] = total[pl.ds(r * rows, rows), :].astype(out_ref.dtype)
+
+
+def product(me, blocks, resident, weights, ordered):
+    count, (rows, depth) = len(blocks), blocks[0].shape
+    columns = sum(w.shape[1] for w in weights)
+    held = resident.shape[0]
+    shape = (count * rows, columns) if ordered else (count, rows, columns)
+    spaces = [
+        pltpu.VMEM((depth - (held if i == 0 else 0), w.shape[1]), w.dtype)
+        for i, w in enumerate(weights)
+    ]
+    pinned = [pltpu.with_memory_space_constraint(b, pltpu.VMEM) for b in blocks]
+    streamed_bytes = sum(2 * s.shape[0] * s.shape[1] for s in spaces)
+    return pl.pallas_call(
+        functools.partial(product_kernel, count, len(weights), ordered),
+        out_shape=jax.ShapeDtypeStruct(shape, jnp.bfloat16),
+        in_specs=[IN_SMEM] + [IN_VMEM] * (count + 1) + [IN_HBM] * len(weights),
+        out_specs=IN_VMEM,
+        scratch_shapes=[
+            *spaces,
+            pltpu.VMEM((count * rows, columns), jnp.float32),
+            pltpu.SemaphoreType.DMA((len(weights), depth // STEP)),
+        ],
+        cost_estimate=pl.CostEstimate(
+            flops=2 * count * rows * depth * columns,
+            bytes_accessed=streamed_bytes,
+            transcendentals=0,
+        ),
+        compiler_params=pltpu.CompilerParams(vmem_limit_bytes=44 * MIB),
+        name="product",
+    )(me, *pinned, pltpu.with_memory_space_constraint(resident, pltpu.VMEM), *weights)
+
+
+def attend(query_all, pairs_all, key_cache, value_cache, lengths):
     requests = query_all.shape[0]
     per_group = HEADS // KV_HEADS
     scaling = 1.0 / math.sqrt(HEAD_DIM)
@@ -85,13 +246,44 @@
         mixed
         + own_prob.astype(jnp.float32)[..., None] * fresh_value.astype(jnp.float32)[:, :, None, :]
     )
-    attended = mixed.reshape(requests, HEADS * HEAD_DIM).astype(jnp.bfloat16)
-    result = jnp.dot(
-        lax.all_gather(attended, "mp", axis=0, tiled=True),
-        o_weight,
-        preferred_element_type=jnp.float32,
-    )
-    return result.astype(jnp.bfloat16)
+    return mixed.reshape(requests, HEADS * HEAD_DIM).astype(jnp.bfloat16)
+
+
+def shards(activations, gain, q_weight, kv_weight, o_weight, key_cache, value_cache, lengths):
+    size = lax.axis_size("mp")
+    normed = normalize(activations, gain)
+    query_cols = q_weight.shape[1]
+    by_swaps = size in (4, 8, 16)
+    me = lax.axis_index("mp").astype(jnp.int32).reshape(1)
+    if by_swaps:
+        held = q_weight.shape[0] * 3 // 8 // STEP * STEP
+        projected = product(
+            me, gather_blocks(normed, size), load(q_weight, held), [q_weight, kv_weight], False
+        )
+    else:
+        piece = lax.all_gather(normed, "mp", axis=0, tiled=True)
+        projected = jnp.concatenate(
+            [
+                jnp.dot(piece, q_weight, preferred_element_type=jnp.float32),
+                jnp.dot(piece, kv_weight, preferred_element_type=jnp.float32),
+            ],
+            axis=1,
+        ).astype(jnp.bfloat16).reshape(size, normed.shape[0], -1)
+    arrived = lax.all_to_all(projected, "mp", split_axis=0, concat_axis=0, tiled=True)
+    arrived = arrived.transpose(1, 0, 2)
+    requests = arrived.shape[0]
+    attended = attend(
+        arrived[..., :query_cols].reshape(requests, -1),
+        arrived[..., query_cols:].reshape(requests, -1),
+        key_cache,
+        value_cache,
+        lengths,
+    )
+    if by_swaps:
+        held = o_weight.shape[0] * 3 // 8 // STEP * STEP
+        return product(me, gather_blocks(attended, size), load(o_weight, held), [o_weight], True)
+    everyone = lax.all_gather(attended, "mp", axis=0, tiled=True)
+    return jnp.dot(everyone, o_weight, preferred_element_type=jnp.float32).astype(jnp.bfloat16)
 
 
 def solution(mesh):

time: 162 us -> 91.5 us (0.56)
  waiting for transfers between devices: 89.7 us -> 27.9 us
  matrix products: 36.2 us -> 4.85 us
  Pallas kernels: 0 us -> 29.5 us
  starting transfers between devices: 9.53 us -> 27.4 us
  between operations: 13.5 us -> 0.4 us
  local copies, waits for them, and re-layouts: 6.73 us -> 0.34 us
  other arithmetic: 5.85 us -> 0.91 us
    all_gather x2 -> x0, waiting for transfers between devices: 81.9 us -> none  [the longest x1 42.7 us: shards(): piece = lax.all_gather(normed, 'mp', axis=0, tiled=True)]
    dot_general x6 -> x3, matrix products: 36.2 us -> 4.85 us  [the longest x1 3.81 us: attend(): jnp.einsum('rgqd,rgtd->rgqt', query, key_cache, preferred_element_type=jn...]
    pallas_call x0 -> x5, Pallas kernels: none -> 29.5 us  [the longest x2 18.9 us: product(): pl.pallas_call(functools.partial(product_kernel, count, len(weights), ord...]
    ppermute x0 -> x30, starting transfers between devices: none -> 21 us  [swap(): return lax.ppermute(block, 'mp', [(i, i ^ distance) for i in range(size)])]
    ppermute x0 -> x30, waiting for transfers between devices: none -> 19.8 us  [swap(): return lax.ppermute(block, 'mp', [(i, i ^ distance) for i in range(size)])]
    unnamed x5, local copies, waits for them, and re-layouts: 5.81 us -> 0.12 us
    all_to_all x2 -> x1, starting transfers between devices: 9.48 us -> 6.39 us  [shards(): lax.all_to_all(projected, 'mp', split_axis=0, concat_axis=0, tiled=True)]
    unnamed x2 -> x1, other arithmetic: 1.71 us -> 0.01 us
  transfers between devices with their start and end apart: 4 -> 31, of which waited for: 3 -> 11; matrix products, arithmetic and copies ran while one was open for 9% -> 0% of each run, Pallas kernels for 0% -> 10%
where the time goes in v2:
time: 91.5 us; the launch traced here: 91.2 us
  Pallas kernels  29.5 us (32%)
  waiting for transfers between devices  27.9 us (30%)
  starting transfers between devices  27.4 us (30%)
  matrix products  4.85 us (5%)
    ppermute x30, starting transfers between devices, swap(): return lax.ppermute(block, 'mp', [(i, i ^ distance) for i in range(size)])  21 us
    ppermute x30, waiting for transfers between devices, swap(): return lax.ppermute(block, 'mp', [(i, i ^ distance) for i in range(size)])  19.8 us
    pallas_call x2, Pallas kernels, product(): pl.pallas_call(functools.partial(product_kernel, count, len(weights), ord...  18.9 us
    pallas_call x2, Pallas kernels, load(): pl.pallas_call(functools.partial(load_kernel, parts), out_shape=pltpu.VME...  9.38 us
    all_to_all x1, waiting for transfers between devices, shards(): lax.all_to_all(projected, 'mp', split_axis=0, concat_axis=0, tiled=True)  8.06 us
    all_to_all x1, starting transfers between devices, shards(): lax.all_to_all(projected, 'mp', split_axis=0, concat_axis=0, tiled=True)  6.39 us
    dot_general x1, matrix products, attend(): jnp.einsum('rgqd,rgtd->rgqt', query, key_cache, preferred_element_type=jn...  3.81 us
  transfers between devices with their start and end apart: 31, of which 11 were waited for; matrix products, arithmetic and copies ran while one was open for 0% of the time, Pallas kernels for 10%

profile of v2, /device:TPU:0, one launch (start us, length us, event | category | flops | bytes accessed | tf_op | source)
XLA Modules:
  0.0 91.2 jit_solution(18330730031895467015)
XLA Ops:
  0.0 1.2 %norm.1.refs_1_ = bf16[4,16384]{1,0:T(4,128)(2,1)S(1)} custom-call(bf16[4,16384]{1,0:T(4,128)(2,1)} %x_hbm.1, bf16[128,128]{1,0:T(8,128)(2,1)} %bitcast.35), custom_call_target="tpu_custom_call" | custom-call | tf_op jit(solution)/shard_map/norm/pallas_call | solution.py:63
  1.2 4.1 %collective-permute-start.7 = (bf16[4,16384]{1,0:T(4,128)(2,1)S(1)}, bf16[4,16384]{1,0:T(4,128)(2,1)S(1)}, u32[]{:S(2)}, u32[]{:S(2)}) collective-permute-start(bf16[4,16384]{1,0:T(4,128)(2,1)S(1)} %norm.1.refs_1_), channel_id=1, source_target_pairs={{0,8},{1,9},{2,10},{3,11},{4,12},{5,13},{6,14},{7,15},{8,0},{9,1},... | collective-permute-start | bytes 393224 | tf_op jit(solution)/shard_map/ppermute | solution.py:79
  5.3 1.3 %collective-permute-start.11 = (bf16[4,16384]{1,0:T(4,128)(2,1)S(1)}, bf16[4,16384]{1,0:T(4,128)(2,1)S(1)}, u32[]{:S(2)}, u32[]{:S(2)}) collective-permute-start(bf16[4,16384]{1,0:T(4,128)(2,1)S(1)} %norm.1.refs_1_), channel_id=1, source_target_pairs={{0,12},{1,13},{2,14},{3,15},{4,8},{5,9},{6,10},{7,11},{8,4},{9,5},... | collective-permute-start | bytes 393224 | tf_op jit(solution)/shard_map/ppermute | solution.py:79
  6.7 0.2 collective-permute-start.3
  6.9 1.5 %collective-permute-start.1 = (bf16[4,16384]{1,0:T(4,128)(2,1)S(1)}, bf16[4,16384]{1,0:T(4,128)(2,1)S(1)}, u32[]{:S(2)}, u32[]{:S(2)}) collective-permute-start(bf16[4,16384]{1,0:T(4,128)(2,1)S(1)} %norm.1.refs_1_), channel_id=1, source_target_pairs={{0,2},{1,3},{2,0},{3,1},{4,6},{5,7},{6,4},{7,5},{8,10},{9,11},{10,... | collective-permute-start | bytes 393224 | tf_op jit(solution)/shard_map/ppermute | solution.py:79
  8.4 6.9 %collective-permute-done.7.refs_9_ = bf16[4,16384]{1,0:T(4,128)(2,1)S(1)} collective-permute-done((bf16[4,16384]{1,0:T(4,128)(2,1)S(1)}, bf16[4,16384]{1,0:T(4,128)(2,1)S(1)}, u32[]{:S(2)}, u32[]{:S(2)}) %collective-permute-start.7) | collective-permute-done | bytes 131104 | tf_op jit(solution)/shard_map/ppermute | solution.py:79
  15.3 1.9 %collective-permute-start.9 = (bf16[4,16384]{1,0:T(4,128)(2,1)S(1)}, bf16[4,16384]{1,0:T(4,128)(2,1)S(1)}, u32[]{:S(2)}, u32[]{:S(2)}) collective-permute-start(bf16[4,16384]{1,0:T(4,128)(2,1)S(1)} %collective-permute-done.7.refs_9_), channel_id=1, source_target_pairs={{0,2},{1,3},{2,0},{3,1},{4,6},{5,7},{6,4},{7,5},{8,10},{9,11},{10,... | collective-permute-start | bytes 393224 | tf_op jit(solution)/shard_map/ppermute | solution.py:79
  17.2 0.0 collective-permute-done.11.refs_13_
  17.2 0.2 collective-permute-start.13
  17.3 1.9 %collective-permute-start.5 = (bf16[4,16384]{1,0:T(4,128)(2,1)S(1)}, bf16[4,16384]{1,0:T(4,128)(2,1)S(1)}, u32[]{:S(2)}, u32[]{:S(2)}) collective-permute-start(bf16[4,16384]{1,0:T(4,128)(2,1)S(1)} %collective-permute-done.3.refs_5_), channel_id=1, source_target_pairs={{0,2},{1,3},{2,0},{3,1},{4,6},{5,7},{6,4},{7,5},{8,10},{9,11},{10,... | collective-permute-start | bytes 393224 | tf_op jit(solution)/shard_map/ppermute | solution.py:79
  19.2 0.0 collective-permute-start.12
  19.2 0.0 collective-permute-done.refs_2_
  19.2 0.5 collective-permute-start.4
  19.7 4.7 %load.2.refs_17_ = bf16[6144,1024]{1,0:T(8,128)(2,1)S(1)} custom-call(bf16[16384,1024]{1,0:T(8,128)(2,1)} %refs_18_.2), custom_call_target="tpu_custom_call" | custom-call | bytes 12582912 | tf_op jit(solution)/shard_map/load/pallas_call | solution.py:112
  24.4 0.0 collective-permute-done.9.refs_11_
  24.4 0.1 collective-permute-start.8
  24.6 0.0 collective-permute-done.13.refs_15_
  24.6 0.4 collective-permute-start.2
  25.0 0.1 collective-permute-start.10
  25.1 0.0 collective-permute-done.12.refs_14_
  25.1 0.4 collective-permute-start.14
  25.5 0.1 collective-permute-start.6
  25.6 0.1 iota_compare_fusion
  25.7 0.1 collective-permute-done.8.refs_10_
  25.9 0.2 collective-permute-done.2.refs_4_
  26.0 0.3 collective-permute-done.10.refs_12_
  26.4 0.2 collective-permute-done.14.refs_16_
  26.6 0.3 collective-permute-done.6.refs_8_
  26.9 10.1 %product.2 = bf16[16,4,1152]{2,1,0:T(4,128)(2,1)} custom-call(s32[1]{0:T(128)} %bitcast.refs_0_, bf16[4,16384]{1,0:T(4,128)(2,1)S(1)} %norm.1.refs_1_, bf16[4,16384]{1,0:T(4,128)(2,1)S(1)} %collective-permute-done.refs_2_, bf16[4,16384]{1,0:T(4,128)(2,1)S(1)} %collective-permute-done.1.refs_3_, bf16[4,16384]{1,0:T(4,128)(2,1)S(1)} %collective-permute-done.2.refs_4_, ...), custom_call_target="tpu_custom_call" | custom-call | flops 2415919104 | bytes 25165824 | tf_op jit(solution)/shard_map/product/pallas_call | solution.py:193
  37.0 6.4 %all-to-all-start = ((bf16[16,4,1152]{2,1,0:T(4,128)(2,1)}), bf16[16,4,1152]{2,1,0:T(4,128)(2,1)S(1)}, u32[]{:S(2)}, u32[]{:S(2)}) async-start(bf16[16,4,1152]{2,1,0:T(4,128)(2,1)} %product.2), calls=%async_computation | async-start | bytes 294912 | tf_op jit(solution)/shard_map/all_to_all | solution.py:272
  43.4 0.1 multiply_cosine_fusion
  43.5 8.1 %all-to-all-done = bf16[16,4,1152]{2,1,0:T(4,128)(2,1)S(1)} async-done(((bf16[16,4,1152]{2,1,0:T(4,128)(2,1)}), bf16[16,4,1152]{2,1,0:T(4,128)(2,1)S(1)}, u32[]{:S(2)}, u32[]{:S(2)}) %all-to-all-start) | async-done | bytes 147488 | tf_op jit(solution)/shard_map/all_to_all | solution.py:272
  51.6 0.2 copy.10
  51.8 0.0 copy-start.1
  51.9 0.1 subtract_convert_fusion.1
  51.9 0.1 subtract_convert_fusion
  52.1 0.1 maximum_bitcast_fusion
  52.2 0.2 fusion.7
  52.4 3.8 %fusion.14 = (f32[4,8,16]{2,1,0:T(8,128)S(1)}, f32[4,8,16,512]{3,2,1,0:T(8,128)S(1)}) fusion(bf16[4,8,512,128]{3,2,1,0:T(8,128)(2,1)} %param.13, bf16[4,8,16,64]{3,2,1,0:T(8,128)(2,1)S(1)} %get-tuple-element.6, bf16[4,8,16,64]{3,2,1,0:T(8,128)(2,1)S(1)} %get-tuple-element.5, pred[4,512]{1,0:T(4,128)(4,1)S(1)} %iota_compare_fusion), kind=kOutput, calls=%fused_computation.38 | convolution fusion | flops 68156928 | bytes 5378048 | tf_op jit(solution)/shard_map/rgqd,rgtd->rgqt/dot_general | solution.py:230
  56.2 0.4 fusion.2
  56.6 0.8 fusion.1
  57.4 0.1 copy.21
  57.6 0.1 collective-permute-start.18
  57.6 1.3 %collective-permute-start.22 = (bf16[4,16384]{1,0:T(4,128)(2,1)S(1)}, bf16[4,16384]{1,0:T(4,128)(2,1)S(1)}, u32[]{:S(2)}, u32[]{:S(2)}) collective-permute-start(bf16[4,16384]{1,0:T(4,128)(2,1)S(1)} %bitcast.25), channel_id=1, source_target_pairs={{0,8},{1,9},{2,10},{3,11},{4,12},{5,13},{6,14},{7,15},{8,0},{9,1},... | collective-permute-start | bytes 393224 | tf_op jit(solution)/shard_map/ppermute | solution.py:79
  58.9 3.1 %collective-permute-start.26 = (bf16[4,16384]{1,0:T(4,128)(2,1)S(1)}, bf16[4,16384]{1,0:T(4,128)(2,1)S(1)}, u32[]{:S(2)}, u32[]{:S(2)}) collective-permute-start(bf16[4,16384]{1,0:T(4,128)(2,1)S(1)} %bitcast.26), channel_id=1, source_target_pairs={{0,12},{1,13},{2,14},{3,15},{4,8},{5,9},{6,10},{7,11},{8,4},{9,5},... | collective-permute-start | bytes 393224 | tf_op jit(solution)/shard_map/ppermute | solution.py:79
  62.0 0.0 collective-permute-start.16
  62.0 2.2 %collective-permute-done.18.refs_5_ = bf16[4,16384]{1,0:T(4,128)(2,1)S(1)} collective-permute-done((bf16[4,16384]{1,0:T(4,128)(2,1)S(1)}, bf16[4,16384]{1,0:T(4,128)(2,1)S(1)}, u32[]{:S(2)}, u32[]{:S(2)}) %collective-permute-start.18) | collective-permute-done | bytes 131104 | tf_op jit(solution)/shard_map/ppermute | solution.py:79
  64.3 0.6 collective-permute-start.20
  64.8 5.7 %collective-permute-done.22.refs_9_ = bf16[4,16384]{1,0:T(4,128)(2,1)S(1)} collective-permute-done((bf16[4,16384]{1,0:T(4,128)(2,1)S(1)}, bf16[4,16384]{1,0:T(4,128)(2,1)S(1)}, u32[]{:S(2)}, u32[]{:S(2)}) %collective-permute-start.22) | collective-permute-done | bytes 131104 | tf_op jit(solution)/shard_map/ppermute | solution.py:79
  70.5 0.2 collective-permute-start.24
  70.8 0.0 collective-permute-done.26.refs_13_
  70.8 1.8 %collective-permute-start.28 = (bf16[4,16384]{1,0:T(4,128)(2,1)S(1)}, bf16[4,16384]{1,0:T(4,128)(2,1)S(1)}, u32[]{:S(2)}, u32[]{:S(2)}) collective-permute-start(bf16[4,16384]{1,0:T(4,128)(2,1)S(1)} %collective-permute-done.26.refs_13_), channel_id=1, source_target_pairs={{0,2},{1,3},{2,0},{3,1},{4,6},{5,7},{6,4},{7,5},{8,10},{9,11},{10,... | collective-permute-start | bytes 393224 | tf_op jit(solution)/shard_map/ppermute | solution.py:79
  72.6 0.0 collective-permute-start.17
  72.6 0.0 collective-permute-done.15.refs_2_
  72.6 0.5 collective-permute-start.19
  73.1 0.1 collective-permute-start.23
  73.2 2.3 %collective-permute-done.24.refs_11_ = bf16[4,16384]{1,0:T(4,128)(2,1)S(1)} collective-permute-done((bf16[4,16384]{1,0:T(4,128)(2,1)S(1)}, bf16[4,16384]{1,0:T(4,128)(2,1)S(1)}, u32[]{:S(2)}, u32[]{:S(2)}) %collective-permute-start.24) | collective-permute-done | bytes 131104 | tf_op jit(solution)/shard_map/ppermute | solution.py:79
  75.5 0.0 collective-permute-start.27
  75.5 1.4 %collective-permute-done.28.refs_15_ = bf16[4,16384]{1,0:T(4,128)(2,1)S(1)} collective-permute-done((bf16[4,16384]{1,0:T(4,128)(2,1)S(1)}, bf16[4,16384]{1,0:T(4,128)(2,1)S(1)}, u32[]{:S(2)}, u32[]{:S(2)}) %collective-permute-start.28) | collective-permute-done | bytes 131104 | tf_op jit(solution)/shard_map/ppermute | solution.py:79
  76.9 0.5 collective-permute-start.25
  77.4 0.1 collective-permute-start.29
  77.5 4.7 %load.3.refs_17_ = bf16[6144,1024]{1,0:T(8,128)(2,1)S(1)} custom-call(bf16[16384,1024]{1,0:T(8,128)(2,1)} %refs_18_.3), custom_call_target="tpu_custom_call" | custom-call | bytes 12582912 | tf_op jit(solution)/shard_map/load/pallas_call | solution.py:112
  82.2 0.0 collective-permute-done.23.refs_10_
  82.2 8.8 %product.3 = bf16[64,1024]{1,0:T(8,128)(2,1)} custom-call(s32[1]{0:T(128)} %bitcast.refs_0_, bf16[4,16384]{1,0:T(4,128)(2,1)S(1)} %bitcast.29, bf16[4,16384]{1,0:T(4,128)(2,1)S(1)} %collective-permute-done.15.refs_2_, bf16[4,16384]{1,0:T(4,128)(2,1)S(1)} %collective-permute-done.16.refs_3_, bf16[4,16384]{1,0:T(4,128)(2,1)S(1)} %collective-permute-done.17.refs_4_, ...), custom_call_target="tpu_custom_call" | custom-call | flops 2147483648 | bytes 20971520 | tf_op jit(solution)/shard_map/product/pallas_call | solution.py:193
  (27 shorter events, 0.2 us)
Async XLA Ops:
  1.2 14.1 %collective-permute-start.7 = (bf16[4,16384]{1,0:T(4,128)(2,1)S(1)}, bf16[4,16384]{1,0:T(4,128)(2,1)S(1)}, u32[]{:S(2)}, u32[]{:S(2)}) collective-permute-start(bf16[4,16384]{1,0:T(4,128)(2,1)S(1)} %norm.1.refs_1_), channel_id=1, source_target_pairs={{0,8},{1,9},{2,10},{3,11},{4,12},{5,13},{6,14},{7,15},{8,0},{9,1},... | collective-permute-start | bytes 393224 | tf_op jit(solution)/shard_map/ppermute | solution.py:79
  5.3 11.9 %collective-permute-start.11 = (bf16[4,16384]{1,0:T(4,128)(2,1)S(1)}, bf16[4,16384]{1,0:T(4,128)(2,1)S(1)}, u32[]{:S(2)}, u32[]{:S(2)}) collective-permute-start(bf16[4,16384]{1,0:T(4,128)(2,1)S(1)} %norm.1.refs_1_), channel_id=1, source_target_pairs={{0,12},{1,13},{2,14},{3,15},{4,8},{5,9},{6,10},{7,11},{8,4},{9,5},... | collective-permute-start | bytes 393224 | tf_op jit(solution)/shard_map/ppermute | solution.py:79
  6.7 10.7 %collective-permute-start.3 = (bf16[4,16384]{1,0:T(4,128)(2,1)S(1)}, bf16[4,16384]{1,0:T(4,128)(2,1)S(1)}, u32[]{:S(2)}, u32[]{:S(2)}) collective-permute-start(bf16[4,16384]{1,0:T(4,128)(2,1)S(1)} %norm.1.refs_1_), channel_id=1, source_target_pairs={{0,4},{1,5},{2,6},{3,7},{4,0},{5,1},{6,2},{7,3},{8,12},{9,13},{10,... | collective-permute-start | bytes 393224 | tf_op jit(solution)/shard_map/ppermute | solution.py:79
  6.9 12.3 %collective-permute-start.1 = (bf16[4,16384]{1,0:T(4,128)(2,1)S(1)}, bf16[4,16384]{1,0:T(4,128)(2,1)S(1)}, u32[]{:S(2)}, u32[]{:S(2)}) collective-permute-start(bf16[4,16384]{1,0:T(4,128)(2,1)S(1)} %norm.1.refs_1_), channel_id=1, source_target_pairs={{0,2},{1,3},{2,0},{3,1},{4,6},{5,7},{6,4},{7,5},{8,10},{9,11},{10,... | collective-permute-start | bytes 393224 | tf_op jit(solution)/shard_map/ppermute | solution.py:79
  8.4 10.8 %collective-permute-start = (bf16[4,16384]{1,0:T(4,128)(2,1)S(1)}, bf16[4,16384]{1,0:T(4,128)(2,1)S(1)}, u32[]{:S(2)}, u32[]{:S(2)}) collective-permute-start(bf16[4,16384]{1,0:T(4,128)(2,1)S(1)} %norm.1.refs_1_), channel_id=1, source_target_pairs={{0,1},{1,0},{2,3},{3,2},{4,5},{5,4},{6,7},{7,6},{8,9},{9,8},{10,11... | collective-permute-start | bytes 393224 | tf_op jit(solution)/shard_map/ppermute | solution.py:79
  15.3 9.1 %collective-permute-start.9 = (bf16[4,16384]{1,0:T(4,128)(2,1)S(1)}, bf16[4,16384]{1,0:T(4,128)(2,1)S(1)}, u32[]{:S(2)}, u32[]{:S(2)}) collective-permute-start(bf16[4,16384]{1,0:T(4,128)(2,1)S(1)} %collective-permute-done.7.refs_9_), channel_id=1, source_target_pairs={{0,2},{1,3},{2,0},{3,1},{4,6},{5,7},{6,4},{7,5},{8,10},{9,11},{10,... | collective-permute-start | bytes 393224 | tf_op jit(solution)/shard_map/ppermute | solution.py:79
  17.2 7.4 %collective-permute-start.13 = (bf16[4,16384]{1,0:T(4,128)(2,1)S(1)}, bf16[4,16384]{1,0:T(4,128)(2,1)S(1)}, u32[]{:S(2)}, u32[]{:S(2)}) collective-permute-start(bf16[4,16384]{1,0:T(4,128)(2,1)S(1)} %collective-permute-done.11.refs_13_), channel_id=1, source_target_pairs={{0,2},{1,3},{2,0},{3,1},{4,6},{5,7},{6,4},{7,5},{8,10},{9,11},{10,... | collective-permute-start | bytes 393224 | tf_op jit(solution)/shard_map/ppermute | solution.py:79
  17.3 7.7 %collective-permute-start.5 = (bf16[4,16384]{1,0:T(4,128)(2,1)S(1)}, bf16[4,16384]{1,0:T(4,128)(2,1)S(1)}, u32[]{:S(2)}, u32[]{:S(2)}) collective-permute-start(bf16[4,16384]{1,0:T(4,128)(2,1)S(1)} %collective-permute-done.3.refs_5_), channel_id=1, source_target_pairs={{0,2},{1,3},{2,0},{3,1},{4,6},{5,7},{6,4},{7,5},{8,10},{9,11},{10,... | collective-permute-start | bytes 393224 | tf_op jit(solution)/shard_map/ppermute | solution.py:79
  19.2 5.9 %collective-permute-start.12 = (bf16[4,16384]{1,0:T(4,128)(2,1)S(1)}, bf16[4,16384]{1,0:T(4,128)(2,1)S(1)}, u32[]{:S(2)}, u32[]{:S(2)}) collective-permute-start(bf16[4,16384]{1,0:T(4,128)(2,1)S(1)} %collective-permute-done.11.refs_13_), channel_id=1, source_target_pairs={{0,1},{1,0},{2,3},{3,2},{4,5},{5,4},{6,7},{7,6},{8,9},{9,8},{10,11... | collective-permute-start | bytes 393224 | tf_op jit(solution)/shard_map/ppermute | solution.py:79
  19.2 6.3 %collective-permute-start.4 = (bf16[4,16384]{1,0:T(4,128)(2,1)S(1)}, bf16[4,16384]{1,0:T(4,128)(2,1)S(1)}, u32[]{:S(2)}, u32[]{:S(2)}) collective-permute-start(bf16[4,16384]{1,0:T(4,128)(2,1)S(1)} %collective-permute-done.3.refs_5_), channel_id=1, source_target_pairs={{0,1},{1,0},{2,3},{3,2},{4,5},{5,4},{6,7},{7,6},{8,9},{9,8},{10,11... | collective-permute-start | bytes 393224 | tf_op jit(solution)/shard_map/ppermute | solution.py:79
  19.7 5.9 %copy-start = (s32[4]{0:T(128)S(1)}, s32[4]{0:T(128)}, u32[]{:S(2)}) copy-start(s32[4]{0:T(128)} %param.15) | copy-start | bytes 52
  24.4 1.4 %collective-permute-start.8 = (bf16[4,16384]{1,0:T(4,128)(2,1)S(1)}, bf16[4,16384]{1,0:T(4,128)(2,1)S(1)}, u32[]{:S(2)}, u32[]{:S(2)}) collective-permute-start(bf16[4,16384]{1,0:T(4,128)(2,1)S(1)} %collective-permute-done.7.refs_9_), channel_id=1, source_target_pairs={{0,1},{1,0},{2,3},{3,2},{4,5},{5,4},{6,7},{7,6},{8,9},{9,8},{10,11... | collective-permute-start | bytes 393224 | tf_op jit(solution)/shard_map/ppermute | solution.py:79
  24.6 1.5 %collective-permute-start.2 = (bf16[4,16384]{1,0:T(4,128)(2,1)S(1)}, bf16[4,16384]{1,0:T(4,128)(2,1)S(1)}, u32[]{:S(2)}, u32[]{:S(2)}) collective-permute-start(bf16[4,16384]{1,0:T(4,128)(2,1)S(1)} %collective-permute-done.1.refs_3_), channel_id=1, source_target_pairs={{0,1},{1,0},{2,3},{3,2},{4,5},{5,4},{6,7},{7,6},{8,9},{9,8},{10,11... | collective-permute-start | bytes 393224 | tf_op jit(solution)/shard_map/ppermute | solution.py:79
  25.0 1.3 %collective-permute-start.10 = (bf16[4,16384]{1,0:T(4,128)(2,1)S(1)}, bf16[4,16384]{1,0:T(4,128)(2,1)S(1)}, u32[]{:S(2)}, u32[]{:S(2)}) collective-permute-start(bf16[4,16384]{1,0:T(4,128)(2,1)S(1)} %collective-permute-done.9.refs_11_), channel_id=1, source_target_pairs={{0,1},{1,0},{2,3},{3,2},{4,5},{5,4},{6,7},{7,6},{8,9},{9,8},{10,11... | collective-permute-start | bytes 393224 | tf_op jit(solution)/shard_map/ppermute | solution.py:79
  25.1 1.4 %collective-permute-start.14 = (bf16[4,16384]{1,0:T(4,128)(2,1)S(1)}, bf16[4,16384]{1,0:T(4,128)(2,1)S(1)}, u32[]{:S(2)}, u32[]{:S(2)}) collective-permute-start(bf16[4,16384]{1,0:T(4,128)(2,1)S(1)} %collective-permute-done.13.refs_15_), channel_id=1, source_target_pairs={{0,1},{1,0},{2,3},{3,2},{4,5},{5,4},{6,7},{7,6},{8,9},{9,8},{10,11... | collective-permute-start | bytes 393224 | tf_op jit(solution)/shard_map/ppermute | solution.py:79
  25.5 1.3 %collective-permute-start.6 = (bf16[4,16384]{1,0:T(4,128)(2,1)S(1)}, bf16[4,16384]{1,0:T(4,128)(2,1)S(1)}, u32[]{:S(2)}, u32[]{:S(2)}) collective-permute-start(bf16[4,16384]{1,0:T(4,128)(2,1)S(1)} %collective-permute-done.5.refs_7_), channel_id=1, source_target_pairs={{0,1},{1,0},{2,3},{3,2},{4,5},{5,4},{6,7},{7,6},{8,9},{9,8},{10,11... | collective-permute-start | bytes 393224 | tf_op jit(solution)/shard_map/ppermute | solution.py:79
  37.0 14.6 %all-to-all-start = ((bf16[16,4,1152]{2,1,0:T(4,128)(2,1)}), bf16[16,4,1152]{2,1,0:T(4,128)(2,1)S(1)}, u32[]{:S(2)}, u32[]{:S(2)}) async-start(bf16[16,4,1152]{2,1,0:T(4,128)(2,1)} %product.2), calls=%async_computation | async-start | bytes 294912 | tf_op jit(solution)/shard_map/all_to_all | solution.py:272
  51.8 4.8 %copy-start.1 = (bf16[4,8,512,128]{3,2,1,0:T(8,128)(2,1)S(1)}, bf16[4,8,512,128]{3,2,1,0:T(8,128)(2,1)}, u32[]{:S(2)}) copy-start(bf16[4,8,512,128]{3,2,1,0:T(8,128)(2,1)} %param.14) | copy-start | bytes 12582916
  57.6 6.7 %collective-permute-start.18 = (bf16[4,16384]{1,0:T(4,128)(2,1)S(1)}, bf16[4,16384]{1,0:T(4,128)(2,1)S(1)}, u32[]{:S(2)}, u32[]{:S(2)}) collective-permute-start(bf16[4,16384]{1,0:T(4,128)(2,1)S(1)} %bitcast.24), channel_id=1, source_target_pairs={{0,4},{1,5},{2,6},{3,7},{4,0},{5,1},{6,2},{7,3},{8,12},{9,13},{10,... | collective-permute-start | bytes 393224 | tf_op jit(solution)/shard_map/ppermute | solution.py:79
  57.6 12.9 %collective-permute-start.22 = (bf16[4,16384]{1,0:T(4,128)(2,1)S(1)}, bf16[4,16384]{1,0:T(4,128)(2,1)S(1)}, u32[]{:S(2)}, u32[]{:S(2)}) collective-permute-start(bf16[4,16384]{1,0:T(4,128)(2,1)S(1)} %bitcast.25), channel_id=1, source_target_pairs={{0,8},{1,9},{2,10},{3,11},{4,12},{5,13},{6,14},{7,15},{8,0},{9,1},... | collective-permute-start | bytes 393224 | tf_op jit(solution)/shard_map/ppermute | solution.py:79
  58.9 11.8 %collective-permute-start.26 = (bf16[4,16384]{1,0:T(4,128)(2,1)S(1)}, bf16[4,16384]{1,0:T(4,128)(2,1)S(1)}, u32[]{:S(2)}, u32[]{:S(2)}) collective-permute-start(bf16[4,16384]{1,0:T(4,128)(2,1)S(1)} %bitcast.26), channel_id=1, source_target_pairs={{0,12},{1,13},{2,14},{3,15},{4,8},{5,9},{6,10},{7,11},{8,4},{9,5},... | collective-permute-start | bytes 393224 | tf_op jit(solution)/shard_map/ppermute | solution.py:79
  62.0 10.6 %collective-permute-start.16 = (bf16[4,16384]{1,0:T(4,128)(2,1)S(1)}, bf16[4,16384]{1,0:T(4,128)(2,1)S(1)}, u32[]{:S(2)}, u32[]{:S(2)}) collective-permute-start(bf16[4,16384]{1,0:T(4,128)(2,1)S(1)} %bitcast.27), channel_id=1, source_target_pairs={{0,2},{1,3},{2,0},{3,1},{4,6},{5,7},{6,4},{7,5},{8,10},{9,11},{10,... | collective-permute-start | bytes 393224 | tf_op jit(solution)/shard_map/ppermute | solution.py:79
  62.0 10.6 %collective-permute-start.15 = (bf16[4,16384]{1,0:T(4,128)(2,1)S(1)}, bf16[4,16384]{1,0:T(4,128)(2,1)S(1)}, u32[]{:S(2)}, u32[]{:S(2)}) collective-permute-start(bf16[4,16384]{1,0:T(4,128)(2,1)S(1)} %bitcast.28), channel_id=1, source_target_pairs={{0,1},{1,0},{2,3},{3,2},{4,5},{5,4},{6,7},{7,6},{8,9},{9,8},{10,11... | collective-permute-start | bytes 393224 | tf_op jit(solution)/shard_map/ppermute | solution.py:79
  64.3 8.8 %collective-permute-start.20 = (bf16[4,16384]{1,0:T(4,128)(2,1)S(1)}, bf16[4,16384]{1,0:T(4,128)(2,1)S(1)}, u32[]{:S(2)}, u32[]{:S(2)}) collective-permute-start(bf16[4,16384]{1,0:T(4,128)(2,1)S(1)} %collective-permute-done.18.refs_5_), channel_id=1, source_target_pairs={{0,2},{1,3},{2,0},{3,1},{4,6},{5,7},{6,4},{7,5},{8,10},{9,11},{10,... | collective-permute-start | bytes 393224 | tf_op jit(solution)/shard_map/ppermute | solution.py:79
  70.5 5.0 %collective-permute-start.24 = (bf16[4,16384]{1,0:T(4,128)(2,1)S(1)}, bf16[4,16384]{1,0:T(4,128)(2,1)S(1)}, u32[]{:S(2)}, u32[]{:S(2)}) collective-permute-start(bf16[4,16384]{1,0:T(4,128)(2,1)S(1)} %collective-permute-done.22.refs_9_), channel_id=1, source_target_pairs={{0,2},{1,3},{2,0},{3,1},{4,6},{5,7},{6,4},{7,5},{8,10},{9,11},{10,... | collective-permute-start | bytes 393224 | tf_op jit(solution)/shard_map/ppermute | solution.py:79
  70.8 6.1 %collective-permute-start.28 = (bf16[4,16384]{1,0:T(4,128)(2,1)S(1)}, bf16[4,16384]{1,0:T(4,128)(2,1)S(1)}, u32[]{:S(2)}, u32[]{:S(2)}) collective-permute-start(bf16[4,16384]{1,0:T(4,128)(2,1)S(1)} %collective-permute-done.26.refs_13_), channel_id=1, source_target_pairs={{0,2},{1,3},{2,0},{3,1},{4,6},{5,7},{6,4},{7,5},{8,10},{9,11},{10,... | collective-permute-start | bytes 393224 | tf_op jit(solution)/shard_map/ppermute | solution.py:79
  72.6 4.3 %collective-permute-start.17 = (bf16[4,16384]{1,0:T(4,128)(2,1)S(1)}, bf16[4,16384]{1,0:T(4,128)(2,1)S(1)}, u32[]{:S(2)}, u32[]{:S(2)}) collective-permute-start(bf16[4,16384]{1,0:T(4,128)(2,1)S(1)} %collective-permute-done.16.refs_3_), channel_id=1, source_target_pairs={{0,1},{1,0},{2,3},{3,2},{4,5},{5,4},{6,7},{7,6},{8,9},{9,8},{10,11... | collective-permute-start | bytes 393224 | tf_op jit(solution)/shard_map/ppermute | solution.py:79
  72.6 4.8 %collective-permute-start.19 = (bf16[4,16384]{1,0:T(4,128)(2,1)S(1)}, bf16[4,16384]{1,0:T(4,128)(2,1)S(1)}, u32[]{:S(2)}, u32[]{:S(2)}) collective-permute-start(bf16[4,16384]{1,0:T(4,128)(2,1)S(1)} %collective-permute-done.18.refs_5_), channel_id=1, source_target_pairs={{0,1},{1,0},{2,3},{3,2},{4,5},{5,4},{6,7},{7,6},{8,9},{9,8},{10,11... | collective-permute-start | bytes 393224 | tf_op jit(solution)/shard_map/ppermute | solution.py:79
  73.1 9.1 %collective-permute-start.23 = (bf16[4,16384]{1,0:T(4,128)(2,1)S(1)}, bf16[4,16384]{1,0:T(4,128)(2,1)S(1)}, u32[]{:S(2)}, u32[]{:S(2)}) collective-permute-start(bf16[4,16384]{1,0:T(4,128)(2,1)S(1)} %collective-permute-done.22.refs_9_), channel_id=1, source_target_pairs={{0,1},{1,0},{2,3},{3,2},{4,5},{5,4},{6,7},{7,6},{8,9},{9,8},{10,11... | collective-permute-start | bytes 393224 | tf_op jit(solution)/shard_map/ppermute | solution.py:79
  75.5 6.7 %collective-permute-start.27 = (bf16[4,16384]{1,0:T(4,128)(2,1)S(1)}, bf16[4,16384]{1,0:T(4,128)(2,1)S(1)}, u32[]{:S(2)}, u32[]{:S(2)}) collective-permute-start(bf16[4,16384]{1,0:T(4,128)(2,1)S(1)} %collective-permute-done.26.refs_13_), channel_id=1, source_target_pairs={{0,1},{1,0},{2,3},{3,2},{4,5},{5,4},{6,7},{7,6},{8,9},{9,8},{10,11... | collective-permute-start | bytes 393224 | tf_op jit(solution)/shard_map/ppermute | solution.py:79
  76.9 5.3 %collective-permute-start.21 = (bf16[4,16384]{1,0:T(4,128)(2,1)S(1)}, bf16[4,16384]{1,0:T(4,128)(2,1)S(1)}, u32[]{:S(2)}, u32[]{:S(2)}) collective-permute-start(bf16[4,16384]{1,0:T(4,128)(2,1)S(1)} %collective-permute-done.20.refs_7_), channel_id=1, source_target_pairs={{0,1},{1,0},{2,3},{3,2},{4,5},{5,4},{6,7},{7,6},{8,9},{9,8},{10,11... | collective-permute-start | bytes 393224 | tf_op jit(solution)/shard_map/ppermute | solution.py:79
  76.9 5.3 %collective-permute-start.25 = (bf16[4,16384]{1,0:T(4,128)(2,1)S(1)}, bf16[4,16384]{1,0:T(4,128)(2,1)S(1)}, u32[]{:S(2)}, u32[]{:S(2)}) collective-permute-start(bf16[4,16384]{1,0:T(4,128)(2,1)S(1)} %collective-permute-done.24.refs_11_), channel_id=1, source_target_pairs={{0,1},{1,0},{2,3},{3,2},{4,5},{5,4},{6,7},{7,6},{8,9},{9,8},{10,11... | collective-permute-start | bytes 393224 | tf_op jit(solution)/shard_map/ppermute | solution.py:79
  77.4 4.8 %collective-permute-start.29 = (bf16[4,16384]{1,0:T(4,128)(2,1)S(1)}, bf16[4,16384]{1,0:T(4,128)(2,1)S(1)}, u32[]{:S(2)}, u32[]{:S(2)}) collective-permute-start(bf16[4,16384]{1,0:T(4,128)(2,1)S(1)} %collective-permute-done.28.refs_15_), channel_id=1, source_target_pairs={{0,1},{1,0},{2,3},{3,2},{4,5},{5,4},{6,7},{7,6},{8,9},{9,8},{10,11... | collective-permute-start | bytes 393224 | tf_op jit(solution)/shard_map/ppermute | solution.py:79

commit v3 on v2

v3 whole, which is shorter than its diff:
```python
import functools
import math

import jax
import jax.numpy as jnp
from jax import lax
from jax.experimental import pallas as pl
from jax.experimental.pallas import tpu as pltpu
from jax.sharding import PartitionSpec as P

HEADS = 128
KV_HEADS = 8
HEAD_DIM = 128
CACHE = 512

MIB = 1 << 20
STEP = 2048
LANES = 128
QUERY_LOADED = 4
OUT_LOADED = 5
PRODUCT_MIB = 30

rope_base = 500000.0
norm_eps = 1e-05

IN_VMEM = pl.BlockSpec(memory_space=pltpu.VMEM)
IN_HBM = pl.BlockSpec(memory_space=pltpu.HBM)
IN_SMEM = pl.BlockSpec(memory_space=pltpu.SMEM)


def rotate(vector, position):
    middle = vector.shape[-1] // 2
    offsets = jnp.arange(middle, dtype=jnp.float32)
    frequency = jnp.exp(offsets * (-2.0 * math.log(rope_base) / vector.shape[-1]))
    angles = position * frequency
    cosine = jnp.cos(angles)
    sine = jnp.sin(angles)
    leading = vector[..., :middle]
    trailing = vector[..., middle:]
    return jnp.concatenate(
        [leading * cosine - trailing * sine, trailing * cosine + leading * sine], axis=-1
    )


def near(array):
    return pltpu.with_memory_space_constraint(array, pltpu.VMEM)


def far(array):
    return pltpu.with_memory_space_constraint(array, pltpu.HBM)


def norm_kernel(x_hbm, gain_hbm, out_ref, x_ref, gain_ref, sems):
    copies = [
        pltpu.make_async_copy(x_hbm, x_ref, sems.at[0]),
        pltpu.make_async_copy(gain_hbm, gain_ref, sems.at[1]),
    ]
    for copy in copies:
        copy.start()
    for copy in copies:
        copy.wait()
    widened = x_ref[...].astype(jnp.float32)
    inverse = lax.rsqrt(jnp.mean(widened * widened, axis=-1, keepdims=True) + norm_eps)
    lanes = gain_ref.shape[1]
    for j in range(gain_ref.shape[0]):
        columns = pl.ds(j * lanes, lanes)
        gain = gain_ref[pl.ds(j, 1), :].astype(jnp.float32)
        out_ref[:, columns] = (x_ref[:, columns].astype(jnp.float32) * inverse * gain).astype(
            out_ref.dtype
        )


def normalize(activations, gain):
    return pl.pallas_call(
        norm_kernel,
        out_shape=pltpu.VMEM(activations.shape, jnp.bfloat16),
        in_specs=[IN_HBM, IN_HBM],
        out_specs=IN_VMEM,
        scratch_shapes=[
            pltpu.VMEM(activations.shape, activations.dtype),
            pltpu.VMEM((gain.shape[0] // LANES, LANES), gain.dtype),
            pltpu.SemaphoreType.DMA((2,)),
        ],
        compiler_params=pltpu.CompilerParams(vmem_limit_bytes=4 * MIB),
        name="norm",
    )(far(activations), far(gain.reshape(-1, LANES)))


def swap(block, size, distance):
    return lax.ppermute(block, "mp", [(i, i ^ distance) for i in range(size)])


def after(block, *others):
    return lax.optimization_barrier((block, *others))[0]


def gather_product(me, block, size, weights, loaded, ordered):
    held = {0: block}
    distant = [d for d in (8, 12) if d < size]
    for d in distant:
        held[d] = swap(block, size, d)
    if 4 < size:
        held[4] = swap(block, size, 4)
        held[6] = swap(block, size, 6)
    held[2] = swap(block, size, 2)
    piece, token = load([weights[0]], [loaded * STEP], [0], me)
    resident = [(0, piece)]
    for d in distant:
        held[d ^ 2] = swap(after(held[d], token), size, 2)
    for d in range(0, size, 2):
        held[d ^ 1] = swap(held[d], size, 1)
    blocks = [held[r] for r in range(size)]
    depth = block.shape[1]
    return product_part(me, blocks, 0, depth, resident, weights, 0, None, True, ordered)[0]


def load_kernel(count, parts, firsts, *refs):
    sources, results, token, sems = refs[:count], refs[-count - 2 : -2], refs[-2], refs[-1]
    copies = []
    for w, (source, result, first) in enumerate(zip(sources, results, firsts)):
        rows = result.shape[0] // parts
        for i in range(parts):
            copies.append(
                pltpu.make_async_copy(
                    source.at[pl.ds(first + i * rows, rows)],
                    result.at[pl.ds(i * rows, rows)],
                    sems.at[w, i],
                )
            )
    for copy in copies:
        copy.start()
    token[0] = 0
    for copy in copies:
        copy.wait()


def load(arrays, rows, firsts, *behind):
    parts = 2
    count = len(arrays)
    shapes = [(r, *a.shape[1:]) for a, r in zip(arrays, rows)]
    size = sum(2 * math.prod(shape) for shape in shapes)
    return pl.pallas_call(
        functools.partial(load_kernel, count, parts, firsts),
        out_shape=(
            *(pltpu.VMEM(shape, a.dtype) for shape, a in zip(shapes, arrays)),
            jax.ShapeDtypeStruct((1,), jnp.int32),
        ),
        in_specs=[IN_HBM] * count + [IN_SMEM] * len(behind),
        out_specs=(IN_VMEM,) * count + (IN_SMEM,),
        scratch_shapes=[pltpu.SemaphoreType.DMA((count, parts))],
        cost_estimate=pl.CostEstimate(flops=0, bytes_accessed=int(size * 1.0), transcendentals=0),
        compiler_params=pltpu.CompilerParams(vmem_limit_bytes=MIB),
        name="load",
    )(*[far(a) for a in arrays], *behind)


def product_kernel(plan, *refs):
    count, first, depth, resident, streamed, ahead, carried, last, ordered = plan
    refs = list(refs)
    me_ref = refs.pop(0)
    blocks = [refs.pop(0) for _ in range(count)]
    held = [(at, refs.pop(0)) for at in resident]
    weights = [refs.pop(0) for _ in streamed]
    before = refs.pop(0) if carried else None
    out_ref = refs.pop(0)
    kept = refs.pop(0) if ahead else None
    if not last:
        refs.pop(0)[0] = 0
    total, sems = refs[0], refs[1]
    buffers = refs[2:]
    rows = blocks[0].shape[0]
    copies = {}
    for w, (weight, buffer, start) in enumerate(zip(weights, buffers, streamed)):
        for at in range(start, first + depth, STEP):
            copies[w, at] = pltpu.make_async_copy(
                weight.at[pl.ds(at, STEP)],
                buffer.at[pl.ds(at - start, STEP)],
                sems.at[w, (at - first) // STEP],
            )
    for key in sorted(copies, key=lambda k: (k[1], -k[0])):
        copies[key].start()
    if ahead:
        keep = pltpu.make_async_copy(
            weights[0].at[pl.ds(first + depth, ahead)], kept, sems.at[len(streamed), 0]
        )
        keep.start()

    def joined(at):
        parts = []
        for block in blocks:
            start = at if block.shape[1] >= first + depth else at - first
            parts.append(block[:, pl.ds(start, STEP)])
        return jnp.concatenate(parts, axis=0)

    for at in range(first, first + depth, STEP):
        x = joined(at)
        column = 0
        for w, (weight, buffer, start) in enumerate(zip(weights, buffers, streamed)):
            if (w, at) in copies:
                copies[w, at].wait()
                piece = buffer[pl.ds(at - start, STEP), :]
            else:
                begin, ref = [h for h in held if h[0] <= at][-1]
                piece = ref[pl.ds(at - begin, STEP), :]
            columns = pl.ds(column, weight.shape[1])
            term = jnp.dot(x, piece, preferred_element_type=jnp.float32)
            if at > first:
                total[:, columns] += term
            elif carried:
                total[:, columns] = before[:, columns] + term
            else:
                total[:, columns] = term
            column += weight.shape[1]
    if ahead:
        keep.wait()
    me = me_ref[0]
    if not last:
        out_ref[...] = total[...]
    elif ordered:
        to = lax.broadcasted_iota(jnp.int32, (count * rows, count * rows), 0)
        source = lax.broadcasted_iota(jnp.int32, (count * rows, count * rows), 1)
        place = to == ((source // rows) ^ me) * rows + source % rows
        out_ref[...] = jnp.dot(
            place.astype(jnp.bfloat16),
            total[...].astype(jnp.bfloat16),
            preferred_element_type=jnp.float32,
        ).astype(out_ref.dtype)
    else:
        for r in range(count):
            out_ref[me ^ r] = total[pl.ds(r * rows, rows), :].astype(out_ref.dtype)


def product_part(me, blocks, first, depth, resident, weights, ahead, before, last, ordered):
    count, rows = len(blocks), blocks[0].shape[0]
    columns = sum(w.shape[1] for w in weights)
    covered = first + sum(a.shape[0] for _, a in resident)
    streamed = tuple(covered if w == 0 else first for w in range(len(weights)))
    plan = (
        count, first, depth, tuple(at for at, _ in resident), streamed, ahead, before is not None, last, ordered
    )
    if not last:
        outs = [pltpu.VMEM((count * rows, columns), jnp.float32)]
        if ahead:
            outs.append(pltpu.VMEM((ahead, weights[0].shape[1]), weights[0].dtype))
        outs.append(jax.ShapeDtypeStruct((1,), jnp.int32))
    else:
        shape = (count * rows, columns) if ordered else (count, rows, columns)
        outs = [jax.ShapeDtypeStruct(shape, jnp.bfloat16)]
    spaces = [
        pltpu.VMEM((max(first + depth - start, 16), w.shape[1]), w.dtype)
        for w, start in zip(weights, streamed)
    ]
    carried = [] if before is None else [near(before)]
    return pl.pallas_call(
        functools.partial(product_kernel, plan),
        out_shape=tuple(outs),
        in_specs=[IN_SMEM]
        + [IN_VMEM] * (count + len(resident))
        + [IN_HBM] * len(weights)
        + [IN_VMEM] * len(carried),
        out_specs=tuple(IN_SMEM if o.dtype == jnp.int32 else IN_VMEM for o in outs),
        scratch_shapes=[
            pltpu.VMEM((count * rows, columns), jnp.float32),
            pltpu.SemaphoreType.DMA((len(weights) + 1, depth // STEP)),
            *spaces,
        ],
        cost_estimate=pl.CostEstimate(
            flops=2 * count * rows * depth * columns,
            bytes_accessed=depth * columns * 2,
            transcendentals=0,
        ),
        compiler_params=pltpu.CompilerParams(vmem_limit_bytes=sum(2 * a.shape[0] * a.shape[1] for a in spaces) + 6 * MIB),
        name="product",
    )(me, *[near(b) for b in blocks], *[near(a) for _, a in resident], *[far(w) for w in weights], *carried)


def attend_kernel(
    lengths_ref, query_ref, fresh_ref, cos_ref, sin_ref, key_hbm, value_hbm, out_ref, key_ref, value_ref, sems
):
    requests, heads, depth = query_ref.shape
    groups, cache = key_ref.shape[1], key_ref.shape[2]
    per_group = heads // groups
    scaling = 1.0 / math.sqrt(depth)
    copies = []
    for r in range(requests):
        copies.append(
            (
                pltpu.make_async_copy(key_hbm.at[r], key_ref.at[r], sems.at[r, 0]),
                pltpu.make_async_copy(value_hbm.at[r], value_ref.at[r], sems.at[r, 1]),
            )
        )
    for pair in copies[:2]:
        for copy in pair:
            copy.start()

    def turned(values, cosine, sine):
        widened = values.astype(jnp.float32)
        swapped = pltpu.roll(widened, depth // 2, 1)
        return (widened * cosine + swapped * sine).astype(jnp.bfloat16)

    for r in range(requests):
        cosine, sine = cos_ref[pl.ds(r, 1), :], sin_ref[pl.ds(r, 1), :]
        query = turned(query_ref[r], cosine, sine)
        fresh = fresh_ref[r]
        fresh_key = turned(fresh[:groups], cosine, sine).astype(jnp.float32)
        fresh_value = fresh[groups:].astype(jnp.float32)

        def spread(rows):
            return jnp.concatenate(
                [jnp.broadcast_to(rows[g : g + 1], (per_group, depth)) for g in range(groups)], axis=0
            )

        own = (
            jnp.sum(query.astype(jnp.float32) * spread(fresh_key), axis=1, keepdims=True) * scaling
        )
        copies[r][0].wait()
        scores = jnp.concatenate(
            [
                lax.dot_general(
                    query[g * per_group : (g + 1) * per_group],
                    key_ref[r, g],
                    (((1,), (1,)), ((), ())),
                    preferred_element_type=jnp.float32,
                )
                for g in range(groups)
            ],
            axis=0,
        )
        visible = lax.broadcasted_iota(jnp.int32, scores.shape, 1) < lengths_ref[r]
        scores = jnp.where(visible, scores * scaling, -1e30)
        highest = jnp.maximum(jnp.max(scores, axis=1, keepdims=True), own)
        weights = jnp.where(visible, jnp.exp(scores - highest), 0.0)
        own_weight = jnp.exp(own - highest)
        inverse = 1.0 / (jnp.sum(weights, axis=1, keepdims=True) + own_weight)
        probs = (weights * inverse).astype(jnp.bfloat16)
        own_prob = (own_weight * inverse).astype(jnp.bfloat16).astype(jnp.float32)
        copies[r][1].wait()
        if r + 2 < requests:
            for copy in copies[r + 2]:
                copy.start()
        mixed = jnp.concatenate(
            [
                jnp.dot(
                    probs[g * per_group : (g + 1) * per_group],
                    value_ref[r, g],
                    preferred_element_type=jnp.float32,
                )
                for g in range(groups)
            ],
            axis=0,
        )
        out_ref[r] = (mixed + own_prob * spread(fresh_value)).astype(out_ref.dtype)


def attend(arrived, query_cols, keys, values, lengths):
    size, requests, _ = arrived.shape
    depth = HEAD_DIM
    query = arrived[..., :query_cols].reshape(size, requests, -1, depth)
    query = query.transpose(1, 0, 2, 3).reshape(requests, -1, depth)
    fresh = arrived[..., query_cols:].transpose(1, 0, 2).reshape(requests, -1, depth)
    middle = depth // 2
    offsets = jnp.arange(middle, dtype=jnp.float32)
    frequency = jnp.exp(offsets * (-2.0 * math.log(rope_base) / depth))
    angles = lengths.astype(jnp.float32)[:, None] * frequency
    cosine, sine = jnp.cos(angles), jnp.sin(angles)
    attended = pl.pallas_call(
        attend_kernel,
        out_shape=jax.ShapeDtypeStruct(query.shape, jnp.bfloat16),
        in_specs=[IN_SMEM] + [IN_VMEM] * 4 + [IN_HBM] * 2,
        out_specs=IN_VMEM,
        scratch_shapes=[
            pltpu.VMEM(keys.shape, keys.dtype),
            pltpu.VMEM(values.shape, values.dtype),
            pltpu.SemaphoreType.DMA((requests, 2)),
        ],
        compiler_params=pltpu.CompilerParams(vmem_limit_bytes=14 * MIB),
        name="attend",
    )(
        lengths,
        query,
        fresh,
        jnp.concatenate([cosine, cosine], axis=1),
        jnp.concatenate([-sine, sine], axis=1),
        far(keys),
        far(values),
    )
    return attended.reshape(requests, -1)


def shards(activations, gain, q_weight, kv_weight, o_weight, key_cache, value_cache, lengths):
    size = lax.axis_size("mp")
    normed = normalize(activations, gain)
    query_cols = q_weight.shape[1]
    by_swaps = size in (4, 8, 16)
    me = lax.axis_index("mp").astype(jnp.int32).reshape(1)
    if by_swaps:
        projected = gather_product(me, normed, size, [q_weight, kv_weight], QUERY_LOADED, False)
    else:
        piece = lax.all_gather(normed, "mp", axis=0, tiled=True)
        projected = jnp.concatenate(
            [
                jnp.dot(piece, q_weight, preferred_element_type=jnp.float32),
                jnp.dot(piece, kv_weight, preferred_element_type=jnp.float32),
            ],
            axis=1,
        ).astype(jnp.bfloat16).reshape(size, normed.shape[0], -1)
    arrived = lax.all_to_all(projected, "mp", split_axis=0, concat_axis=0, tiled=True)
    attended = attend(arrived, query_cols, key_cache, value_cache, after(lengths, projected))
    if by_swaps:
        return gather_product(me, attended, size, [o_weight], OUT_LOADED, True)
    everyone = lax.all_gather(attended, "mp", axis=0, tiled=True)
    return jnp.dot(everyone, o_weight, preferred_element_type=jnp.float32).astype(jnp.bfloat16)


def solution(mesh):
    placed = (
        P(("groups", "mp"), None),
        P(),
        P(None, "mp"),
        P(None, "mp"),
        P(None, "mp"),
        P(("groups", "mp"), None, None, None),
        P(("groups", "mp"), None, None, None),
        P(("groups", "mp")),
    )
    return jax.shard_map(
        shards, mesh=mesh, in_specs=placed, out_specs=P("groups", "mp"), check_vma=False
    )
```

time: 91.5 us -> 88.6 us (0.968)
  Pallas kernels: 29.5 us -> 36.7 us
  matrix products: 4.85 us -> 0 us
  waiting for transfers between devices: 27.9 us -> 23.8 us
    pallas_call x4 -> x5, Pallas kernels: 28.3 us -> 35.5 us  [the longest x2 16.2 us: product_part(): pl.pallas_call(functools.partial(product_kernel, plan), out_shape=tuple(o...]
    dot_general x3 -> x0, matrix products: 4.85 us -> none  [the longest x1 3.81 us: attend(): jnp.einsum('rgqd,rgtd->rgqt', query, key_cache, preferred_element_type=jn...]
    ppermute x30, waiting for transfers between devices: 19.8 us -> 15.9 us  [swap(): return lax.ppermute(block, 'mp', [(i, i ^ distance) for i in range(size)])]
  transfers between devices with their start and end apart: 31 -> 31, of which waited for: 11 -> 10; matrix products, arithmetic and copies ran while one was open for 0% -> 0% of each run, Pallas kernels for 10% -> 16%
where the time goes in v3:
time: 88.6 us; the launch traced here: 88.3 us
  Pallas kernels  36.7 us (41%)
  starting transfers between devices  27 us (30%)
  waiting for transfers between devices  23.8 us (27%)
    ppermute x30, starting transfers between devices, swap(): return lax.ppermute(block, 'mp', [(i, i ^ distance) for i in range(size)])  21 us
    pallas_call x2, Pallas kernels, product_part(): pl.pallas_call(functools.partial(product_kernel, plan), out_shape=tuple(o...  16.2 us
    ppermute x30, waiting for transfers between devices, swap(): return lax.ppermute(block, 'mp', [(i, i ^ distance) for i in range(size)])  15.9 us
    pallas_call x2, Pallas kernels, load(): pl.pallas_call(functools.partial(load_kernel, count, parts, firsts), out_...  13.8 us
    all_to_all x1, waiting for transfers between devices, shards(): lax.all_to_all(projected, 'mp', split_axis=0, concat_axis=0, tiled=True)  7.98 us
    all_to_all x1, starting transfers between devices, shards(): lax.all_to_all(projected, 'mp', split_axis=0, concat_axis=0, tiled=True)  5.99 us
    pallas_call x1, Pallas kernels, attend(): pl.pallas_call(attend_kernel, out_shape=jax.ShapeDtypeStruct(query.shape,...  5.45 us
  transfers between devices with their start and end apart: 31, of which 10 were waited for; matrix products, arithmetic and copies ran while one was open for 0% of the time, Pallas kernels for 16%

profile of v3, /device:TPU:0, one launch (start us, length us, event | category | flops | bytes accessed | tf_op | source)
XLA Modules:
  0.0 88.3 jit_solution(8855551157461017889)
XLA Ops:
  0.0 1.2 %norm.1.refs_1_ = bf16[4,16384]{1,0:T(4,128)(2,1)S(1)} custom-call(bf16[4,16384]{1,0:T(4,128)(2,1)} %x_hbm.1, bf16[128,128]{1,0:T(8,128)(2,1)} %bitcast.24), custom_call_target="tpu_custom_call" | custom-call | tf_op jit(solution)/shard_map/norm/pallas_call | solution.py:74
  1.2 5.1 %collective-permute-start.11 = (bf16[4,16384]{1,0:T(4,128)(2,1)S(1)}, bf16[4,16384]{1,0:T(4,128)(2,1)S(1)}, u32[]{:S(2)}, u32[]{:S(2)}) collective-permute-start(bf16[4,16384]{1,0:T(4,128)(2,1)S(1)} %norm.1.refs_1_), channel_id=1, source_target_pairs={{0,12},{1,13},{2,14},{3,15},{4,8},{5,9},{6,10},{7,11},{8,4},{9,5},... | collective-permute-start | bytes 393224 | tf_op jit(solution)/shard_map/ppermute | solution.py:90
  6.3 0.0 collective-permute-start.7
  6.3 1.7 %collective-permute-start.5 = (bf16[4,16384]{1,0:T(4,128)(2,1)S(1)}, bf16[4,16384]{1,0:T(4,128)(2,1)S(1)}, u32[]{:S(2)}, u32[]{:S(2)}) collective-permute-start(bf16[4,16384]{1,0:T(4,128)(2,1)S(1)} %norm.1.refs_1_), channel_id=1, source_target_pairs={{0,6},{1,7},{2,4},{3,5},{4,2},{5,3},{6,0},{7,1},{8,14},{9,15},{10,... | collective-permute-start | bytes 393224 | tf_op jit(solution)/shard_map/ppermute | solution.py:90
  8.1 1.2 %collective-permute-start.3 = (bf16[4,16384]{1,0:T(4,128)(2,1)S(1)}, bf16[4,16384]{1,0:T(4,128)(2,1)S(1)}, u32[]{:S(2)}, u32[]{:S(2)}) collective-permute-start(bf16[4,16384]{1,0:T(4,128)(2,1)S(1)} %norm.1.refs_1_), channel_id=1, source_target_pairs={{0,4},{1,5},{2,6},{3,7},{4,0},{5,1},{6,2},{7,3},{8,12},{9,13},{10,... | collective-permute-start | bytes 393224 | tf_op jit(solution)/shard_map/ppermute | solution.py:90
  9.3 0.5 collective-permute-start.1
  9.8 6.3 %load.2 = (bf16[8192,1024]{1,0:T(8,128)(2,1)S(1)}, s32[1]{0:T(128)}) custom-call(bf16[16384,1024]{1,0:T(8,128)(2,1)} %refs_18_.2, s32[1]{0:T(128)} %bitcast.refs_1_.refs_0_), custom_call_target="tpu_custom_call" | custom-call | bytes 16777216 | tf_op jit(solution)/shard_map/load/pallas_call | solution.py:142
  16.1 0.0 collective-permute-done.11.refs_13_
  16.1 0.1 collective-permute-start
  16.2 1.3 %collective-permute-done.7.refs_9_ = bf16[4,16384]{1,0:T(4,128)(2,1)S(1)} collective-permute-done((bf16[4,16384]{1,0:T(4,128)(2,1)S(1)}, bf16[4,16384]{1,0:T(4,128)(2,1)S(1)}, u32[]{:S(2)}, u32[]{:S(2)}) %collective-permute-start.7) | collective-permute-done | bytes 131104 | tf_op jit(solution)/shard_map/ppermute | solution.py:90
  17.5 0.0 collective-permute-start.12
  17.5 0.0 collective-permute-done.5.refs_7_
  17.5 0.5 collective-permute-start.8
  18.0 0.5 collective-permute-done.3.refs_5_
  18.6 1.4 %collective-permute-start.9 = (bf16[4,16384]{1,0:T(4,128)(2,1)S(1)}, bf16[4,16384]{1,0:T(4,128)(2,1)S(1)}, u32[]{:S(2)}, u32[]{:S(2)}) collective-permute-start(bf16[4,16384]{1,0:T(4,128)(2,1)S(1)} %collective-permute-done.7.refs_9_), channel_id=1, source_target_pairs={{0,2},{1,3},{2,0},{3,1},{4,6},{5,7},{6,4},{7,5},{8,10},{9,11},{10,... | collective-permute-start | bytes 393224 | tf_op jit(solution)/shard_map/ppermute | solution.py:90
  19.9 0.0 collective-permute-done.1.refs_3_
  19.9 0.7 collective-permute-start.13
  20.6 0.0 collective-permute-done.refs_2_
  20.6 0.0 collective-permute-start.6
  20.6 0.0 collective-permute-done.12.refs_14_
  20.6 0.5 collective-permute-start.4
  21.1 0.0 collective-permute-done.8.refs_10_
  21.1 0.1 collective-permute-start.2
  21.2 3.7 %collective-permute-done.9.refs_11_ = bf16[4,16384]{1,0:T(4,128)(2,1)S(1)} collective-permute-done((bf16[4,16384]{1,0:T(4,128)(2,1)S(1)}, bf16[4,16384]{1,0:T(4,128)(2,1)S(1)}, u32[]{:S(2)}, u32[]{:S(2)}) %collective-permute-start.9) | collective-permute-done | bytes 131104 | tf_op jit(solution)/shard_map/ppermute | solution.py:90
  24.9 0.0 collective-permute-start.10
  24.9 1.4 %collective-permute-done.13.refs_15_ = bf16[4,16384]{1,0:T(4,128)(2,1)S(1)} collective-permute-done((bf16[4,16384]{1,0:T(4,128)(2,1)S(1)}, bf16[4,16384]{1,0:T(4,128)(2,1)S(1)}, u32[]{:S(2)}, u32[]{:S(2)}) %collective-permute-start.13) | collective-permute-done | bytes 131104 | tf_op jit(solution)/shard_map/ppermute | solution.py:90
  26.3 0.0 collective-permute-start.14
  26.4 0.0 collective-permute-done.2.refs_4_
  26.4 0.0 collective-permute-done.10.refs_12_
  26.4 1.3 %collective-permute-done.14.refs_16_ = bf16[4,16384]{1,0:T(4,128)(2,1)S(1)} collective-permute-done((bf16[4,16384]{1,0:T(4,128)(2,1)S(1)}, bf16[4,16384]{1,0:T(4,128)(2,1)S(1)}, u32[]{:S(2)}, u32[]{:S(2)}) %collective-permute-start.14) | collective-permute-done | bytes 131104 | tf_op jit(solution)/shard_map/ppermute | solution.py:90
  27.7 9.1 %product.2 = bf16[16,4,1152]{2,1,0:T(4,128)(2,1)} custom-call(s32[1]{0:T(128)} %bitcast.refs_1_.refs_0_, bf16[4,16384]{1,0:T(4,128)(2,1)S(1)} %norm.1.refs_1_, bf16[4,16384]{1,0:T(4,128)(2,1)S(1)} %collective-permute-done.refs_2_, bf16[4,16384]{1,0:T(4,128)(2,1)S(1)} %collective-permute-done.1.refs_3_, bf16[4,16384]{1,0:T(4,128)(2,1)S(1)} %collective-permute-done.2.refs_4_, ...), custom_call_target="tpu_custom_call" | custom-call | flops 2415919104 | bytes 37748736 | tf_op jit(solution)/shard_map/product/pallas_call | solution.py:254
  36.8 6.0 %all-to-all-start = ((bf16[16,4,1152]{2,1,0:T(4,128)(2,1)}), bf16[16,4,1152]{2,1,0:T(4,128)(2,1)S(1)}, u32[]{:S(2)}, u32[]{:S(2)}) async-start(bf16[16,4,1152]{2,1,0:T(4,128)(2,1)} %product.2), calls=%async_computation | async-start | bytes 294912 | tf_op jit(solution)/shard_map/all_to_all | solution.py:407
  42.8 0.1 fusion
  42.9 0.1 pad_maximum_fusion
  43.0 8.0 %all-to-all-done = bf16[16,4,1152]{2,1,0:T(4,128)(2,1)S(1)} async-done(((bf16[16,4,1152]{2,1,0:T(4,128)(2,1)}), bf16[16,4,1152]{2,1,0:T(4,128)(2,1)S(1)}, u32[]{:S(2)}, u32[]{:S(2)}) %all-to-all-start) | async-done | bytes 147488 | tf_op jit(solution)/shard_map/all_to_all | solution.py:407
  51.0 0.1 reshape.23
  51.1 5.4 %attend.1 = bf16[4,128,128]{2,1,0:T(8,128)(2,1)S(1)} custom-call(s32[4]{0:T(128)S(1)} %copy-done, bf16[4,128,128]{2,1,0:T(8,128)(2,1)S(1)} %bitcast.21, bf16[4,16,128]{2,1,0:T(8,128)(2,1)S(1)} %bitcast.23, f32[4,128]{1,0:T(4,128)S(1)} %get-tuple-element.26.cos_ref, f32[4,128]{1,0:T(4,128)S(1)} %get-tuple-element.27.sin_ref, ...), custom_call_target="tpu_custom_call" | custom-call | tf_op jit(solution)/shard_map/attend/pallas_call | solution.py:366
  56.6 0.1 copy.17
  56.7 0.8 collective-permute-start.26
  57.5 0.0 collective-permute-start.22
  57.6 2.3 %collective-permute-start.20 = (bf16[4,16384]{1,0:T(4,128)(2,1)S(1)}, bf16[4,16384]{1,0:T(4,128)(2,1)S(1)}, u32[]{:S(2)}, u32[]{:S(2)}) collective-permute-start(bf16[4,16384]{1,0:T(4,128)(2,1)S(1)} %bitcast.16), channel_id=1, source_target_pairs={{0,6},{1,7},{2,4},{3,5},{4,2},{5,3},{6,0},{7,1},{8,14},{9,15},{10,... | collective-permute-start | bytes 393224 | tf_op jit(solution)/shard_map/ppermute | solution.py:90
  59.9 1.3 %collective-permute-start.18 = (bf16[4,16384]{1,0:T(4,128)(2,1)S(1)}, bf16[4,16384]{1,0:T(4,128)(2,1)S(1)}, u32[]{:S(2)}, u32[]{:S(2)}) collective-permute-start(bf16[4,16384]{1,0:T(4,128)(2,1)S(1)} %bitcast.17), channel_id=1, source_target_pairs={{0,4},{1,5},{2,6},{3,7},{4,0},{5,1},{6,2},{7,3},{8,12},{9,13},{10,... | collective-permute-start | bytes 393224 | tf_op jit(solution)/shard_map/ppermute | solution.py:90
  61.2 1.5 %collective-permute-start.16 = (bf16[4,16384]{1,0:T(4,128)(2,1)S(1)}, bf16[4,16384]{1,0:T(4,128)(2,1)S(1)}, u32[]{:S(2)}, u32[]{:S(2)}) collective-permute-start(bf16[4,16384]{1,0:T(4,128)(2,1)S(1)} %bitcast.18), channel_id=1, source_target_pairs={{0,2},{1,3},{2,0},{3,1},{4,6},{5,7},{6,4},{7,5},{8,10},{9,11},{10,... | collective-permute-start | bytes 393224 | tf_op jit(solution)/shard_map/ppermute | solution.py:90
  62.6 7.5 %load.3 = (bf16[10240,1024]{1,0:T(8,128)(2,1)S(1)}, s32[1]{0:T(128)}) custom-call(bf16[16384,1024]{1,0:T(8,128)(2,1)} %refs_18_.3, s32[1]{0:T(128)} %bitcast.refs_1_.refs_0_), custom_call_target="tpu_custom_call" | custom-call | bytes 20971520 | tf_op jit(solution)/shard_map/load/pallas_call | solution.py:142
  70.1 0.1 collective-permute-start.15
  70.2 0.0 collective-permute-done.22.refs_9_
  70.2 0.5 collective-permute-start.27
  70.7 0.0 collective-permute-done.20.refs_7_
  70.7 0.1 collective-permute-start.23
  70.8 1.1 %collective-permute-done.18.refs_5_ = bf16[4,16384]{1,0:T(4,128)(2,1)S(1)} collective-permute-done((bf16[4,16384]{1,0:T(4,128)(2,1)S(1)}, bf16[4,16384]{1,0:T(4,128)(2,1)S(1)}, u32[]{:S(2)}, u32[]{:S(2)}) %collective-permute-start.18) | collective-permute-done | bytes 131104 | tf_op jit(solution)/shard_map/ppermute | solution.py:90
  71.9 0.7 collective-permute-start.24
  72.5 1.4 %collective-permute-start.28 = (bf16[4,16384]{1,0:T(4,128)(2,1)S(1)}, bf16[4,16384]{1,0:T(4,128)(2,1)S(1)}, u32[]{:S(2)}, u32[]{:S(2)}) collective-permute-start(bf16[4,16384]{1,0:T(4,128)(2,1)S(1)} %collective-permute-done.26.refs_13_), channel_id=1, source_target_pairs={{0,2},{1,3},{2,0},{3,1},{4,6},{5,7},{6,4},{7,5},{8,10},{9,11},{10,... | collective-permute-start | bytes 393224 | tf_op jit(solution)/shard_map/ppermute | solution.py:90
  73.9 0.0 collective-permute-done.15.refs_2_
  73.9 0.0 collective-permute-start.21
  73.9 0.0 collective-permute-done.27.refs_14_
  73.9 0.5 collective-permute-start.19
  74.4 0.0 collective-permute-done.23.refs_10_
  74.4 0.1 collective-permute-start.17
  74.5 3.8 %collective-permute-done.24.refs_11_ = bf16[4,16384]{1,0:T(4,128)(2,1)S(1)} collective-permute-done((bf16[4,16384]{1,0:T(4,128)(2,1)S(1)}, bf16[4,16384]{1,0:T(4,128)(2,1)S(1)}, u32[]{:S(2)}, u32[]{:S(2)}) %collective-permute-start.24) | collective-permute-done | bytes 131104 | tf_op jit(solution)/shard_map/ppermute | solution.py:90
  78.3 0.0 collective-permute-start.25
  78.3 1.4 %collective-permute-done.28.refs_15_ = bf16[4,16384]{1,0:T(4,128)(2,1)S(1)} collective-permute-done((bf16[4,16384]{1,0:T(4,128)(2,1)S(1)}, bf16[4,16384]{1,0:T(4,128)(2,1)S(1)}, u32[]{:S(2)}, u32[]{:S(2)}) %collective-permute-start.28) | collective-permute-done | bytes 131104 | tf_op jit(solution)/shard_map/ppermute | solution.py:90
  79.7 0.0 collective-permute-start.29
  79.7 1.3 %collective-permute-done.29.refs_16_ = bf16[4,16384]{1,0:T(4,128)(2,1)S(1)} collective-permute-done((bf16[4,16384]{1,0:T(4,128)(2,1)S(1)}, bf16[4,16384]{1,0:T(4,128)(2,1)S(1)}, u32[]{:S(2)}, u32[]{:S(2)}) %collective-permute-start.29) | collective-permute-done | bytes 131104 | tf_op jit(solution)/shard_map/ppermute | solution.py:90
  81.0 7.1 %product.3 = bf16[64,1024]{1,0:T(8,128)(2,1)} custom-call(s32[1]{0:T(128)} %bitcast.refs_1_.refs_0_, bf16[4,16384]{1,0:T(4,128)(2,1)S(1)} %bitcast.20, bf16[4,16384]{1,0:T(4,128)(2,1)S(1)} %collective-permute-done.15.refs_2_, bf16[4,16384]{1,0:T(4,128)(2,1)S(1)} %collective-permute-done.16.refs_3_, bf16[4,16384]{1,0:T(4,128)(2,1)S(1)} %collective-permute-done.17.refs_4_, ...), custom_call_target="tpu_custom_call" | custom-call | flops 2147483648 | bytes 33554432 | tf_op jit(solution)/shard_map/product/pallas_call | solution.py:254
  (16 shorter events, 0.1 us)
Async XLA Ops:
  1.2 14.9 %collective-permute-start.11 = (bf16[4,16384]{1,0:T(4,128)(2,1)S(1)}, bf16[4,16384]{1,0:T(4,128)(2,1)S(1)}, u32[]{:S(2)}, u32[]{:S(2)}) collective-permute-start(bf16[4,16384]{1,0:T(4,128)(2,1)S(1)} %norm.1.refs_1_), channel_id=1, source_target_pairs={{0,12},{1,13},{2,14},{3,15},{4,8},{5,9},{6,10},{7,11},{8,4},{9,5},... | collective-permute-start | bytes 393224 | tf_op jit(solution)/shard_map/ppermute | solution.py:90
  6.3 11.2 %collective-permute-start.7 = (bf16[4,16384]{1,0:T(4,128)(2,1)S(1)}, bf16[4,16384]{1,0:T(4,128)(2,1)S(1)}, u32[]{:S(2)}, u32[]{:S(2)}) collective-permute-start(bf16[4,16384]{1,0:T(4,128)(2,1)S(1)} %norm.1.refs_1_), channel_id=1, source_target_pairs={{0,8},{1,9},{2,10},{3,11},{4,12},{5,13},{6,14},{7,15},{8,0},{9,1},... | collective-permute-start | bytes 393224 | tf_op jit(solution)/shard_map/ppermute | solution.py:90
  6.3 11.2 %collective-permute-start.5 = (bf16[4,16384]{1,0:T(4,128)(2,1)S(1)}, bf16[4,16384]{1,0:T(4,128)(2,1)S(1)}, u32[]{:S(2)}, u32[]{:S(2)}) collective-permute-start(bf16[4,16384]{1,0:T(4,128)(2,1)S(1)} %norm.1.refs_1_), channel_id=1, source_target_pairs={{0,6},{1,7},{2,4},{3,5},{4,2},{5,3},{6,0},{7,1},{8,14},{9,15},{10,... | collective-permute-start | bytes 393224 | tf_op jit(solution)/shard_map/ppermute | solution.py:90
  8.1 10.5 %collective-permute-start.3 = (bf16[4,16384]{1,0:T(4,128)(2,1)S(1)}, bf16[4,16384]{1,0:T(4,128)(2,1)S(1)}, u32[]{:S(2)}, u32[]{:S(2)}) collective-permute-start(bf16[4,16384]{1,0:T(4,128)(2,1)S(1)} %norm.1.refs_1_), channel_id=1, source_target_pairs={{0,4},{1,5},{2,6},{3,7},{4,0},{5,1},{6,2},{7,3},{8,12},{9,13},{10,... | collective-permute-start | bytes 393224 | tf_op jit(solution)/shard_map/ppermute | solution.py:90
  9.3 10.6 %collective-permute-start.1 = (bf16[4,16384]{1,0:T(4,128)(2,1)S(1)}, bf16[4,16384]{1,0:T(4,128)(2,1)S(1)}, u32[]{:S(2)}, u32[]{:S(2)}) collective-permute-start(bf16[4,16384]{1,0:T(4,128)(2,1)S(1)} %norm.1.refs_1_), channel_id=1, source_target_pairs={{0,2},{1,3},{2,0},{3,1},{4,6},{5,7},{6,4},{7,5},{8,10},{9,11},{10,... | collective-permute-start | bytes 393224 | tf_op jit(solution)/shard_map/ppermute | solution.py:90
  16.1 4.5 %collective-permute-start = (bf16[4,16384]{1,0:T(4,128)(2,1)S(1)}, bf16[4,16384]{1,0:T(4,128)(2,1)S(1)}, u32[]{:S(2)}, u32[]{:S(2)}) collective-permute-start(bf16[4,16384]{1,0:T(4,128)(2,1)S(1)} %norm.1.refs_1_), channel_id=1, source_target_pairs={{0,1},{1,0},{2,3},{3,2},{4,5},{5,4},{6,7},{7,6},{8,9},{9,8},{10,11... | collective-permute-start | bytes 393224 | tf_op jit(solution)/shard_map/ppermute | solution.py:90
  17.5 3.1 %collective-permute-start.12 = (bf16[4,16384]{1,0:T(4,128)(2,1)S(1)}, bf16[4,16384]{1,0:T(4,128)(2,1)S(1)}, u32[]{:S(2)}, u32[]{:S(2)}) collective-permute-start(bf16[4,16384]{1,0:T(4,128)(2,1)S(1)} %collective-permute-done.11.refs_13_), channel_id=1, source_target_pairs={{0,1},{1,0},{2,3},{3,2},{4,5},{5,4},{6,7},{7,6},{8,9},{9,8},{10,11... | collective-permute-start | bytes 393224 | tf_op jit(solution)/shard_map/ppermute | solution.py:90
  17.5 3.6 %collective-permute-start.8 = (bf16[4,16384]{1,0:T(4,128)(2,1)S(1)}, bf16[4,16384]{1,0:T(4,128)(2,1)S(1)}, u32[]{:S(2)}, u32[]{:S(2)}) collective-permute-start(bf16[4,16384]{1,0:T(4,128)(2,1)S(1)} %collective-permute-done.7.refs_9_), channel_id=1, source_target_pairs={{0,1},{1,0},{2,3},{3,2},{4,5},{5,4},{6,7},{7,6},{8,9},{9,8},{10,11... | collective-permute-start | bytes 393224 | tf_op jit(solution)/shard_map/ppermute | solution.py:90
  18.6 6.3 %collective-permute-start.9 = (bf16[4,16384]{1,0:T(4,128)(2,1)S(1)}, bf16[4,16384]{1,0:T(4,128)(2,1)S(1)}, u32[]{:S(2)}, u32[]{:S(2)}) collective-permute-start(bf16[4,16384]{1,0:T(4,128)(2,1)S(1)} %collective-permute-done.7.refs_9_), channel_id=1, source_target_pairs={{0,2},{1,3},{2,0},{3,1},{4,6},{5,7},{6,4},{7,5},{8,10},{9,11},{10,... | collective-permute-start | bytes 393224 | tf_op jit(solution)/shard_map/ppermute | solution.py:90
  19.9 6.4 %collective-permute-start.13 = (bf16[4,16384]{1,0:T(4,128)(2,1)S(1)}, bf16[4,16384]{1,0:T(4,128)(2,1)S(1)}, u32[]{:S(2)}, u32[]{:S(2)}) collective-permute-start(bf16[4,16384]{1,0:T(4,128)(2,1)S(1)} %collective-permute-done.11.refs_13_), channel_id=1, source_target_pairs={{0,2},{1,3},{2,0},{3,1},{4,6},{5,7},{6,4},{7,5},{8,10},{9,11},{10,... | collective-permute-start | bytes 393224 | tf_op jit(solution)/shard_map/ppermute | solution.py:90
  20.6 5.7 %collective-permute-start.6 = (bf16[4,16384]{1,0:T(4,128)(2,1)S(1)}, bf16[4,16384]{1,0:T(4,128)(2,1)S(1)}, u32[]{:S(2)}, u32[]{:S(2)}) collective-permute-start(bf16[4,16384]{1,0:T(4,128)(2,1)S(1)} %collective-permute-done.5.refs_7_), channel_id=1, source_target_pairs={{0,1},{1,0},{2,3},{3,2},{4,5},{5,4},{6,7},{7,6},{8,9},{9,8},{10,11... | collective-permute-start | bytes 393224 | tf_op jit(solution)/shard_map/ppermute | solution.py:90
  20.6 5.7 %collective-permute-start.4 = (bf16[4,16384]{1,0:T(4,128)(2,1)S(1)}, bf16[4,16384]{1,0:T(4,128)(2,1)S(1)}, u32[]{:S(2)}, u32[]{:S(2)}) collective-permute-start(bf16[4,16384]{1,0:T(4,128)(2,1)S(1)} %collective-permute-done.3.refs_5_), channel_id=1, source_target_pairs={{0,1},{1,0},{2,3},{3,2},{4,5},{5,4},{6,7},{7,6},{8,9},{9,8},{10,11... | collective-permute-start | bytes 393224 | tf_op jit(solution)/shard_map/ppermute | solution.py:90
  21.1 5.2 %collective-permute-start.2 = (bf16[4,16384]{1,0:T(4,128)(2,1)S(1)}, bf16[4,16384]{1,0:T(4,128)(2,1)S(1)}, u32[]{:S(2)}, u32[]{:S(2)}) collective-permute-start(bf16[4,16384]{1,0:T(4,128)(2,1)S(1)} %collective-permute-done.1.refs_3_), channel_id=1, source_target_pairs={{0,1},{1,0},{2,3},{3,2},{4,5},{5,4},{6,7},{7,6},{8,9},{9,8},{10,11... | collective-permute-start | bytes 393224 | tf_op jit(solution)/shard_map/ppermute | solution.py:90
  24.9 1.5 %collective-permute-start.10 = (bf16[4,16384]{1,0:T(4,128)(2,1)S(1)}, bf16[4,16384]{1,0:T(4,128)(2,1)S(1)}, u32[]{:S(2)}, u32[]{:S(2)}) collective-permute-start(bf16[4,16384]{1,0:T(4,128)(2,1)S(1)} %collective-permute-done.9.refs_11_), channel_id=1, source_target_pairs={{0,1},{1,0},{2,3},{3,2},{4,5},{5,4},{6,7},{7,6},{8,9},{9,8},{10,11... | collective-permute-start | bytes 393224 | tf_op jit(solution)/shard_map/ppermute | solution.py:90
  26.3 1.3 %collective-permute-start.14 = (bf16[4,16384]{1,0:T(4,128)(2,1)S(1)}, bf16[4,16384]{1,0:T(4,128)(2,1)S(1)}, u32[]{:S(2)}, u32[]{:S(2)}) collective-permute-start(bf16[4,16384]{1,0:T(4,128)(2,1)S(1)} %collective-permute-done.13.refs_15_), channel_id=1, source_target_pairs={{0,1},{1,0},{2,3},{3,2},{4,5},{5,4},{6,7},{7,6},{8,9},{9,8},{10,11... | collective-permute-start | bytes 393224 | tf_op jit(solution)/shard_map/ppermute | solution.py:90
  27.7 15.1 %copy-start = (s32[4]{0:T(128)S(1)}, s32[4]{0:T(128)}, u32[]{:S(2)}) copy-start(s32[4]{0:T(128)} %lengths_ref) | copy-start | bytes 52
  36.8 14.2 %all-to-all-start = ((bf16[16,4,1152]{2,1,0:T(4,128)(2,1)}), bf16[16,4,1152]{2,1,0:T(4,128)(2,1)S(1)}, u32[]{:S(2)}, u32[]{:S(2)}) async-start(bf16[16,4,1152]{2,1,0:T(4,128)(2,1)} %product.2), calls=%async_computation | async-start | bytes 294912 | tf_op jit(solution)/shard_map/all_to_all | solution.py:407
  56.7 13.4 %collective-permute-start.26 = (bf16[4,16384]{1,0:T(4,128)(2,1)S(1)}, bf16[4,16384]{1,0:T(4,128)(2,1)S(1)}, u32[]{:S(2)}, u32[]{:S(2)}) collective-permute-start(bf16[4,16384]{1,0:T(4,128)(2,1)S(1)} %bitcast.14), channel_id=1, source_target_pairs={{0,12},{1,13},{2,14},{3,15},{4,8},{5,9},{6,10},{7,11},{8,4},{9,5},... | collective-permute-start | bytes 393224 | tf_op jit(solution)/shard_map/ppermute | solution.py:90
  57.5 12.7 %collective-permute-start.22 = (bf16[4,16384]{1,0:T(4,128)(2,1)S(1)}, bf16[4,16384]{1,0:T(4,128)(2,1)S(1)}, u32[]{:S(2)}, u32[]{:S(2)}) collective-permute-start(bf16[4,16384]{1,0:T(4,128)(2,1)S(1)} %bitcast.15), channel_id=1, source_target_pairs={{0,8},{1,9},{2,10},{3,11},{4,12},{5,13},{6,14},{7,15},{8,0},{9,1},... | collective-permute-start | bytes 393224 | tf_op jit(solution)/shard_map/ppermute | solution.py:90
  57.6 13.1 %collective-permute-start.20 = (bf16[4,16384]{1,0:T(4,128)(2,1)S(1)}, bf16[4,16384]{1,0:T(4,128)(2,1)S(1)}, u32[]{:S(2)}, u32[]{:S(2)}) collective-permute-start(bf16[4,16384]{1,0:T(4,128)(2,1)S(1)} %bitcast.16), channel_id=1, source_target_pairs={{0,6},{1,7},{2,4},{3,5},{4,2},{5,3},{6,0},{7,1},{8,14},{9,15},{10,... | collective-permute-start | bytes 393224 | tf_op jit(solution)/shard_map/ppermute | solution.py:90
  59.9 12.0 %collective-permute-start.18 = (bf16[4,16384]{1,0:T(4,128)(2,1)S(1)}, bf16[4,16384]{1,0:T(4,128)(2,1)S(1)}, u32[]{:S(2)}, u32[]{:S(2)}) collective-permute-start(bf16[4,16384]{1,0:T(4,128)(2,1)S(1)} %bitcast.17), channel_id=1, source_target_pairs={{0,4},{1,5},{2,6},{3,7},{4,0},{5,1},{6,2},{7,3},{8,12},{9,13},{10,... | collective-permute-start | bytes 393224 | tf_op jit(solution)/shard_map/ppermute | solution.py:90
  61.2 11.4 %collective-permute-start.16 = (bf16[4,16384]{1,0:T(4,128)(2,1)S(1)}, bf16[4,16384]{1,0:T(4,128)(2,1)S(1)}, u32[]{:S(2)}, u32[]{:S(2)}) collective-permute-start(bf16[4,16384]{1,0:T(4,128)(2,1)S(1)} %bitcast.18), channel_id=1, source_target_pairs={{0,2},{1,3},{2,0},{3,1},{4,6},{5,7},{6,4},{7,5},{8,10},{9,11},{10,... | collective-permute-start | bytes 393224 | tf_op jit(solution)/shard_map/ppermute | solution.py:90
  70.1 3.8 %collective-permute-start.15 = (bf16[4,16384]{1,0:T(4,128)(2,1)S(1)}, bf16[4,16384]{1,0:T(4,128)(2,1)S(1)}, u32[]{:S(2)}, u32[]{:S(2)}) collective-permute-start(bf16[4,16384]{1,0:T(4,128)(2,1)S(1)} %bitcast.19), channel_id=1, source_target_pairs={{0,1},{1,0},{2,3},{3,2},{4,5},{5,4},{6,7},{7,6},{8,9},{9,8},{10,11... | collective-permute-start | bytes 393224 | tf_op jit(solution)/shard_map/ppermute | solution.py:90
  70.2 3.7 %collective-permute-start.27 = (bf16[4,16384]{1,0:T(4,128)(2,1)S(1)}, bf16[4,16384]{1,0:T(4,128)(2,1)S(1)}, u32[]{:S(2)}, u32[]{:S(2)}) collective-permute-start(bf16[4,16384]{1,0:T(4,128)(2,1)S(1)} %collective-permute-done.26.refs_13_), channel_id=1, source_target_pairs={{0,1},{1,0},{2,3},{3,2},{4,5},{5,4},{6,7},{7,6},{8,9},{9,8},{10,11... | collective-permute-start | bytes 393224 | tf_op jit(solution)/shard_map/ppermute | solution.py:90
  70.7 3.7 %collective-permute-start.23 = (bf16[4,16384]{1,0:T(4,128)(2,1)S(1)}, bf16[4,16384]{1,0:T(4,128)(2,1)S(1)}, u32[]{:S(2)}, u32[]{:S(2)}) collective-permute-start(bf16[4,16384]{1,0:T(4,128)(2,1)S(1)} %collective-permute-done.22.refs_9_), channel_id=1, source_target_pairs={{0,1},{1,0},{2,3},{3,2},{4,5},{5,4},{6,7},{7,6},{8,9},{9,8},{10,11... | collective-permute-start | bytes 393224 | tf_op jit(solution)/shard_map/ppermute | solution.py:90
  71.9 6.4 %collective-permute-start.24 = (bf16[4,16384]{1,0:T(4,128)(2,1)S(1)}, bf16[4,16384]{1,0:T(4,128)(2,1)S(1)}, u32[]{:S(2)}, u32[]{:S(2)}) collective-permute-start(bf16[4,16384]{1,0:T(4,128)(2,1)S(1)} %collective-permute-done.22.refs_9_), channel_id=1, source_target_pairs={{0,2},{1,3},{2,0},{3,1},{4,6},{5,7},{6,4},{7,5},{8,10},{9,11},{10,... | collective-permute-start | bytes 393224 | tf_op jit(solution)/shard_map/ppermute | solution.py:90
  72.5 7.1 %collective-permute-start.28 = (bf16[4,16384]{1,0:T(4,128)(2,1)S(1)}, bf16[4,16384]{1,0:T(4,128)(2,1)S(1)}, u32[]{:S(2)}, u32[]{:S(2)}) collective-permute-start(bf16[4,16384]{1,0:T(4,128)(2,1)S(1)} %collective-permute-done.26.refs_13_), channel_id=1, source_target_pairs={{0,2},{1,3},{2,0},{3,1},{4,6},{5,7},{6,4},{7,5},{8,10},{9,11},{10,... | collective-permute-start | bytes 393224 | tf_op jit(solution)/shard_map/ppermute | solution.py:90
  73.9 5.8 %collective-permute-start.21 = (bf16[4,16384]{1,0:T(4,128)(2,1)S(1)}, bf16[4,16384]{1,0:T(4,128)(2,1)S(1)}, u32[]{:S(2)}, u32[]{:S(2)}) collective-permute-start(bf16[4,16384]{1,0:T(4,128)(2,1)S(1)} %collective-permute-done.20.refs_7_), channel_id=1, source_target_pairs={{0,1},{1,0},{2,3},{3,2},{4,5},{5,4},{6,7},{7,6},{8,9},{9,8},{10,11... | collective-permute-start | bytes 393224 | tf_op jit(solution)/shard_map/ppermute | solution.py:90
  73.9 5.8 %collective-permute-start.19 = (bf16[4,16384]{1,0:T(4,128)(2,1)S(1)}, bf16[4,16384]{1,0:T(4,128)(2,1)S(1)}, u32[]{:S(2)}, u32[]{:S(2)}) collective-permute-start(bf16[4,16384]{1,0:T(4,128)(2,1)S(1)} %collective-permute-done.18.refs_5_), channel_id=1, source_target_pairs={{0,1},{1,0},{2,3},{3,2},{4,5},{5,4},{6,7},{7,6},{8,9},{9,8},{10,11... | collective-permute-start | bytes 393224 | tf_op jit(solution)/shard_map/ppermute | solution.py:90
  74.4 5.3 %collective-permute-start.17 = (bf16[4,16384]{1,0:T(4,128)(2,1)S(1)}, bf16[4,16384]{1,0:T(4,128)(2,1)S(1)}, u32[]{:S(2)}, u32[]{:S(2)}) collective-permute-start(bf16[4,16384]{1,0:T(4,128)(2,1)S(1)} %collective-permute-done.16.refs_3_), channel_id=1, source_target_pairs={{0,1},{1,0},{2,3},{3,2},{4,5},{5,4},{6,7},{7,6},{8,9},{9,8},{10,11... | collective-permute-start | bytes 393224 | tf_op jit(solution)/shard_map/ppermute | solution.py:90
  78.3 1.4 %collective-permute-start.25 = (bf16[4,16384]{1,0:T(4,128)(2,1)S(1)}, bf16[4,16384]{1,0:T(4,128)(2,1)S(1)}, u32[]{:S(2)}, u32[]{:S(2)}) collective-permute-start(bf16[4,16384]{1,0:T(4,128)(2,1)S(1)} %collective-permute-done.24.refs_11_), channel_id=1, source_target_pairs={{0,1},{1,0},{2,3},{3,2},{4,5},{5,4},{6,7},{7,6},{8,9},{9,8},{10,11... | collective-permute-start | bytes 393224 | tf_op jit(solution)/shard_map/ppermute | solution.py:90
  79.7 1.3 %collective-permute-start.29 = (bf16[4,16384]{1,0:T(4,128)(2,1)S(1)}, bf16[4,16384]{1,0:T(4,128)(2,1)S(1)}, u32[]{:S(2)}, u32[]{:S(2)}) collective-permute-start(bf16[4,16384]{1,0:T(4,128)(2,1)S(1)} %collective-permute-done.28.refs_15_), channel_id=1, source_target_pairs={{0,1},{1,0},{2,3},{3,2},{4,5},{5,4},{6,7},{7,6},{8,9},{9,8},{10,11... | collective-permute-start | bytes 393224 | tf_op jit(solution)/shard_map/ppermute | solution.py:90

commit v4 on v3

--- a/solution.py
+++ b/solution.py
@@ -135,7 +135,7 @@
 
 
 def load(arrays, rows, firsts, *behind):
-    parts = 2
+    parts = 2 if all(r % 2 == 0 for r in rows) else 1
     count = len(arrays)
     shapes = [(r, *a.shape[1:]) for a, r in zip(arrays, rows)]
     size = sum(2 * math.prod(shape) for shape in shapes)
@@ -145,7 +145,7 @@
             *(pltpu.VMEM(shape, a.dtype) for shape, a in zip(shapes, arrays)),
             jax.ShapeDtypeStruct((1,), jnp.int32),
         ),
-        in_specs=[IN_HBM] * count + [IN_SMEM] * len(behind),
+        in_specs=[IN_HBM] * count + [pl.BlockSpec(memory_space=pl.ANY)] * len(behind),
         out_specs=(IN_VMEM,) * count + (IN_SMEM,),
         scratch_shapes=[pltpu.SemaphoreType.DMA((count, parts))],
         cost_estimate=pl.CostEstimate(flops=0, bytes_accessed=int(size * 1.0), transcendentals=0),
@@ -275,21 +275,33 @@
 
 
 def attend_kernel(
-    lengths_ref, query_ref, fresh_ref, cos_ref, sin_ref, key_hbm, value_hbm, out_ref, key_ref, value_ref, sems
+    lengths_ref,
+    query_ref,
+    fresh_ref,
+    cos_ref,
+    sin_ref,
+    first_key_ref,
+    first_value_ref,
+    key_hbm,
+    value_hbm,
+    out_ref,
+    key_ref,
+    value_ref,
+    sems,
 ):
     requests, heads, depth = query_ref.shape
-    groups, cache = key_ref.shape[1], key_ref.shape[2]
+    groups = key_ref.shape[1]
     per_group = heads // groups
     scaling = 1.0 / math.sqrt(depth)
     copies = []
-    for r in range(requests):
+    for r in range(1, requests):
         copies.append(
             (
-                pltpu.make_async_copy(key_hbm.at[r], key_ref.at[r], sems.at[r, 0]),
-                pltpu.make_async_copy(value_hbm.at[r], value_ref.at[r], sems.at[r, 1]),
+                pltpu.make_async_copy(key_hbm.at[r], key_ref.at[r - 1], sems.at[r - 1, 0]),
+                pltpu.make_async_copy(value_hbm.at[r], value_ref.at[r - 1], sems.at[r - 1, 1]),
             )
         )
-    for pair in copies[:2]:
+    for pair in copies:
         for copy in pair:
             copy.start()
 
@@ -313,12 +325,16 @@
         own = (
             jnp.sum(query.astype(jnp.float32) * spread(fresh_key), axis=1, keepdims=True) * scaling
         )
-        copies[r][0].wait()
+        if r > 0:
+            copies[r - 1][0].wait()
+            keys = key_ref.at[r - 1]
+        else:
+            keys = first_key_ref.at[0]
         scores = jnp.concatenate(
             [
                 lax.dot_general(
                     query[g * per_group : (g + 1) * per_group],
-                    key_ref[r, g],
+                    keys[g],
                     (((1,), (1,)), ((), ())),
                     preferred_element_type=jnp.float32,
                 )
@@ -334,15 +350,16 @@
         inverse = 1.0 / (jnp.sum(weights, axis=1, keepdims=True) + own_weight)
         probs = (weights * inverse).astype(jnp.bfloat16)
         own_prob = (own_weight * inverse).astype(jnp.bfloat16).astype(jnp.float32)
-        copies[r][1].wait()
-        if r + 2 < requests:
-            for copy in copies[r + 2]:
-                copy.start()
+        if r > 0:
+            copies[r - 1][1].wait()
+            values = value_ref.at[r - 1]
+        else:
+            values = first_value_ref.at[0]
         mixed = jnp.concatenate(
             [
                 jnp.dot(
                     probs[g * per_group : (g + 1) * per_group],
-                    value_ref[r, g],
+                    values[g],
                     preferred_element_type=jnp.float32,
                 )
                 for g in range(groups)
@@ -352,7 +369,7 @@
         out_ref[r] = (mixed + own_prob * spread(fresh_value)).astype(out_ref.dtype)
 
 
-def attend(arrived, query_cols, keys, values, lengths):
+def attend(arrived, query_cols, keys, values, first_key, first_value, lengths):
     size, requests, _ = arrived.shape
     depth = HEAD_DIM
     query = arrived[..., :query_cols].reshape(size, requests, -1, depth)
@@ -366,12 +383,12 @@
     attended = pl.pallas_call(
         attend_kernel,
         out_shape=jax.ShapeDtypeStruct(query.shape, jnp.bfloat16),
-        in_specs=[IN_SMEM] + [IN_VMEM] * 4 + [IN_HBM] * 2,
+        in_specs=[IN_SMEM] + [IN_VMEM] * 6 + [IN_HBM] * 2,
         out_specs=IN_VMEM,
         scratch_shapes=[
-            pltpu.VMEM(keys.shape, keys.dtype),
-            pltpu.VMEM(values.shape, values.dtype),
-            pltpu.SemaphoreType.DMA((requests, 2)),
+            pltpu.VMEM((requests - 1, *keys.shape[1:]), keys.dtype),
+            pltpu.VMEM((requests - 1, *values.shape[1:]), values.dtype),
+            pltpu.SemaphoreType.DMA((requests - 1, 2)),
         ],
         compiler_params=pltpu.CompilerParams(vmem_limit_bytes=14 * MIB),
         name="attend",
@@ -381,6 +398,8 @@
         fresh,
         jnp.concatenate([cosine, cosine], axis=1),
         jnp.concatenate([-sine, sine], axis=1),
+        near(first_key),
+        near(first_value),
         far(keys),
         far(values),
     )
@@ -405,7 +424,10 @@
             axis=1,
         ).astype(jnp.bfloat16).reshape(size, normed.shape[0], -1)
     arrived = lax.all_to_all(projected, "mp", split_axis=0, concat_axis=0, tiled=True)
-    attended = attend(arrived, query_cols, key_cache, value_cache, after(lengths, projected))
+    first_key, first_value, _ = load([key_cache, value_cache], [1, 1], [0, 0], projected)
+    attended = attend(
+        arrived, query_cols, key_cache, value_cache, first_key, first_value, after(lengths, projected)
+    )
     if by_swaps:
         return gather_product(me, attended, size, [o_weight], OUT_LOADED, True)
     everyone = lax.all_gather(attended, "mp", axis=0, tiled=True)

time: 88.6 us -> 87.4 us (0.986)
  waiting for transfers between devices: 23.8 us -> 21.8 us
  Pallas kernels: 36.7 us -> 37.6 us
    all_to_all x1, waiting for transfers between devices: 7.98 us -> 5.9 us  [shards(): lax.all_to_all(projected, 'mp', split_axis=0, concat_axis=0, tiled=True)]
    pallas_call x2 -> x3, Pallas kernels: 13.8 us -> 15.9 us  [load(): pl.pallas_call(functools.partial(load_kernel, count, parts, firsts), out_...]
    pallas_call x1, Pallas kernels: 5.45 us -> 4.31 us  [attend(): pl.pallas_call(attend_kernel, out_shape=jax.ShapeDtypeStruct(query.shape,...]
  transfers between devices with their start and end apart: 31 -> 31, of which waited for: 10 -> 10; matrix products, arithmetic and copies ran while one was open for 0% -> 0% of each run, Pallas kernels for 16% -> 18%
where the time goes in v4:
time: 87.4 us; the launch traced here: 87.2 us
  Pallas kernels  37.6 us (43%)
  starting transfers between devices  27 us (31%)
  waiting for transfers between devices  21.8 us (25%)
    ppermute x30, starting transfers between devices, swap(): return lax.ppermute(block, 'mp', [(i, i ^ distance) for i in range(size)])  21 us
    pallas_call x2, Pallas kernels, product_part(): pl.pallas_call(functools.partial(product_kernel, plan), out_shape=tuple(o...  16.2 us
    pallas_call x3, Pallas kernels, load(): pl.pallas_call(functools.partial(load_kernel, count, parts, firsts), out_...  15.9 us
    ppermute x30, waiting for transfers between devices, swap(): return lax.ppermute(block, 'mp', [(i, i ^ distance) for i in range(size)])  15.9 us
    all_to_all x1, starting transfers between devices, shards(): lax.all_to_all(projected, 'mp', split_axis=0, concat_axis=0, tiled=True)  5.99 us
    all_to_all x1, waiting for transfers between devices, shards(): lax.all_to_all(projected, 'mp', split_axis=0, concat_axis=0, tiled=True)  5.9 us
    pallas_call x1, Pallas kernels, attend(): pl.pallas_call(attend_kernel, out_shape=jax.ShapeDtypeStruct(query.shape,...  4.31 us
  transfers between devices with their start and end apart: 31, of which 10 were waited for; matrix products, arithmetic and copies ran while one was open for 0% of the time, Pallas kernels for 18%

profile of v4, /device:TPU:0, one launch (start us, length us, event | category | flops | bytes accessed | tf_op | source)
XLA Modules:
  0.0 87.2 jit_solution(902340699919831554)
XLA Ops:
  0.0 1.2 %norm.1.refs_1_ = bf16[4,16384]{1,0:T(4,128)(2,1)S(1)} custom-call(bf16[4,16384]{1,0:T(4,128)(2,1)} %x_hbm.1, bf16[128,128]{1,0:T(8,128)(2,1)} %bitcast.24), custom_call_target="tpu_custom_call" | custom-call | tf_op jit(solution)/shard_map/norm/pallas_call | solution.py:74
  1.2 5.1 %collective-permute-start.11 = (bf16[4,16384]{1,0:T(4,128)(2,1)S(1)}, bf16[4,16384]{1,0:T(4,128)(2,1)S(1)}, u32[]{:S(2)}, u32[]{:S(2)}) collective-permute-start(bf16[4,16384]{1,0:T(4,128)(2,1)S(1)} %norm.1.refs_1_), channel_id=1, source_target_pairs={{0,12},{1,13},{2,14},{3,15},{4,8},{5,9},{6,10},{7,11},{8,4},{9,5},... | collective-permute-start | bytes 393224 | tf_op jit(solution)/shard_map/ppermute | solution.py:90
  6.3 0.0 collective-permute-start.7
  6.3 1.7 %collective-permute-start.5 = (bf16[4,16384]{1,0:T(4,128)(2,1)S(1)}, bf16[4,16384]{1,0:T(4,128)(2,1)S(1)}, u32[]{:S(2)}, u32[]{:S(2)}) collective-permute-start(bf16[4,16384]{1,0:T(4,128)(2,1)S(1)} %norm.1.refs_1_), channel_id=1, source_target_pairs={{0,6},{1,7},{2,4},{3,5},{4,2},{5,3},{6,0},{7,1},{8,14},{9,15},{10,... | collective-permute-start | bytes 393224 | tf_op jit(solution)/shard_map/ppermute | solution.py:90
  8.1 1.2 %collective-permute-start.3 = (bf16[4,16384]{1,0:T(4,128)(2,1)S(1)}, bf16[4,16384]{1,0:T(4,128)(2,1)S(1)}, u32[]{:S(2)}, u32[]{:S(2)}) collective-permute-start(bf16[4,16384]{1,0:T(4,128)(2,1)S(1)} %norm.1.refs_1_), channel_id=1, source_target_pairs={{0,4},{1,5},{2,6},{3,7},{4,0},{5,1},{6,2},{7,3},{8,12},{9,13},{10,... | collective-permute-start | bytes 393224 | tf_op jit(solution)/shard_map/ppermute | solution.py:90
  9.3 0.5 collective-permute-start.1
  9.8 6.3 %load.3 = (bf16[8192,1024]{1,0:T(8,128)(2,1)S(1)}, s32[1]{0:T(128)}) custom-call(bf16[16384,1024]{1,0:T(8,128)(2,1)} %refs_18_.2, s32[1]{0:T(128)} %bitcast.refs_1_.refs_0_), custom_call_target="tpu_custom_call" | custom-call | bytes 16777216 | tf_op jit(solution)/shard_map/load/pallas_call | solution.py:142
  16.1 0.1 collective-permute-start
  16.2 1.3 %collective-permute-done.7.refs_9_ = bf16[4,16384]{1,0:T(4,128)(2,1)S(1)} collective-permute-done((bf16[4,16384]{1,0:T(4,128)(2,1)S(1)}, bf16[4,16384]{1,0:T(4,128)(2,1)S(1)}, u32[]{:S(2)}, u32[]{:S(2)}) %collective-permute-start.7) | collective-permute-done | bytes 131104 | tf_op jit(solution)/shard_map/ppermute | solution.py:90
  17.5 0.0 collective-permute-start.12
  17.5 0.0 collective-permute-done.5.refs_7_
  17.5 0.5 collective-permute-start.8
  18.0 0.5 collective-permute-done.3.refs_5_
  18.6 1.4 %collective-permute-start.9 = (bf16[4,16384]{1,0:T(4,128)(2,1)S(1)}, bf16[4,16384]{1,0:T(4,128)(2,1)S(1)}, u32[]{:S(2)}, u32[]{:S(2)}) collective-permute-start(bf16[4,16384]{1,0:T(4,128)(2,1)S(1)} %collective-permute-done.7.refs_9_), channel_id=1, source_target_pairs={{0,2},{1,3},{2,0},{3,1},{4,6},{5,7},{6,4},{7,5},{8,10},{9,11},{10,... | collective-permute-start | bytes 393224 | tf_op jit(solution)/shard_map/ppermute | solution.py:90
  19.9 0.0 collective-permute-done.1.refs_3_
  19.9 0.7 collective-permute-start.13
  20.6 0.0 collective-permute-done.refs_2_
  20.6 0.0 collective-permute-start.6
  20.6 0.0 collective-permute-done.12.refs_14_
  20.6 0.5 collective-permute-start.4
  21.1 0.0 collective-permute-done.8.refs_10_
  21.1 0.1 collective-permute-start.2
  21.2 3.7 %collective-permute-done.9.refs_11_ = bf16[4,16384]{1,0:T(4,128)(2,1)S(1)} collective-permute-done((bf16[4,16384]{1,0:T(4,128)(2,1)S(1)}, bf16[4,16384]{1,0:T(4,128)(2,1)S(1)}, u32[]{:S(2)}, u32[]{:S(2)}) %collective-permute-start.9) | collective-permute-done | bytes 131104 | tf_op jit(solution)/shard_map/ppermute | solution.py:90
  24.9 0.0 collective-permute-start.10
  24.9 1.4 %collective-permute-done.13.refs_15_ = bf16[4,16384]{1,0:T(4,128)(2,1)S(1)} collective-permute-done((bf16[4,16384]{1,0:T(4,128)(2,1)S(1)}, bf16[4,16384]{1,0:T(4,128)(2,1)S(1)}, u32[]{:S(2)}, u32[]{:S(2)}) %collective-permute-start.13) | collective-permute-done | bytes 131104 | tf_op jit(solution)/shard_map/ppermute | solution.py:90
  26.4 0.0 collective-permute-done.2.refs_4_
  26.4 0.0 collective-permute-done.10.refs_12_
  26.4 1.3 %collective-permute-done.14.refs_16_ = bf16[4,16384]{1,0:T(4,128)(2,1)S(1)} collective-permute-done((bf16[4,16384]{1,0:T(4,128)(2,1)S(1)}, bf16[4,16384]{1,0:T(4,128)(2,1)S(1)}, u32[]{:S(2)}, u32[]{:S(2)}) %collective-permute-start.14) | collective-permute-done | bytes 131104 | tf_op jit(solution)/shard_map/ppermute | solution.py:90
  27.7 9.1 %product.2.refs_2_ = bf16[16,4,1152]{2,1,0:T(4,128)(2,1)} custom-call(s32[1]{0:T(128)} %bitcast.refs_1_.refs_0_, bf16[4,16384]{1,0:T(4,128)(2,1)S(1)} %norm.1.refs_1_, bf16[4,16384]{1,0:T(4,128)(2,1)S(1)} %collective-permute-done.refs_2_, bf16[4,16384]{1,0:T(4,128)(2,1)S(1)} %collective-permute-done.1.refs_3_, ...), custom_call_target="tpu_custom_call" | custom-call | flops 2415919104 | bytes 37748736 | tf_op jit(solution)/shard_map/product/pallas_call | solution.py:254
  36.8 6.0 %all-to-all-start = ((bf16[16,4,1152]{2,1,0:T(4,128)(2,1)}), bf16[16,4,1152]{2,1,0:T(4,128)(2,1)S(1)}, u32[]{:S(2)}, u32[]{:S(2)}) async-start(bf16[16,4,1152]{2,1,0:T(4,128)(2,1)} %product.2.refs_2_), calls=%async_computation | async-start | bytes 294912 | tf_op jit(solution)/shard_map/all_to_all | solution.py:426
  42.8 2.1 %load.4 = (bf16[1,8,512,128]{3,2,1,0:T(8,128)(2,1)S(1)}, bf16[1,8,512,128]{3,2,1,0:T(8,128)(2,1)S(1)}, s32[1]{0:T(128)}) custom-call(bf16[4,8,512,128]{3,2,1,0:T(8,128)(2,1)} %key_hbm.1, bf16[4,8,512,128]{3,2,1,0:T(8,128)(2,1)} %value_hbm.1, bf16[16,4,1152]{2,1,0:T(4,128)(2,1)} %product.2.refs_2_), custom_call_target="tpu_custom_call" | custom-call | bytes 2097152 | tf_op jit(solution)/shard_map/load/pallas_call | solution.py:142
  44.9 0.1 fusion
  45.0 0.1 pad_maximum_fusion
  45.1 5.9 %all-to-all-done = bf16[16,4,1152]{2,1,0:T(4,128)(2,1)S(1)} async-done(((bf16[16,4,1152]{2,1,0:T(4,128)(2,1)}), bf16[16,4,1152]{2,1,0:T(4,128)(2,1)S(1)}, u32[]{:S(2)}, u32[]{:S(2)}) %all-to-all-start) | async-done | bytes 147488 | tf_op jit(solution)/shard_map/all_to_all | solution.py:426
  51.0 0.1 reshape.23
  51.1 4.3 %attend.1 = bf16[4,128,128]{2,1,0:T(8,128)(2,1)S(1)} custom-call(s32[4]{0:T(128)S(1)} %copy-done, bf16[4,128,128]{2,1,0:T(8,128)(2,1)S(1)} %bitcast.21, bf16[4,16,128]{2,1,0:T(8,128)(2,1)S(1)} %bitcast.23, f32[4,128]{1,0:T(4,128)S(1)} %get-tuple-element.30.cos_ref, f32[4,128]{1,0:T(4,128)S(1)} %get-tuple-element.31.sin_ref, ...), custom_call_target="tpu_custom_call" | custom-call | tf_op jit(solution)/shard_map/attend/pallas_call | solution.py:383
  55.4 0.1 copy.17
  55.6 0.8 collective-permute-start.26
  56.4 0.0 collective-permute-start.22
  56.4 2.3 %collective-permute-start.20 = (bf16[4,16384]{1,0:T(4,128)(2,1)S(1)}, bf16[4,16384]{1,0:T(4,128)(2,1)S(1)}, u32[]{:S(2)}, u32[]{:S(2)}) collective-permute-start(bf16[4,16384]{1,0:T(4,128)(2,1)S(1)} %bitcast.16), channel_id=1, source_target_pairs={{0,6},{1,7},{2,4},{3,5},{4,2},{5,3},{6,0},{7,1},{8,14},{9,15},{10,... | collective-permute-start | bytes 393224 | tf_op jit(solution)/shard_map/ppermute | solution.py:90
  58.7 1.3 %collective-permute-start.18 = (bf16[4,16384]{1,0:T(4,128)(2,1)S(1)}, bf16[4,16384]{1,0:T(4,128)(2,1)S(1)}, u32[]{:S(2)}, u32[]{:S(2)}) collective-permute-start(bf16[4,16384]{1,0:T(4,128)(2,1)S(1)} %bitcast.17), channel_id=1, source_target_pairs={{0,4},{1,5},{2,6},{3,7},{4,0},{5,1},{6,2},{7,3},{8,12},{9,13},{10,... | collective-permute-start | bytes 393224 | tf_op jit(solution)/shard_map/ppermute | solution.py:90
  60.0 1.5 %collective-permute-start.16 = (bf16[4,16384]{1,0:T(4,128)(2,1)S(1)}, bf16[4,16384]{1,0:T(4,128)(2,1)S(1)}, u32[]{:S(2)}, u32[]{:S(2)}) collective-permute-start(bf16[4,16384]{1,0:T(4,128)(2,1)S(1)} %bitcast.18), channel_id=1, source_target_pairs={{0,2},{1,3},{2,0},{3,1},{4,6},{5,7},{6,4},{7,5},{8,10},{9,11},{10,... | collective-permute-start | bytes 393224 | tf_op jit(solution)/shard_map/ppermute | solution.py:90
  61.5 7.5 %load.5 = (bf16[10240,1024]{1,0:T(8,128)(2,1)S(1)}, s32[1]{0:T(128)}) custom-call(bf16[16384,1024]{1,0:T(8,128)(2,1)} %refs_18_.3, s32[1]{0:T(128)} %bitcast.refs_1_.refs_0_), custom_call_target="tpu_custom_call" | custom-call | bytes 20971520 | tf_op jit(solution)/shard_map/load/pallas_call | solution.py:142
  69.0 0.0 collective-permute-done.26.refs_13_
  69.0 0.1 collective-permute-start.15
  69.1 0.5 collective-permute-start.27
  69.6 0.1 collective-permute-start.23
  69.7 1.1 %collective-permute-done.18.refs_5_ = bf16[4,16384]{1,0:T(4,128)(2,1)S(1)} collective-permute-done((bf16[4,16384]{1,0:T(4,128)(2,1)S(1)}, bf16[4,16384]{1,0:T(4,128)(2,1)S(1)}, u32[]{:S(2)}, u32[]{:S(2)}) %collective-permute-start.18) | collective-permute-done | bytes 131104 | tf_op jit(solution)/shard_map/ppermute | solution.py:90
  70.7 0.7 collective-permute-start.24
  71.4 0.0 collective-permute-done.16.refs_3_
  71.4 1.4 %collective-permute-start.28 = (bf16[4,16384]{1,0:T(4,128)(2,1)S(1)}, bf16[4,16384]{1,0:T(4,128)(2,1)S(1)}, u32[]{:S(2)}, u32[]{:S(2)}) collective-permute-start(bf16[4,16384]{1,0:T(4,128)(2,1)S(1)} %collective-permute-done.26.refs_13_), channel_id=1, source_target_pairs={{0,2},{1,3},{2,0},{3,1},{4,6},{5,7},{6,4},{7,5},{8,10},{9,11},{10,... | collective-permute-start | bytes 393224 | tf_op jit(solution)/shard_map/ppermute | solution.py:90
  72.8 0.0 collective-permute-done.27.refs_14_
  72.8 0.5 collective-permute-start.19
  73.3 0.1 collective-permute-start.17
  73.3 3.8 %collective-permute-done.24.refs_11_ = bf16[4,16384]{1,0:T(4,128)(2,1)S(1)} collective-permute-done((bf16[4,16384]{1,0:T(4,128)(2,1)S(1)}, bf16[4,16384]{1,0:T(4,128)(2,1)S(1)}, u32[]{:S(2)}, u32[]{:S(2)}) %collective-permute-start.24) | collective-permute-done | bytes 131104 | tf_op jit(solution)/shard_map/ppermute | solution.py:90
  77.1 0.0 collective-permute-start.25
  77.1 1.4 %collective-permute-done.28.refs_15_ = bf16[4,16384]{1,0:T(4,128)(2,1)S(1)} collective-permute-done((bf16[4,16384]{1,0:T(4,128)(2,1)S(1)}, bf16[4,16384]{1,0:T(4,128)(2,1)S(1)}, u32[]{:S(2)}, u32[]{:S(2)}) %collective-permute-start.28) | collective-permute-done | bytes 131104 | tf_op jit(solution)/shard_map/ppermute | solution.py:90
  78.5 0.0 collective-permute-start.29
  78.5 0.0 collective-permute-done.21.refs_8_
  78.5 0.0 collective-permute-done.19.refs_6_
  78.5 0.0 collective-permute-done.17.refs_4_
  78.6 0.0 collective-permute-done.25.refs_12_
  78.6 1.3 %collective-permute-done.29.refs_16_ = bf16[4,16384]{1,0:T(4,128)(2,1)S(1)} collective-permute-done((bf16[4,16384]{1,0:T(4,128)(2,1)S(1)}, bf16[4,16384]{1,0:T(4,128)(2,1)S(1)}, u32[]{:S(2)}, u32[]{:S(2)}) %collective-permute-start.29) | collective-permute-done | bytes 131104 | tf_op jit(solution)/shard_map/ppermute | solution.py:90
  79.9 7.1 %product.3 = bf16[64,1024]{1,0:T(8,128)(2,1)} custom-call(s32[1]{0:T(128)} %bitcast.refs_1_.refs_0_, bf16[4,16384]{1,0:T(4,128)(2,1)S(1)} %bitcast.20, bf16[4,16384]{1,0:T(4,128)(2,1)S(1)} %collective-permute-done.15.refs_2_, bf16[4,16384]{1,0:T(4,128)(2,1)S(1)} %collective-permute-done.16.refs_3_, bf16[4,16384]{1,0:T(4,128)(2,1)S(1)} %collective-permute-done.17.refs_4_, ...), custom_call_target="tpu_custom_call" | custom-call | flops 2147483648 | bytes 33554432 | tf_op jit(solution)/shard_map/product/pallas_call | solution.py:254
  (17 shorter events, 0.1 us)
Async XLA Ops:
  1.2 14.9 %collective-permute-start.11 = (bf16[4,16384]{1,0:T(4,128)(2,1)S(1)}, bf16[4,16384]{1,0:T(4,128)(2,1)S(1)}, u32[]{:S(2)}, u32[]{:S(2)}) collective-permute-start(bf16[4,16384]{1,0:T(4,128)(2,1)S(1)} %norm.1.refs_1_), channel_id=1, source_target_pairs={{0,12},{1,13},{2,14},{3,15},{4,8},{5,9},{6,10},{7,11},{8,4},{9,5},... | collective-permute-start | bytes 393224 | tf_op jit(solution)/shard_map/ppermute | solution.py:90
  6.3 11.2 %collective-permute-start.7 = (bf16[4,16384]{1,0:T(4,128)(2,1)S(1)}, bf16[4,16384]{1,0:T(4,128)(2,1)S(1)}, u32[]{:S(2)}, u32[]{:S(2)}) collective-permute-start(bf16[4,16384]{1,0:T(4,128)(2,1)S(1)} %norm.1.refs_1_), channel_id=1, source_target_pairs={{0,8},{1,9},{2,10},{3,11},{4,12},{5,13},{6,14},{7,15},{8,0},{9,1},... | collective-permute-start | bytes 393224 | tf_op jit(solution)/shard_map/ppermute | solution.py:90
  6.3 11.2 %collective-permute-start.5 = (bf16[4,16384]{1,0:T(4,128)(2,1)S(1)}, bf16[4,16384]{1,0:T(4,128)(2,1)S(1)}, u32[]{:S(2)}, u32[]{:S(2)}) collective-permute-start(bf16[4,16384]{1,0:T(4,128)(2,1)S(1)} %norm.1.refs_1_), channel_id=1, source_target_pairs={{0,6},{1,7},{2,4},{3,5},{4,2},{5,3},{6,0},{7,1},{8,14},{9,15},{10,... | collective-permute-start | bytes 393224 | tf_op jit(solution)/shard_map/ppermute | solution.py:90
  8.1 10.5 %collective-permute-start.3 = (bf16[4,16384]{1,0:T(4,128)(2,1)S(1)}, bf16[4,16384]{1,0:T(4,128)(2,1)S(1)}, u32[]{:S(2)}, u32[]{:S(2)}) collective-permute-start(bf16[4,16384]{1,0:T(4,128)(2,1)S(1)} %norm.1.refs_1_), channel_id=1, source_target_pairs={{0,4},{1,5},{2,6},{3,7},{4,0},{5,1},{6,2},{7,3},{8,12},{9,13},{10,... | collective-permute-start | bytes 393224 | tf_op jit(solution)/shard_map/ppermute | solution.py:90
  9.3 10.6 %collective-permute-start.1 = (bf16[4,16384]{1,0:T(4,128)(2,1)S(1)}, bf16[4,16384]{1,0:T(4,128)(2,1)S(1)}, u32[]{:S(2)}, u32[]{:S(2)}) collective-permute-start(bf16[4,16384]{1,0:T(4,128)(2,1)S(1)} %norm.1.refs_1_), channel_id=1, source_target_pairs={{0,2},{1,3},{2,0},{3,1},{4,6},{5,7},{6,4},{7,5},{8,10},{9,11},{10,... | collective-permute-start | bytes 393224 | tf_op jit(solution)/shard_map/ppermute | solution.py:90
  16.1 4.5 %collective-permute-start = (bf16[4,16384]{1,0:T(4,128)(2,1)S(1)}, bf16[4,16384]{1,0:T(4,128)(2,1)S(1)}, u32[]{:S(2)}, u32[]{:S(2)}) collective-permute-start(bf16[4,16384]{1,0:T(4,128)(2,1)S(1)} %norm.1.refs_1_), channel_id=1, source_target_pairs={{0,1},{1,0},{2,3},{3,2},{4,5},{5,4},{6,7},{7,6},{8,9},{9,8},{10,11... | collective-permute-start | bytes 393224 | tf_op jit(solution)/shard_map/ppermute | solution.py:90
  17.5 3.1 %collective-permute-start.12 = (bf16[4,16384]{1,0:T(4,128)(2,1)S(1)}, bf16[4,16384]{1,0:T(4,128)(2,1)S(1)}, u32[]{:S(2)}, u32[]{:S(2)}) collective-permute-start(bf16[4,16384]{1,0:T(4,128)(2,1)S(1)} %collective-permute-done.11.refs_13_), channel_id=1, source_target_pairs={{0,1},{1,0},{2,3},{3,2},{4,5},{5,4},{6,7},{7,6},{8,9},{9,8},{10,11... | collective-permute-start | bytes 393224 | tf_op jit(solution)/shard_map/ppermute | solution.py:90
  17.5 3.6 %collective-permute-start.8 = (bf16[4,16384]{1,0:T(4,128)(2,1)S(1)}, bf16[4,16384]{1,0:T(4,128)(2,1)S(1)}, u32[]{:S(2)}, u32[]{:S(2)}) collective-permute-start(bf16[4,16384]{1,0:T(4,128)(2,1)S(1)} %collective-permute-done.7.refs_9_), channel_id=1, source_target_pairs={{0,1},{1,0},{2,3},{3,2},{4,5},{5,4},{6,7},{7,6},{8,9},{9,8},{10,11... | collective-permute-start | bytes 393224 | tf_op jit(solution)/shard_map/ppermute | solution.py:90
  18.6 6.3 %collective-permute-start.9 = (bf16[4,16384]{1,0:T(4,128)(2,1)S(1)}, bf16[4,16384]{1,0:T(4,128)(2,1)S(1)}, u32[]{:S(2)}, u32[]{:S(2)}) collective-permute-start(bf16[4,16384]{1,0:T(4,128)(2,1)S(1)} %collective-permute-done.7.refs_9_), channel_id=1, source_target_pairs={{0,2},{1,3},{2,0},{3,1},{4,6},{5,7},{6,4},{7,5},{8,10},{9,11},{10,... | collective-permute-start | bytes 393224 | tf_op jit(solution)/shard_map/ppermute | solution.py:90
  19.9 6.4 %collective-permute-start.13 = (bf16[4,16384]{1,0:T(4,128)(2,1)S(1)}, bf16[4,16384]{1,0:T(4,128)(2,1)S(1)}, u32[]{:S(2)}, u32[]{:S(2)}) collective-permute-start(bf16[4,16384]{1,0:T(4,128)(2,1)S(1)} %collective-permute-done.11.refs_13_), channel_id=1, source_target_pairs={{0,2},{1,3},{2,0},{3,1},{4,6},{5,7},{6,4},{7,5},{8,10},{9,11},{10,... | collective-permute-start | bytes 393224 | tf_op jit(solution)/shard_map/ppermute | solution.py:90
  20.6 5.7 %collective-permute-start.6 = (bf16[4,16384]{1,0:T(4,128)(2,1)S(1)}, bf16[4,16384]{1,0:T(4,128)(2,1)S(1)}, u32[]{:S(2)}, u32[]{:S(2)}) collective-permute-start(bf16[4,16384]{1,0:T(4,128)(2,1)S(1)} %collective-permute-done.5.refs_7_), channel_id=1, source_target_pairs={{0,1},{1,0},{2,3},{3,2},{4,5},{5,4},{6,7},{7,6},{8,9},{9,8},{10,11... | collective-permute-start | bytes 393224 | tf_op jit(solution)/shard_map/ppermute | solution.py:90
  20.6 5.7 %collective-permute-start.4 = (bf16[4,16384]{1,0:T(4,128)(2,1)S(1)}, bf16[4,16384]{1,0:T(4,128)(2,1)S(1)}, u32[]{:S(2)}, u32[]{:S(2)}) collective-permute-start(bf16[4,16384]{1,0:T(4,128)(2,1)S(1)} %collective-permute-done.3.refs_5_), channel_id=1, source_target_pairs={{0,1},{1,0},{2,3},{3,2},{4,5},{5,4},{6,7},{7,6},{8,9},{9,8},{10,11... | collective-permute-start | bytes 393224 | tf_op jit(solution)/shard_map/ppermute | solution.py:90
  21.1 5.2 %collective-permute-start.2 = (bf16[4,16384]{1,0:T(4,128)(2,1)S(1)}, bf16[4,16384]{1,0:T(4,128)(2,1)S(1)}, u32[]{:S(2)}, u32[]{:S(2)}) collective-permute-start(bf16[4,16384]{1,0:T(4,128)(2,1)S(1)} %collective-permute-done.1.refs_3_), channel_id=1, source_target_pairs={{0,1},{1,0},{2,3},{3,2},{4,5},{5,4},{6,7},{7,6},{8,9},{9,8},{10,11... | collective-permute-start | bytes 393224 | tf_op jit(solution)/shard_map/ppermute | solution.py:90
  24.9 1.5 %collective-permute-start.10 = (bf16[4,16384]{1,0:T(4,128)(2,1)S(1)}, bf16[4,16384]{1,0:T(4,128)(2,1)S(1)}, u32[]{:S(2)}, u32[]{:S(2)}) collective-permute-start(bf16[4,16384]{1,0:T(4,128)(2,1)S(1)} %collective-permute-done.9.refs_11_), channel_id=1, source_target_pairs={{0,1},{1,0},{2,3},{3,2},{4,5},{5,4},{6,7},{7,6},{8,9},{9,8},{10,11... | collective-permute-start | bytes 393224 | tf_op jit(solution)/shard_map/ppermute | solution.py:90
  26.3 1.3 %collective-permute-start.14 = (bf16[4,16384]{1,0:T(4,128)(2,1)S(1)}, bf16[4,16384]{1,0:T(4,128)(2,1)S(1)}, u32[]{:S(2)}, u32[]{:S(2)}) collective-permute-start(bf16[4,16384]{1,0:T(4,128)(2,1)S(1)} %collective-permute-done.13.refs_15_), channel_id=1, source_target_pairs={{0,1},{1,0},{2,3},{3,2},{4,5},{5,4},{6,7},{7,6},{8,9},{9,8},{10,11... | collective-permute-start | bytes 393224 | tf_op jit(solution)/shard_map/ppermute | solution.py:90
  27.7 15.1 %copy-start = (s32[4]{0:T(128)S(1)}, s32[4]{0:T(128)}, u32[]{:S(2)}) copy-start(s32[4]{0:T(128)} %lengths_ref) | copy-start | bytes 52
  36.8 14.2 %all-to-all-start = ((bf16[16,4,1152]{2,1,0:T(4,128)(2,1)}), bf16[16,4,1152]{2,1,0:T(4,128)(2,1)S(1)}, u32[]{:S(2)}, u32[]{:S(2)}) async-start(bf16[16,4,1152]{2,1,0:T(4,128)(2,1)} %product.2.refs_2_), calls=%async_computation | async-start | bytes 294912 | tf_op jit(solution)/shard_map/all_to_all | solution.py:426
  55.6 13.4 %collective-permute-start.26 = (bf16[4,16384]{1,0:T(4,128)(2,1)S(1)}, bf16[4,16384]{1,0:T(4,128)(2,1)S(1)}, u32[]{:S(2)}, u32[]{:S(2)}) collective-permute-start(bf16[4,16384]{1,0:T(4,128)(2,1)S(1)} %bitcast.14), channel_id=1, source_target_pairs={{0,12},{1,13},{2,14},{3,15},{4,8},{5,9},{6,10},{7,11},{8,4},{9,5},... | collective-permute-start | bytes 393224 | tf_op jit(solution)/shard_map/ppermute | solution.py:90
  56.4 12.7 %collective-permute-start.22 = (bf16[4,16384]{1,0:T(4,128)(2,1)S(1)}, bf16[4,16384]{1,0:T(4,128)(2,1)S(1)}, u32[]{:S(2)}, u32[]{:S(2)}) collective-permute-start(bf16[4,16384]{1,0:T(4,128)(2,1)S(1)} %bitcast.15), channel_id=1, source_target_pairs={{0,8},{1,9},{2,10},{3,11},{4,12},{5,13},{6,14},{7,15},{8,0},{9,1},... | collective-permute-start | bytes 393224 | tf_op jit(solution)/shard_map/ppermute | solution.py:90
  56.4 13.1 %collective-permute-start.20 = (bf16[4,16384]{1,0:T(4,128)(2,1)S(1)}, bf16[4,16384]{1,0:T(4,128)(2,1)S(1)}, u32[]{:S(2)}, u32[]{:S(2)}) collective-permute-start(bf16[4,16384]{1,0:T(4,128)(2,1)S(1)} %bitcast.16), channel_id=1, source_target_pairs={{0,6},{1,7},{2,4},{3,5},{4,2},{5,3},{6,0},{7,1},{8,14},{9,15},{10,... | collective-permute-start | bytes 393224 | tf_op jit(solution)/shard_map/ppermute | solution.py:90
  58.7 12.0 %collective-permute-start.18 = (bf16[4,16384]{1,0:T(4,128)(2,1)S(1)}, bf16[4,16384]{1,0:T(4,128)(2,1)S(1)}, u32[]{:S(2)}, u32[]{:S(2)}) collective-permute-start(bf16[4,16384]{1,0:T(4,128)(2,1)S(1)} %bitcast.17), channel_id=1, source_target_pairs={{0,4},{1,5},{2,6},{3,7},{4,0},{5,1},{6,2},{7,3},{8,12},{9,13},{10,... | collective-permute-start | bytes 393224 | tf_op jit(solution)/shard_map/ppermute | solution.py:90
  60.0 11.4 %collective-permute-start.16 = (bf16[4,16384]{1,0:T(4,128)(2,1)S(1)}, bf16[4,16384]{1,0:T(4,128)(2,1)S(1)}, u32[]{:S(2)}, u32[]{:S(2)}) collective-permute-start(bf16[4,16384]{1,0:T(4,128)(2,1)S(1)} %bitcast.18), channel_id=1, source_target_pairs={{0,2},{1,3},{2,0},{3,1},{4,6},{5,7},{6,4},{7,5},{8,10},{9,11},{10,... | collective-permute-start | bytes 393224 | tf_op jit(solution)/shard_map/ppermute | solution.py:90
  69.0 3.8 %collective-permute-start.15 = (bf16[4,16384]{1,0:T(4,128)(2,1)S(1)}, bf16[4,16384]{1,0:T(4,128)(2,1)S(1)}, u32[]{:S(2)}, u32[]{:S(2)}) collective-permute-start(bf16[4,16384]{1,0:T(4,128)(2,1)S(1)} %bitcast.19), channel_id=1, source_target_pairs={{0,1},{1,0},{2,3},{3,2},{4,5},{5,4},{6,7},{7,6},{8,9},{9,8},{10,11... | collective-permute-start | bytes 393224 | tf_op jit(solution)/shard_map/ppermute | solution.py:90
  69.1 3.7 %collective-permute-start.27 = (bf16[4,16384]{1,0:T(4,128)(2,1)S(1)}, bf16[4,16384]{1,0:T(4,128)(2,1)S(1)}, u32[]{:S(2)}, u32[]{:S(2)}) collective-permute-start(bf16[4,16384]{1,0:T(4,128)(2,1)S(1)} %collective-permute-done.26.refs_13_), channel_id=1, source_target_pairs={{0,1},{1,0},{2,3},{3,2},{4,5},{5,4},{6,7},{7,6},{8,9},{9,8},{10,11... | collective-permute-start | bytes 393224 | tf_op jit(solution)/shard_map/ppermute | solution.py:90
  69.6 3.7 %collective-permute-start.23 = (bf16[4,16384]{1,0:T(4,128)(2,1)S(1)}, bf16[4,16384]{1,0:T(4,128)(2,1)S(1)}, u32[]{:S(2)}, u32[]{:S(2)}) collective-permute-start(bf16[4,16384]{1,0:T(4,128)(2,1)S(1)} %collective-permute-done.22.refs_9_), channel_id=1, source_target_pairs={{0,1},{1,0},{2,3},{3,2},{4,5},{5,4},{6,7},{7,6},{8,9},{9,8},{10,11... | collective-permute-start | bytes 393224 | tf_op jit(solution)/shard_map/ppermute | solution.py:90
  70.7 6.4 %collective-permute-start.24 = (bf16[4,16384]{1,0:T(4,128)(2,1)S(1)}, bf16[4,16384]{1,0:T(4,128)(2,1)S(1)}, u32[]{:S(2)}, u32[]{:S(2)}) collective-permute-start(bf16[4,16384]{1,0:T(4,128)(2,1)S(1)} %collective-permute-done.22.refs_9_), channel_id=1, source_target_pairs={{0,2},{1,3},{2,0},{3,1},{4,6},{5,7},{6,4},{7,5},{8,10},{9,11},{10,... | collective-permute-start | bytes 393224 | tf_op jit(solution)/shard_map/ppermute | solution.py:90
  71.4 7.1 %collective-permute-start.28 = (bf16[4,16384]{1,0:T(4,128)(2,1)S(1)}, bf16[4,16384]{1,0:T(4,128)(2,1)S(1)}, u32[]{:S(2)}, u32[]{:S(2)}) collective-permute-start(bf16[4,16384]{1,0:T(4,128)(2,1)S(1)} %collective-permute-done.26.refs_13_), channel_id=1, source_target_pairs={{0,2},{1,3},{2,0},{3,1},{4,6},{5,7},{6,4},{7,5},{8,10},{9,11},{10,... | collective-permute-start | bytes 393224 | tf_op jit(solution)/shard_map/ppermute | solution.py:90
  72.7 5.8 %collective-permute-start.21 = (bf16[4,16384]{1,0:T(4,128)(2,1)S(1)}, bf16[4,16384]{1,0:T(4,128)(2,1)S(1)}, u32[]{:S(2)}, u32[]{:S(2)}) collective-permute-start(bf16[4,16384]{1,0:T(4,128)(2,1)S(1)} %collective-permute-done.20.refs_7_), channel_id=1, source_target_pairs={{0,1},{1,0},{2,3},{3,2},{4,5},{5,4},{6,7},{7,6},{8,9},{9,8},{10,11... | collective-permute-start | bytes 393224 | tf_op jit(solution)/shard_map/ppermute | solution.py:90
  72.8 5.8 %collective-permute-start.19 = (bf16[4,16384]{1,0:T(4,128)(2,1)S(1)}, bf16[4,16384]{1,0:T(4,128)(2,1)S(1)}, u32[]{:S(2)}, u32[]{:S(2)}) collective-permute-start(bf16[4,16384]{1,0:T(4,128)(2,1)S(1)} %collective-permute-done.18.refs_5_), channel_id=1, source_target_pairs={{0,1},{1,0},{2,3},{3,2},{4,5},{5,4},{6,7},{7,6},{8,9},{9,8},{10,11... | collective-permute-start | bytes 393224 | tf_op jit(solution)/shard_map/ppermute | solution.py:90
  73.3 5.3 %collective-permute-start.17 = (bf16[4,16384]{1,0:T(4,128)(2,1)S(1)}, bf16[4,16384]{1,0:T(4,128)(2,1)S(1)}, u32[]{:S(2)}, u32[]{:S(2)}) collective-permute-start(bf16[4,16384]{1,0:T(4,128)(2,1)S(1)} %collective-permute-done.16.refs_3_), channel_id=1, source_target_pairs={{0,1},{1,0},{2,3},{3,2},{4,5},{5,4},{6,7},{7,6},{8,9},{9,8},{10,11... | collective-permute-start | bytes 393224 | tf_op jit(solution)/shard_map/ppermute | solution.py:90
  77.1 1.4 %collective-permute-start.25 = (bf16[4,16384]{1,0:T(4,128)(2,1)S(1)}, bf16[4,16384]{1,0:T(4,128)(2,1)S(1)}, u32[]{:S(2)}, u32[]{:S(2)}) collective-permute-start(bf16[4,16384]{1,0:T(4,128)(2,1)S(1)} %collective-permute-done.24.refs_11_), channel_id=1, source_target_pairs={{0,1},{1,0},{2,3},{3,2},{4,5},{5,4},{6,7},{7,6},{8,9},{9,8},{10,11... | collective-permute-start | bytes 393224 | tf_op jit(solution)/shard_map/ppermute | solution.py:90
  78.5 1.3 %collective-permute-start.29 = (bf16[4,16384]{1,0:T(4,128)(2,1)S(1)}, bf16[4,16384]{1,0:T(4,128)(2,1)S(1)}, u32[]{:S(2)}, u32[]{:S(2)}) collective-permute-start(bf16[4,16384]{1,0:T(4,128)(2,1)S(1)} %collective-permute-done.28.refs_15_), channel_id=1, source_target_pairs={{0,1},{1,0},{2,3},{3,2},{4,5},{5,4},{6,7},{7,6},{8,9},{9,8},{10,11... | collective-permute-start | bytes 393224 | tf_op jit(solution)/shard_map/ppermute | solution.py:90

commit v5 on v4

--- a/solution.py
+++ b/solution.py
@@ -99,10 +99,10 @@
     distant = [d for d in (8, 12) if d < size]
     for d in distant:
         held[d] = swap(block, size, d)
+    held[2] = swap(block, size, 2)
     if 4 < size:
         held[4] = swap(block, size, 4)
-        held[6] = swap(block, size, 6)
-    held[2] = swap(block, size, 2)
+        held[6] = swap(held[2], size, 4)
     piece, token = load([weights[0]], [loaded * STEP], [0], me)
     resident = [(0, piece)]
     for d in distant:
@@ -148,7 +148,7 @@
         in_specs=[IN_HBM] * count + [pl.BlockSpec(memory_space=pl.ANY)] * len(behind),
         out_specs=(IN_VMEM,) * count + (IN_SMEM,),
         scratch_shapes=[pltpu.SemaphoreType.DMA((count, parts))],
-        cost_estimate=pl.CostEstimate(flops=0, bytes_accessed=int(size * 1.0), transcendentals=0),
+        cost_estimate=pl.CostEstimate(flops=0, bytes_accessed=25165824, transcendentals=0),
         compiler_params=pltpu.CompilerParams(vmem_limit_bytes=MIB),
         name="load",
     )(*[far(a) for a in arrays], *behind)

time: 87.4 us -> 85.6 us (0.979)
  starting transfers between devices: 27 us -> 23.2 us
  waiting for transfers between devices: 21.8 us -> 23.7 us
    ppermute x30, starting transfers between devices: 21 us -> 18.1 us  [swap(): return lax.ppermute(block, 'mp', [(i, i ^ distance) for i in range(size)])]
    ppermute x30, waiting for transfers between devices: 15.9 us -> 17.8 us  [swap(): return lax.ppermute(block, 'mp', [(i, i ^ distance) for i in range(size)])]
    all_to_all x1, starting transfers between devices: 5.99 us -> 5.03 us  [shards(): lax.all_to_all(projected, 'mp', split_axis=0, concat_axis=0, tiled=True)]
  transfers between devices with their start and end apart: 31 -> 31, of which waited for: 10 -> 11; matrix products, arithmetic and copies ran while one was open for 0% -> 0% of each run, Pallas kernels for 18% -> 19%
where the time goes in v5:
time: 85.6 us; the launch traced here: 85.3 us
  Pallas kernels  37.6 us (44%)
  waiting for transfers between devices  23.7 us (28%)
  starting transfers between devices  23.2 us (27%)
    ppermute x30, starting transfers between devices, swap(): return lax.ppermute(block, 'mp', [(i, i ^ distance) for i in range(size)])  18.1 us
    ppermute x30, waiting for transfers between devices, swap(): return lax.ppermute(block, 'mp', [(i, i ^ distance) for i in range(size)])  17.8 us
    pallas_call x2, Pallas kernels, product_part(): pl.pallas_call(functools.partial(product_kernel, plan), out_shape=tuple(o...  16.2 us
    pallas_call x3, Pallas kernels, load(): pl.pallas_call(functools.partial(load_kernel, count, parts, firsts), out_...  15.9 us
    all_to_all x1, waiting for transfers between devices, shards(): lax.all_to_all(projected, 'mp', split_axis=0, concat_axis=0, tiled=True)  5.9 us
    all_to_all x1, starting transfers between devices, shards(): lax.all_to_all(projected, 'mp', split_axis=0, concat_axis=0, tiled=True)  5.03 us
    pallas_call x1, Pallas kernels, attend(): pl.pallas_call(attend_kernel, out_shape=jax.ShapeDtypeStruct(query.shape,...  4.31 us
  transfers between devices with their start and end apart: 31, of which 11 were waited for; matrix products, arithmetic and copies ran while one was open for 0% of the time, Pallas kernels for 19%

profile of v5, /device:TPU:0, one launch (start us, length us, event | category | flops | bytes accessed | tf_op | source)
XLA Modules:
  0.0 85.3 jit_solution(1087717444498255871)
XLA Ops:
  0.0 1.2 %norm.1.refs_1_ = bf16[4,16384]{1,0:T(4,128)(2,1)S(1)} custom-call(bf16[4,16384]{1,0:T(4,128)(2,1)} %x_hbm.1, bf16[128,128]{1,0:T(8,128)(2,1)} %bitcast.23), custom_call_target="tpu_custom_call" | custom-call | tf_op jit(solution)/shard_map/norm/pallas_call | solution.py:74
  1.2 5.1 %collective-permute-start.11 = (bf16[4,16384]{1,0:T(4,128)(2,1)S(1)}, bf16[4,16384]{1,0:T(4,128)(2,1)S(1)}, u32[]{:S(2)}, u32[]{:S(2)}) collective-permute-start(bf16[4,16384]{1,0:T(4,128)(2,1)S(1)} %norm.1.refs_1_), channel_id=1, source_target_pairs={{0,12},{1,13},{2,14},{3,15},{4,8},{5,9},{6,10},{7,11},{8,4},{9,5},... | collective-permute-start | bytes 393224 | tf_op jit(solution)/shard_map/ppermute | solution.py:90
  6.3 0.0 collective-permute-start.7
  6.3 1.5 %collective-permute-start.1 = (bf16[4,16384]{1,0:T(4,128)(2,1)S(1)}, bf16[4,16384]{1,0:T(4,128)(2,1)S(1)}, u32[]{:S(2)}, u32[]{:S(2)}) collective-permute-start(bf16[4,16384]{1,0:T(4,128)(2,1)S(1)} %norm.1.refs_1_), channel_id=1, source_target_pairs={{0,2},{1,3},{2,0},{3,1},{4,6},{5,7},{6,4},{7,5},{8,10},{9,11},{10,... | collective-permute-start | bytes 393224 | tf_op jit(solution)/shard_map/ppermute | solution.py:90
  7.9 0.8 collective-permute-start.3
  8.6 0.0 collective-permute-start
  8.6 6.3 %load.3 = (bf16[8192,1024]{1,0:T(8,128)(2,1)S(1)}, s32[1]{0:T(128)}) custom-call(bf16[16384,1024]{1,0:T(8,128)(2,1)} %refs_18_.2, s32[1]{0:T(128)} %bitcast.refs_1_.refs_0_), custom_call_target="tpu_custom_call" | custom-call | bytes 25165824 | tf_op jit(solution)/shard_map/load/pallas_call | solution.py:142
  15.0 0.0 collective-permute-done.11.refs_13_
  15.0 2.4 %collective-permute-done.7.refs_9_ = bf16[4,16384]{1,0:T(4,128)(2,1)S(1)} collective-permute-done((bf16[4,16384]{1,0:T(4,128)(2,1)S(1)}, bf16[4,16384]{1,0:T(4,128)(2,1)S(1)}, u32[]{:S(2)}, u32[]{:S(2)}) %collective-permute-start.7) | collective-permute-done | bytes 131104 | tf_op jit(solution)/shard_map/ppermute | solution.py:90
  17.4 0.0 collective-permute-start.12
  17.4 0.5 collective-permute-start.8
  17.9 0.0 collective-permute-done.1.refs_3_
  17.9 0.0 collective-permute-start.5
  17.9 0.0 collective-permute-done.3.refs_5_
  17.9 1.6 %collective-permute-start.9 = (bf16[4,16384]{1,0:T(4,128)(2,1)S(1)}, bf16[4,16384]{1,0:T(4,128)(2,1)S(1)}, u32[]{:S(2)}, u32[]{:S(2)}) collective-permute-start(bf16[4,16384]{1,0:T(4,128)(2,1)S(1)} %collective-permute-done.7.refs_9_), channel_id=1, source_target_pairs={{0,2},{1,3},{2,0},{3,1},{4,6},{5,7},{6,4},{7,5},{8,10},{9,11},{10,... | collective-permute-start | bytes 393224 | tf_op jit(solution)/shard_map/ppermute | solution.py:90
  19.5 0.0 collective-permute-done.refs_2_
  19.5 0.5 collective-permute-start.13
  20.0 0.0 collective-permute-done.12.refs_14_
  20.0 0.0 collective-permute-start.2
  20.0 0.0 collective-permute-done.8.refs_10_
  20.0 0.5 collective-permute-start.4
  20.6 2.8 %collective-permute-done.5.refs_7_ = bf16[4,16384]{1,0:T(4,128)(2,1)S(1)} collective-permute-done((bf16[4,16384]{1,0:T(4,128)(2,1)S(1)}, bf16[4,16384]{1,0:T(4,128)(2,1)S(1)}, u32[]{:S(2)}, u32[]{:S(2)}) %collective-permute-start.5) | collective-permute-done | bytes 131104 | tf_op jit(solution)/shard_map/ppermute | solution.py:90
  23.3 1.0 %collective-permute-done.9.refs_11_ = bf16[4,16384]{1,0:T(4,128)(2,1)S(1)} collective-permute-done((bf16[4,16384]{1,0:T(4,128)(2,1)S(1)}, bf16[4,16384]{1,0:T(4,128)(2,1)S(1)}, u32[]{:S(2)}, u32[]{:S(2)}) %collective-permute-start.9) | collective-permute-done | bytes 131104 | tf_op jit(solution)/shard_map/ppermute | solution.py:90
  24.4 0.0 collective-permute-start.10
  24.4 1.9 %collective-permute-done.13.refs_15_ = bf16[4,16384]{1,0:T(4,128)(2,1)S(1)} collective-permute-done((bf16[4,16384]{1,0:T(4,128)(2,1)S(1)}, bf16[4,16384]{1,0:T(4,128)(2,1)S(1)}, u32[]{:S(2)}, u32[]{:S(2)}) %collective-permute-start.13) | collective-permute-done | bytes 131104 | tf_op jit(solution)/shard_map/ppermute | solution.py:90
  26.2 0.0 collective-permute-start.14
  26.2 0.0 collective-permute-done.4.refs_6_
  26.2 0.0 collective-permute-done.2.refs_4_
  26.3 0.0 collective-permute-done.6.refs_8_
  26.3 1.3 %collective-permute-done.14.refs_16_ = bf16[4,16384]{1,0:T(4,128)(2,1)S(1)} collective-permute-done((bf16[4,16384]{1,0:T(4,128)(2,1)S(1)}, bf16[4,16384]{1,0:T(4,128)(2,1)S(1)}, u32[]{:S(2)}, u32[]{:S(2)}) %collective-permute-start.14) | collective-permute-done | bytes 131104 | tf_op jit(solution)/shard_map/ppermute | solution.py:90
  27.6 9.1 %product.2.refs_2_ = bf16[16,4,1152]{2,1,0:T(4,128)(2,1)} custom-call(s32[1]{0:T(128)} %bitcast.refs_1_.refs_0_, bf16[4,16384]{1,0:T(4,128)(2,1)S(1)} %norm.1.refs_1_, bf16[4,16384]{1,0:T(4,128)(2,1)S(1)} %collective-permute-done.refs_2_, bf16[4,16384]{1,0:T(4,128)(2,1)S(1)} %collective-permute-done.1.refs_3_, ...), custom_call_target="tpu_custom_call" | custom-call | flops 2415919104 | bytes 37748736 | tf_op jit(solution)/shard_map/product/pallas_call | solution.py:254
  36.7 5.0 %all-to-all-start = ((bf16[16,4,1152]{2,1,0:T(4,128)(2,1)}), bf16[16,4,1152]{2,1,0:T(4,128)(2,1)S(1)}, u32[]{:S(2)}, u32[]{:S(2)}) async-start(bf16[16,4,1152]{2,1,0:T(4,128)(2,1)} %product.2.refs_2_), calls=%async_computation | async-start | bytes 294912 | tf_op jit(solution)/shard_map/all_to_all | solution.py:426
  41.7 2.1 %load.4 = (bf16[1,8,512,128]{3,2,1,0:T(8,128)(2,1)S(1)}, bf16[1,8,512,128]{3,2,1,0:T(8,128)(2,1)S(1)}, s32[1]{0:T(128)}) custom-call(bf16[4,8,512,128]{3,2,1,0:T(8,128)(2,1)} %key_hbm.1, bf16[4,8,512,128]{3,2,1,0:T(8,128)(2,1)} %value_hbm.1, bf16[16,4,1152]{2,1,0:T(4,128)(2,1)} %product.2.refs_2_), custom_call_target="tpu_custom_call" | custom-call | bytes 25165824 | tf_op jit(solution)/shard_map/load/pallas_call | solution.py:142
  43.8 0.1 fusion
  43.9 0.1 pad_maximum_fusion
  44.0 5.9 %all-to-all-done = bf16[16,4,1152]{2,1,0:T(4,128)(2,1)S(1)} async-done(((bf16[16,4,1152]{2,1,0:T(4,128)(2,1)}), bf16[16,4,1152]{2,1,0:T(4,128)(2,1)S(1)}, u32[]{:S(2)}, u32[]{:S(2)}) %all-to-all-start) | async-done | bytes 147488 | tf_op jit(solution)/shard_map/all_to_all | solution.py:426
  50.0 0.1 reshape.23
  50.1 4.3 %attend.1 = bf16[4,128,128]{2,1,0:T(8,128)(2,1)S(1)} custom-call(s32[4]{0:T(128)S(1)} %copy-done, bf16[4,128,128]{2,1,0:T(8,128)(2,1)S(1)} %bitcast.20, bf16[4,16,128]{2,1,0:T(8,128)(2,1)S(1)} %bitcast.22, f32[4,128]{1,0:T(4,128)S(1)} %get-tuple-element.30.cos_ref, f32[4,128]{1,0:T(4,128)S(1)} %get-tuple-element.31.sin_ref, ...), custom_call_target="tpu_custom_call" | custom-call | tf_op jit(solution)/shard_map/attend/pallas_call | solution.py:383
  54.4 0.1 copy.17
  54.5 0.8 collective-permute-start.26
  55.3 0.0 collective-permute-start.22
  55.4 0.9 %collective-permute-start.16 = (bf16[4,16384]{1,0:T(4,128)(2,1)S(1)}, bf16[4,16384]{1,0:T(4,128)(2,1)S(1)}, u32[]{:S(2)}, u32[]{:S(2)}) collective-permute-start(bf16[4,16384]{1,0:T(4,128)(2,1)S(1)} %bitcast.16), channel_id=1, source_target_pairs={{0,2},{1,3},{2,0},{3,1},{4,6},{5,7},{6,4},{7,5},{8,10},{9,11},{10,... | collective-permute-start | bytes 393224 | tf_op jit(solution)/shard_map/ppermute | solution.py:90
  56.3 2.7 %collective-permute-start.18 = (bf16[4,16384]{1,0:T(4,128)(2,1)S(1)}, bf16[4,16384]{1,0:T(4,128)(2,1)S(1)}, u32[]{:S(2)}, u32[]{:S(2)}) collective-permute-start(bf16[4,16384]{1,0:T(4,128)(2,1)S(1)} %bitcast.17), channel_id=1, source_target_pairs={{0,4},{1,5},{2,6},{3,7},{4,0},{5,1},{6,2},{7,3},{8,12},{9,13},{10,... | collective-permute-start | bytes 393224 | tf_op jit(solution)/shard_map/ppermute | solution.py:90
  59.0 7.5 %load.5 = (bf16[10240,1024]{1,0:T(8,128)(2,1)S(1)}, s32[1]{0:T(128)}) custom-call(bf16[16384,1024]{1,0:T(8,128)(2,1)} %refs_18_.3, s32[1]{0:T(128)} %bitcast.refs_1_.refs_0_), custom_call_target="tpu_custom_call" | custom-call | bytes 25165824 | tf_op jit(solution)/shard_map/load/pallas_call | solution.py:142
  66.5 1.4 %collective-permute-done.22.refs_9_ = bf16[4,16384]{1,0:T(4,128)(2,1)S(1)} collective-permute-done((bf16[4,16384]{1,0:T(4,128)(2,1)S(1)}, bf16[4,16384]{1,0:T(4,128)(2,1)S(1)}, u32[]{:S(2)}, u32[]{:S(2)}) %collective-permute-start.22) | collective-permute-done | bytes 131104 | tf_op jit(solution)/shard_map/ppermute | solution.py:90
  67.9 0.5 collective-permute-start.23
  68.4 0.0 collective-permute-done.16.refs_3_
  68.4 0.0 collective-permute-start.20
  68.4 0.0 collective-permute-done.18.refs_5_
  68.4 0.9 %collective-permute-start.24 = (bf16[4,16384]{1,0:T(4,128)(2,1)S(1)}, bf16[4,16384]{1,0:T(4,128)(2,1)S(1)}, u32[]{:S(2)}, u32[]{:S(2)}) collective-permute-start(bf16[4,16384]{1,0:T(4,128)(2,1)S(1)} %collective-permute-done.22.refs_9_), channel_id=1, source_target_pairs={{0,2},{1,3},{2,0},{3,1},{4,6},{5,7},{6,4},{7,5},{8,10},{9,11},{10,... | collective-permute-start | bytes 393224 | tf_op jit(solution)/shard_map/ppermute | solution.py:90
  69.3 0.0 collective-permute-done.15.refs_2_
  69.3 1.2 %collective-permute-start.28 = (bf16[4,16384]{1,0:T(4,128)(2,1)S(1)}, bf16[4,16384]{1,0:T(4,128)(2,1)S(1)}, u32[]{:S(2)}, u32[]{:S(2)}) collective-permute-start(bf16[4,16384]{1,0:T(4,128)(2,1)S(1)} %collective-permute-done.26.refs_13_), channel_id=1, source_target_pairs={{0,2},{1,3},{2,0},{3,1},{4,6},{5,7},{6,4},{7,5},{8,10},{9,11},{10,... | collective-permute-start | bytes 393224 | tf_op jit(solution)/shard_map/ppermute | solution.py:90
  70.5 0.0 collective-permute-done.27.refs_14_
  70.5 0.0 collective-permute-start.17
  70.5 0.0 collective-permute-done.23.refs_10_
  70.5 0.5 collective-permute-start.19
  71.0 2.8 %collective-permute-done.20.refs_7_ = bf16[4,16384]{1,0:T(4,128)(2,1)S(1)} collective-permute-done((bf16[4,16384]{1,0:T(4,128)(2,1)S(1)}, bf16[4,16384]{1,0:T(4,128)(2,1)S(1)}, u32[]{:S(2)}, u32[]{:S(2)}) %collective-permute-start.20) | collective-permute-done | bytes 131104 | tf_op jit(solution)/shard_map/ppermute | solution.py:90
  73.8 0.0 collective-permute-start.21
  73.8 1.0 %collective-permute-done.24.refs_11_ = bf16[4,16384]{1,0:T(4,128)(2,1)S(1)} collective-permute-done((bf16[4,16384]{1,0:T(4,128)(2,1)S(1)}, bf16[4,16384]{1,0:T(4,128)(2,1)S(1)}, u32[]{:S(2)}, u32[]{:S(2)}) %collective-permute-start.24) | collective-permute-done | bytes 131104 | tf_op jit(solution)/shard_map/ppermute | solution.py:90
  74.8 1.9 %collective-permute-done.28.refs_15_ = bf16[4,16384]{1,0:T(4,128)(2,1)S(1)} collective-permute-done((bf16[4,16384]{1,0:T(4,128)(2,1)S(1)}, bf16[4,16384]{1,0:T(4,128)(2,1)S(1)}, u32[]{:S(2)}, u32[]{:S(2)}) %collective-permute-start.28) | collective-permute-done | bytes 131104 | tf_op jit(solution)/shard_map/ppermute | solution.py:90
  76.7 0.0 collective-permute-done.17.refs_4_
  76.7 0.0 collective-permute-done.21.refs_8_
  76.7 1.3 %collective-permute-done.29.refs_16_ = bf16[4,16384]{1,0:T(4,128)(2,1)S(1)} collective-permute-done((bf16[4,16384]{1,0:T(4,128)(2,1)S(1)}, bf16[4,16384]{1,0:T(4,128)(2,1)S(1)}, u32[]{:S(2)}, u32[]{:S(2)}) %collective-permute-start.29) | collective-permute-done | bytes 131104 | tf_op jit(solution)/shard_map/ppermute | solution.py:90
  78.0 7.1 %product.3 = bf16[64,1024]{1,0:T(8,128)(2,1)} custom-call(s32[1]{0:T(128)} %bitcast.refs_1_.refs_0_, bf16[4,16384]{1,0:T(4,128)(2,1)S(1)} %bitcast.19, bf16[4,16384]{1,0:T(4,128)(2,1)S(1)} %collective-permute-done.15.refs_2_, bf16[4,16384]{1,0:T(4,128)(2,1)S(1)} %collective-permute-done.16.refs_3_, bf16[4,16384]{1,0:T(4,128)(2,1)S(1)} %collective-permute-done.17.refs_4_, ...), custom_call_target="tpu_custom_call" | custom-call | flops 2147483648 | bytes 33554432 | tf_op jit(solution)/shard_map/product/pallas_call | solution.py:254
  (17 shorter events, 0.1 us)
Async XLA Ops:
  1.2 13.7 %collective-permute-start.11 = (bf16[4,16384]{1,0:T(4,128)(2,1)S(1)}, bf16[4,16384]{1,0:T(4,128)(2,1)S(1)}, u32[]{:S(2)}, u32[]{:S(2)}) collective-permute-start(bf16[4,16384]{1,0:T(4,128)(2,1)S(1)} %norm.1.refs_1_), channel_id=1, source_target_pairs={{0,12},{1,13},{2,14},{3,15},{4,8},{5,9},{6,10},{7,11},{8,4},{9,5},... | collective-permute-start | bytes 393224 | tf_op jit(solution)/shard_map/ppermute | solution.py:90
  6.3 11.1 %collective-permute-start.7 = (bf16[4,16384]{1,0:T(4,128)(2,1)S(1)}, bf16[4,16384]{1,0:T(4,128)(2,1)S(1)}, u32[]{:S(2)}, u32[]{:S(2)}) collective-permute-start(bf16[4,16384]{1,0:T(4,128)(2,1)S(1)} %norm.1.refs_1_), channel_id=1, source_target_pairs={{0,8},{1,9},{2,10},{3,11},{4,12},{5,13},{6,14},{7,15},{8,0},{9,1},... | collective-permute-start | bytes 393224 | tf_op jit(solution)/shard_map/ppermute | solution.py:90
  6.3 11.6 %collective-permute-start.1 = (bf16[4,16384]{1,0:T(4,128)(2,1)S(1)}, bf16[4,16384]{1,0:T(4,128)(2,1)S(1)}, u32[]{:S(2)}, u32[]{:S(2)}) collective-permute-start(bf16[4,16384]{1,0:T(4,128)(2,1)S(1)} %norm.1.refs_1_), channel_id=1, source_target_pairs={{0,2},{1,3},{2,0},{3,1},{4,6},{5,7},{6,4},{7,5},{8,10},{9,11},{10,... | collective-permute-start | bytes 393224 | tf_op jit(solution)/shard_map/ppermute | solution.py:90
  7.9 10.1 %collective-permute-start.3 = (bf16[4,16384]{1,0:T(4,128)(2,1)S(1)}, bf16[4,16384]{1,0:T(4,128)(2,1)S(1)}, u32[]{:S(2)}, u32[]{:S(2)}) collective-permute-start(bf16[4,16384]{1,0:T(4,128)(2,1)S(1)} %norm.1.refs_1_), channel_id=1, source_target_pairs={{0,4},{1,5},{2,6},{3,7},{4,0},{5,1},{6,2},{7,3},{8,12},{9,13},{10,... | collective-permute-start | bytes 393224 | tf_op jit(solution)/shard_map/ppermute | solution.py:90
  8.6 10.9 %collective-permute-start = (bf16[4,16384]{1,0:T(4,128)(2,1)S(1)}, bf16[4,16384]{1,0:T(4,128)(2,1)S(1)}, u32[]{:S(2)}, u32[]{:S(2)}) collective-permute-start(bf16[4,16384]{1,0:T(4,128)(2,1)S(1)} %norm.1.refs_1_), channel_id=1, source_target_pairs={{0,1},{1,0},{2,3},{3,2},{4,5},{5,4},{6,7},{7,6},{8,9},{9,8},{10,11... | collective-permute-start | bytes 393224 | tf_op jit(solution)/shard_map/ppermute | solution.py:90
  17.4 2.6 %collective-permute-start.12 = (bf16[4,16384]{1,0:T(4,128)(2,1)S(1)}, bf16[4,16384]{1,0:T(4,128)(2,1)S(1)}, u32[]{:S(2)}, u32[]{:S(2)}) collective-permute-start(bf16[4,16384]{1,0:T(4,128)(2,1)S(1)} %collective-permute-done.11.refs_13_), channel_id=1, source_target_pairs={{0,1},{1,0},{2,3},{3,2},{4,5},{5,4},{6,7},{7,6},{8,9},{9,8},{10,11... | collective-permute-start | bytes 393224 | tf_op jit(solution)/shard_map/ppermute | solution.py:90
  17.4 2.6 %collective-permute-start.8 = (bf16[4,16384]{1,0:T(4,128)(2,1)S(1)}, bf16[4,16384]{1,0:T(4,128)(2,1)S(1)}, u32[]{:S(2)}, u32[]{:S(2)}) collective-permute-start(bf16[4,16384]{1,0:T(4,128)(2,1)S(1)} %collective-permute-done.7.refs_9_), channel_id=1, source_target_pairs={{0,1},{1,0},{2,3},{3,2},{4,5},{5,4},{6,7},{7,6},{8,9},{9,8},{10,11... | collective-permute-start | bytes 393224 | tf_op jit(solution)/shard_map/ppermute | solution.py:90
  17.9 5.4 %collective-permute-start.5 = (bf16[4,16384]{1,0:T(4,128)(2,1)S(1)}, bf16[4,16384]{1,0:T(4,128)(2,1)S(1)}, u32[]{:S(2)}, u32[]{:S(2)}) collective-permute-start(bf16[4,16384]{1,0:T(4,128)(2,1)S(1)} %collective-permute-done.1.refs_3_), channel_id=1, source_target_pairs={{0,4},{1,5},{2,6},{3,7},{4,0},{5,1},{6,2},{7,3},{8,12},{9,13},{10,... | collective-permute-start | bytes 393224 | tf_op jit(solution)/shard_map/ppermute | solution.py:90
  17.9 6.4 %collective-permute-start.9 = (bf16[4,16384]{1,0:T(4,128)(2,1)S(1)}, bf16[4,16384]{1,0:T(4,128)(2,1)S(1)}, u32[]{:S(2)}, u32[]{:S(2)}) collective-permute-start(bf16[4,16384]{1,0:T(4,128)(2,1)S(1)} %collective-permute-done.7.refs_9_), channel_id=1, source_target_pairs={{0,2},{1,3},{2,0},{3,1},{4,6},{5,7},{6,4},{7,5},{8,10},{9,11},{10,... | collective-permute-start | bytes 393224 | tf_op jit(solution)/shard_map/ppermute | solution.py:90
  19.5 6.7 %collective-permute-start.13 = (bf16[4,16384]{1,0:T(4,128)(2,1)S(1)}, bf16[4,16384]{1,0:T(4,128)(2,1)S(1)}, u32[]{:S(2)}, u32[]{:S(2)}) collective-permute-start(bf16[4,16384]{1,0:T(4,128)(2,1)S(1)} %collective-permute-done.11.refs_13_), channel_id=1, source_target_pairs={{0,2},{1,3},{2,0},{3,1},{4,6},{5,7},{6,4},{7,5},{8,10},{9,11},{10,... | collective-permute-start | bytes 393224 | tf_op jit(solution)/shard_map/ppermute | solution.py:90
  20.0 6.2 %collective-permute-start.2 = (bf16[4,16384]{1,0:T(4,128)(2,1)S(1)}, bf16[4,16384]{1,0:T(4,128)(2,1)S(1)}, u32[]{:S(2)}, u32[]{:S(2)}) collective-permute-start(bf16[4,16384]{1,0:T(4,128)(2,1)S(1)} %collective-permute-done.1.refs_3_), channel_id=1, source_target_pairs={{0,1},{1,0},{2,3},{3,2},{4,5},{5,4},{6,7},{7,6},{8,9},{9,8},{10,11... | collective-permute-start | bytes 393224 | tf_op jit(solution)/shard_map/ppermute | solution.py:90
  20.0 6.2 %collective-permute-start.4 = (bf16[4,16384]{1,0:T(4,128)(2,1)S(1)}, bf16[4,16384]{1,0:T(4,128)(2,1)S(1)}, u32[]{:S(2)}, u32[]{:S(2)}) collective-permute-start(bf16[4,16384]{1,0:T(4,128)(2,1)S(1)} %collective-permute-done.3.refs_5_), channel_id=1, source_target_pairs={{0,1},{1,0},{2,3},{3,2},{4,5},{5,4},{6,7},{7,6},{8,9},{9,8},{10,11... | collective-permute-start | bytes 393224 | tf_op jit(solution)/shard_map/ppermute | solution.py:90
  23.3 2.9 %collective-permute-start.6 = (bf16[4,16384]{1,0:T(4,128)(2,1)S(1)}, bf16[4,16384]{1,0:T(4,128)(2,1)S(1)}, u32[]{:S(2)}, u32[]{:S(2)}) collective-permute-start(bf16[4,16384]{1,0:T(4,128)(2,1)S(1)} %collective-permute-done.5.refs_7_), channel_id=1, source_target_pairs={{0,1},{1,0},{2,3},{3,2},{4,5},{5,4},{6,7},{7,6},{8,9},{9,8},{10,11... | collective-permute-start | bytes 393224 | tf_op jit(solution)/shard_map/ppermute | solution.py:90
  24.4 1.9 %collective-permute-start.10 = (bf16[4,16384]{1,0:T(4,128)(2,1)S(1)}, bf16[4,16384]{1,0:T(4,128)(2,1)S(1)}, u32[]{:S(2)}, u32[]{:S(2)}) collective-permute-start(bf16[4,16384]{1,0:T(4,128)(2,1)S(1)} %collective-permute-done.9.refs_11_), channel_id=1, source_target_pairs={{0,1},{1,0},{2,3},{3,2},{4,5},{5,4},{6,7},{7,6},{8,9},{9,8},{10,11... | collective-permute-start | bytes 393224 | tf_op jit(solution)/shard_map/ppermute | solution.py:90
  26.2 1.3 %collective-permute-start.14 = (bf16[4,16384]{1,0:T(4,128)(2,1)S(1)}, bf16[4,16384]{1,0:T(4,128)(2,1)S(1)}, u32[]{:S(2)}, u32[]{:S(2)}) collective-permute-start(bf16[4,16384]{1,0:T(4,128)(2,1)S(1)} %collective-permute-done.13.refs_15_), channel_id=1, source_target_pairs={{0,1},{1,0},{2,3},{3,2},{4,5},{5,4},{6,7},{7,6},{8,9},{9,8},{10,11... | collective-permute-start | bytes 393224 | tf_op jit(solution)/shard_map/ppermute | solution.py:90
  27.6 14.1 %copy-start = (s32[4]{0:T(128)S(1)}, s32[4]{0:T(128)}, u32[]{:S(2)}) copy-start(s32[4]{0:T(128)} %lengths_ref) | copy-start | bytes 52
  36.7 13.2 %all-to-all-start = ((bf16[16,4,1152]{2,1,0:T(4,128)(2,1)}), bf16[16,4,1152]{2,1,0:T(4,128)(2,1)S(1)}, u32[]{:S(2)}, u32[]{:S(2)}) async-start(bf16[16,4,1152]{2,1,0:T(4,128)(2,1)} %product.2.refs_2_), calls=%async_computation | async-start | bytes 294912 | tf_op jit(solution)/shard_map/all_to_all | solution.py:426
  54.5 12.0 %collective-permute-start.26 = (bf16[4,16384]{1,0:T(4,128)(2,1)S(1)}, bf16[4,16384]{1,0:T(4,128)(2,1)S(1)}, u32[]{:S(2)}, u32[]{:S(2)}) collective-permute-start(bf16[4,16384]{1,0:T(4,128)(2,1)S(1)} %bitcast.14), channel_id=1, source_target_pairs={{0,12},{1,13},{2,14},{3,15},{4,8},{5,9},{6,10},{7,11},{8,4},{9,5},... | collective-permute-start | bytes 393224 | tf_op jit(solution)/shard_map/ppermute | solution.py:90
  55.3 12.5 %collective-permute-start.22 = (bf16[4,16384]{1,0:T(4,128)(2,1)S(1)}, bf16[4,16384]{1,0:T(4,128)(2,1)S(1)}, u32[]{:S(2)}, u32[]{:S(2)}) collective-permute-start(bf16[4,16384]{1,0:T(4,128)(2,1)S(1)} %bitcast.15), channel_id=1, source_target_pairs={{0,8},{1,9},{2,10},{3,11},{4,12},{5,13},{6,14},{7,15},{8,0},{9,1},... | collective-permute-start | bytes 393224 | tf_op jit(solution)/shard_map/ppermute | solution.py:90
  55.4 13.0 %collective-permute-start.16 = (bf16[4,16384]{1,0:T(4,128)(2,1)S(1)}, bf16[4,16384]{1,0:T(4,128)(2,1)S(1)}, u32[]{:S(2)}, u32[]{:S(2)}) collective-permute-start(bf16[4,16384]{1,0:T(4,128)(2,1)S(1)} %bitcast.16), channel_id=1, source_target_pairs={{0,2},{1,3},{2,0},{3,1},{4,6},{5,7},{6,4},{7,5},{8,10},{9,11},{10,... | collective-permute-start | bytes 393224 | tf_op jit(solution)/shard_map/ppermute | solution.py:90
  56.3 12.1 %collective-permute-start.18 = (bf16[4,16384]{1,0:T(4,128)(2,1)S(1)}, bf16[4,16384]{1,0:T(4,128)(2,1)S(1)}, u32[]{:S(2)}, u32[]{:S(2)}) collective-permute-start(bf16[4,16384]{1,0:T(4,128)(2,1)S(1)} %bitcast.17), channel_id=1, source_target_pairs={{0,4},{1,5},{2,6},{3,7},{4,0},{5,1},{6,2},{7,3},{8,12},{9,13},{10,... | collective-permute-start | bytes 393224 | tf_op jit(solution)/shard_map/ppermute | solution.py:90
  59.0 10.3 %collective-permute-start.15 = (bf16[4,16384]{1,0:T(4,128)(2,1)S(1)}, bf16[4,16384]{1,0:T(4,128)(2,1)S(1)}, u32[]{:S(2)}, u32[]{:S(2)}) collective-permute-start(bf16[4,16384]{1,0:T(4,128)(2,1)S(1)} %bitcast.18), channel_id=1, source_target_pairs={{0,1},{1,0},{2,3},{3,2},{4,5},{5,4},{6,7},{7,6},{8,9},{9,8},{10,11... | collective-permute-start | bytes 393224 | tf_op jit(solution)/shard_map/ppermute | solution.py:90
  67.9 2.6 %collective-permute-start.27 = (bf16[4,16384]{1,0:T(4,128)(2,1)S(1)}, bf16[4,16384]{1,0:T(4,128)(2,1)S(1)}, u32[]{:S(2)}, u32[]{:S(2)}) collective-permute-start(bf16[4,16384]{1,0:T(4,128)(2,1)S(1)} %collective-permute-done.26.refs_13_), channel_id=1, source_target_pairs={{0,1},{1,0},{2,3},{3,2},{4,5},{5,4},{6,7},{7,6},{8,9},{9,8},{10,11... | collective-permute-start | bytes 393224 | tf_op jit(solution)/shard_map/ppermute | solution.py:90
  67.9 2.6 %collective-permute-start.23 = (bf16[4,16384]{1,0:T(4,128)(2,1)S(1)}, bf16[4,16384]{1,0:T(4,128)(2,1)S(1)}, u32[]{:S(2)}, u32[]{:S(2)}) collective-permute-start(bf16[4,16384]{1,0:T(4,128)(2,1)S(1)} %collective-permute-done.22.refs_9_), channel_id=1, source_target_pairs={{0,1},{1,0},{2,3},{3,2},{4,5},{5,4},{6,7},{7,6},{8,9},{9,8},{10,11... | collective-permute-start | bytes 393224 | tf_op jit(solution)/shard_map/ppermute | solution.py:90
  68.4 5.4 %collective-permute-start.20 = (bf16[4,16384]{1,0:T(4,128)(2,1)S(1)}, bf16[4,16384]{1,0:T(4,128)(2,1)S(1)}, u32[]{:S(2)}, u32[]{:S(2)}) collective-permute-start(bf16[4,16384]{1,0:T(4,128)(2,1)S(1)} %collective-permute-done.16.refs_3_), channel_id=1, source_target_pairs={{0,4},{1,5},{2,6},{3,7},{4,0},{5,1},{6,2},{7,3},{8,12},{9,13},{10,... | collective-permute-start | bytes 393224 | tf_op jit(solution)/shard_map/ppermute | solution.py:90
  68.4 6.4 %collective-permute-start.24 = (bf16[4,16384]{1,0:T(4,128)(2,1)S(1)}, bf16[4,16384]{1,0:T(4,128)(2,1)S(1)}, u32[]{:S(2)}, u32[]{:S(2)}) collective-permute-start(bf16[4,16384]{1,0:T(4,128)(2,1)S(1)} %collective-permute-done.22.refs_9_), channel_id=1, source_target_pairs={{0,2},{1,3},{2,0},{3,1},{4,6},{5,7},{6,4},{7,5},{8,10},{9,11},{10,... | collective-permute-start | bytes 393224 | tf_op jit(solution)/shard_map/ppermute | solution.py:90
  69.3 7.4 %collective-permute-start.28 = (bf16[4,16384]{1,0:T(4,128)(2,1)S(1)}, bf16[4,16384]{1,0:T(4,128)(2,1)S(1)}, u32[]{:S(2)}, u32[]{:S(2)}) collective-permute-start(bf16[4,16384]{1,0:T(4,128)(2,1)S(1)} %collective-permute-done.26.refs_13_), channel_id=1, source_target_pairs={{0,2},{1,3},{2,0},{3,1},{4,6},{5,7},{6,4},{7,5},{8,10},{9,11},{10,... | collective-permute-start | bytes 393224 | tf_op jit(solution)/shard_map/ppermute | solution.py:90
  70.5 6.2 %collective-permute-start.17 = (bf16[4,16384]{1,0:T(4,128)(2,1)S(1)}, bf16[4,16384]{1,0:T(4,128)(2,1)S(1)}, u32[]{:S(2)}, u32[]{:S(2)}) collective-permute-start(bf16[4,16384]{1,0:T(4,128)(2,1)S(1)} %collective-permute-done.16.refs_3_), channel_id=1, source_target_pairs={{0,1},{1,0},{2,3},{3,2},{4,5},{5,4},{6,7},{7,6},{8,9},{9,8},{10,11... | collective-permute-start | bytes 393224 | tf_op jit(solution)/shard_map/ppermute | solution.py:90
  70.5 6.2 %collective-permute-start.19 = (bf16[4,16384]{1,0:T(4,128)(2,1)S(1)}, bf16[4,16384]{1,0:T(4,128)(2,1)S(1)}, u32[]{:S(2)}, u32[]{:S(2)}) collective-permute-start(bf16[4,16384]{1,0:T(4,128)(2,1)S(1)} %collective-permute-done.18.refs_5_), channel_id=1, source_target_pairs={{0,1},{1,0},{2,3},{3,2},{4,5},{5,4},{6,7},{7,6},{8,9},{9,8},{10,11... | collective-permute-start | bytes 393224 | tf_op jit(solution)/shard_map/ppermute | solution.py:90
  73.8 2.9 %collective-permute-start.21 = (bf16[4,16384]{1,0:T(4,128)(2,1)S(1)}, bf16[4,16384]{1,0:T(4,128)(2,1)S(1)}, u32[]{:S(2)}, u32[]{:S(2)}) collective-permute-start(bf16[4,16384]{1,0:T(4,128)(2,1)S(1)} %collective-permute-done.20.refs_7_), channel_id=1, source_target_pairs={{0,1},{1,0},{2,3},{3,2},{4,5},{5,4},{6,7},{7,6},{8,9},{9,8},{10,11... | collective-permute-start | bytes 393224 | tf_op jit(solution)/shard_map/ppermute | solution.py:90
  74.8 1.9 %collective-permute-start.25 = (bf16[4,16384]{1,0:T(4,128)(2,1)S(1)}, bf16[4,16384]{1,0:T(4,128)(2,1)S(1)}, u32[]{:S(2)}, u32[]{:S(2)}) collective-permute-start(bf16[4,16384]{1,0:T(4,128)(2,1)S(1)} %collective-permute-done.24.refs_11_), channel_id=1, source_target_pairs={{0,1},{1,0},{2,3},{3,2},{4,5},{5,4},{6,7},{7,6},{8,9},{9,8},{10,11... | collective-permute-start | bytes 393224 | tf_op jit(solution)/shard_map/ppermute | solution.py:90
  76.7 1.3 %collective-permute-start.29 = (bf16[4,16384]{1,0:T(4,128)(2,1)S(1)}, bf16[4,16384]{1,0:T(4,128)(2,1)S(1)}, u32[]{:S(2)}, u32[]{:S(2)}) collective-permute-start(bf16[4,16384]{1,0:T(4,128)(2,1)S(1)} %collective-permute-done.28.refs_15_), channel_id=1, source_target_pairs={{0,1},{1,0},{2,3},{3,2},{4,5},{5,4},{6,7},{7,6},{8,9},{9,8},{10,11... | collective-permute-start | bytes 393224 | tf_op jit(solution)/shard_map/ppermute | solution.py:90
